TPU v7x, 32 devices: a whole 2x2x4 slice. The times are simulated.
32 devices in a mesh: table: 16 (over z, y, x), dp: 2 (over core).
Axes of the slice: x: 2, y: 2, z: 4, core: 2. Of those that a mesh axis runs over, the one named last changes fastest.
Arguments:
- emb_table: float32 [32768, 128], P('table'), may hold values from -4 to 4
- versions: int32 [32768], P('table'), may hold values from 0 to 999
- conf_local: int32 [4096], P('table'), may hold values from 0 to 2047, as said below
- conf_version: int32 [4096], P('table'), may hold values from 0 to 999
- conf_values: float32 [4096, 128], P('table'), may hold values from -4 to 4
- owners: int32 [4096, 26, 1], P(('table', 'dp')), may hold values from 0 to 15; in each aligned block of 3328 rows (0 to 3327, 3328 to 6655, ..., all dimensions but the last counted through in order) at most 312 rows name the same one
- row_local: int32 [4096, 26, 2], P(('table', 'dp')), may hold values from 0 to 2047
- lengths: int32 [4096, 26], P(('table', 'dp')), may hold values from 1 to 2
- dense_out: bfloat16 [4096, 128], P(('table', 'dp')), may hold values from -6 to 6
- labels: int32 [4096], P(('table', 'dp')), may hold values 0 or 1
- cross_down: bfloat16 [1, 3456, 512], P(None, None, 'dp'), may hold values from -0.109375 to 0.109375
- cross_up: bfloat16 [1, 512, 3456], P(None, 'dp'), may hold values from -0.25 to 0.25
- cross_bias: float32 [1, 3456], replicated, may hold values from -3 to 3
- head_weight: float32 [3456], replicated, may hold values from -0.109375 to 0.109375
Outputs:
- logits: float32 [4096], P(('table', 'dp'))
- emb_grad: float32 [32768, 128], P(('table', 'dp'))
Inputs may be any that keep to these rules, and one draw needn't show every extreme that they name: `owners`: in each aligned block of the 3328 bags of one device (samples in order, bags within a sample in order), at most 312 bags name one holder; in some block one holder is named by exactly 312 bags. `conf_local`: within each holder's 256 entries the local row numbers are distinct.
All inputs are finite; a program needn't handle non-finite values. No bound on the sum of `labels` on one device may be relied on, other than what follows from the above.
Results may differ from a plain program's by a relative error of at most 0.0035.
Values may be sent and summed in bfloat16 or wider, within the bound.
No kernel may reach another device: no remote copies, remote signals or barrier semaphores. Data moves between devices by JAX's collectives and lax.ppermute only.
A program may use at most 64 MiB of HBM per device.

v0:
```python
import jax
import jax.numpy as jnp
from jax import lax
from jax.sharding import PartitionSpec as P

loss_scale = 64.0


def dense_step(inputs, labels, cross_down, cross_up, cross_bias, head_weight):
    base_float = inputs.astype(jnp.float32)
    state = base_float
    cross_index = 0
    crossed = jnp.dot(inputs, cross_down[cross_index], preferred_element_type=jnp.float32).astype(
        jnp.bfloat16
    )
    factor = (
        jnp.dot(crossed, cross_up[cross_index], preferred_element_type=jnp.float32)
        + cross_bias[cross_index]
    )
    factors = [factor]
    state = base_float * factor + state
    logits = jnp.sum(state * head_weight, axis=1)
    signal = loss_scale * (jax.nn.sigmoid(logits) - labels.astype(jnp.float32))
    grad_state = signal[:, None] * head_weight[None, :]
    cross_index = 0
    grad_base = grad_state * factors[cross_index]
    grad_lift = (grad_state * base_float).astype(jnp.bfloat16)
    grad_cross = lax.dot_general(
        grad_lift,
        cross_up[cross_index],
        (((1,), (1,)), ((), ())),
        preferred_element_type=jnp.float32,
    ).astype(jnp.bfloat16)
    grad_state = grad_state + lax.dot_general(
        grad_cross,
        cross_down[cross_index],
        (((1,), (1,)), ((), ())),
        preferred_element_type=jnp.float32,
    )
    return (logits, grad_state + grad_base)


def body(
    emb_table,
    versions,
    conf_local,
    conf_version,
    conf_values,
    owners,
    row_local,
    lengths,
    dense_out,
    labels,
    cross_down,
    cross_up,
    cross_bias,
    head_weight,
):
    peers = lax.axis_size("table")
    rows_dev, emb_width = emb_table.shape
    is_newer = conf_version > versions[conf_local]
    current = emb_table[conf_local]
    updated = emb_table.at[conf_local].set(jnp.where(is_newer[:, None], conf_values, current))
    samples, features, slot_count = row_local.shape
    bag_count = samples * features
    capacity = 3 * bag_count // (2 * peers)
    owner_flat = owners.reshape(bag_count)
    onehot_owner = (owner_flat[:, None] == jnp.arange(peers, dtype=jnp.int32)[None, :]).astype(
        jnp.int32
    )
    earlier = jnp.cumsum(onehot_owner, axis=0) - onehot_owner
    rank_in_owner = jnp.sum(earlier * onehot_owner, axis=1)
    position = owner_flat * capacity + rank_in_owner
    request_rows = (
        jnp.zeros((peers * capacity, slot_count), jnp.int32)
        .at[position]
        .set(row_local.reshape(bag_count, slot_count))
    )
    request_rows = request_rows.reshape(peers, capacity, slot_count)
    request_len = (
        jnp.zeros((peers * capacity,), jnp.int32).at[position].set(lengths.reshape(bag_count))
    )
    request_len = request_len.reshape(peers, capacity)
    slot_index = jnp.arange(slot_count, dtype=jnp.int32)
    asked_rows = lax.all_to_all(request_rows, "table", split_axis=0, concat_axis=0, tiled=True)
    asked_len = lax.all_to_all(request_len, "table", split_axis=0, concat_axis=0, tiled=True)
    live_mask = slot_index[None, None, :] < asked_len[:, :, None]
    looked_up = jnp.where(live_mask[..., None], updated[asked_rows], 0.0)
    answer = lax.all_to_all(
        jnp.sum(looked_up, axis=2).astype(jnp.bfloat16),
        "table",
        split_axis=0,
        concat_axis=0,
        tiled=True,
    ).astype(jnp.float32)
    answer, got_rows, got_len = (answer, asked_rows, asked_len)
    pooled = answer.reshape(peers * capacity, emb_width)[position].reshape(
        samples, features * emb_width
    )
    inputs = jnp.concatenate([dense_out.astype(jnp.float32), pooled], axis=1).astype(jnp.bfloat16)
    full_down, full_up = (
        lax.all_gather(cross_down, "dp", axis=2, tiled=True),
        lax.all_gather(cross_up, "dp", axis=1, tiled=True),
    )
    logits, grad_input = dense_step(inputs, labels, full_down, full_up, cross_bias, head_weight)
    bag_grad = grad_input[:, emb_width:].reshape(bag_count, emb_width)
    send_grad = jnp.zeros((peers * capacity, emb_width), jnp.float32).at[position].set(bag_grad)
    send_grad = send_grad.reshape(peers, capacity, emb_width)
    got_grad = lax.all_to_all(send_grad, "table", split_axis=0, concat_axis=0, tiled=True)
    live_held = slot_index[None, None, :] < got_len[:, :, None]
    updates = jnp.where(live_held[..., None], got_grad[:, :, None, :], 0.0)
    local_grad = (
        jnp.zeros((rows_dev, emb_width), jnp.float32)
        .at[got_rows.reshape(-1)]
        .add(updates.reshape(-1, emb_width))
    )
    emb_grad = lax.psum_scatter(local_grad, "dp", scatter_dimension=0, tiled=True)
    return (logits, emb_grad)


def solution(mesh):
    in_specs = (
        P("table", None),
        P("table"),
        P("table"),
        P("table"),
        P("table", None),
        P(("table", "dp"), None, None),
        P(("table", "dp"), None, None),
        P(("table", "dp"), None),
        P(("table", "dp"), None),
        P(("table", "dp")),
        P(None, None, "dp"),
        P(None, "dp", None),
        P(),
        P(),
    )
    out_specs = (P(("table", "dp")), P(("table", "dp"), None))
    return jax.shard_map(body, mesh=mesh, in_specs=in_specs, out_specs=out_specs, check_vma=False)
```

profile of v0, /device:TPU:0, one launch (start us, length us, event | category | flops | bytes accessed | tf_op | source)
XLA Modules:
  0.0 354.2 jit_solution(17870530851974267329)
XLA Ops:
  8.4 4.6 %reduce-window.6 = s32[16,26,128]{2,1,0:T(8,128)S(1)} reduce-window(s32[16,26,128]{2,1,0:T(8,128)S(1)} %fusion.32, s32[]{:T(128)} %constant.7.clone.1), window={size=1x1x128 pad=0_0x0_0x127_0}, to_apply=%region_0.1 | reduce-window | flops 6762496 | bytes 425988 | tf_op jit(solution)/shard_map/reduce-window
  14.6 12.7 %scatter_custom_fusion = s32[4992]{0:T(1024)S(1)} fusion(s32[3328]{0:T(1024)S(1)} %fusion.40, s32[3328]{0:T(1024)S(1)} %reshape.174, s32[]{:T(128)} %constant.7.clone.1), kind=kCustom, calls=%fused_computation.60 | custom fusion | bytes 19972 | tf_op jit(solution)/shard_map/scatter | solution.py:81
  28.0 8.3 %all-to-all-start = ((s32[16,1,312]{2,1,0:T(1,128)}), s32[16,1,312]{2,1,0:T(1,128)S(1)}, u32[]{:S(2)}, u32[]{:S(2)}) async-start(s32[16,1,312]{2,1,0:T(1,128)} %all_to_all.15), calls=%async_computation | async-start | bytes 49152 | tf_op jit(solution)/shard_map/all_to_all | solution.py:86
  38.0 14.9 %scatter_custom_fusion.2 = s32[4992,2]{1,0:T(8,128)} fusion(s32[3328]{0:T(1024)S(1)} %fusion.40, s32[3328,2]{1,0:T(8,128)S(1)} %copy.32, s32[]{:T(128)} %constant.7.clone.1), kind=kCustom, calls=%fused_computation.34 | custom fusion | bytes 39940 | tf_op jit(solution)/shard_map/scatter | solution.py:77
  52.9 3.3 copy.33
  56.2 1.7 gather_fusion
  58.0 2.1 scatter_custom_fusion.1
  60.1 6.9 %all-to-all-start.1 = ((s32[16,312,2]{1,2,0:T(2,128)}), s32[16,312,2]{1,2,0:T(2,128)S(1)}, u32[]{:S(2)}, u32[]{:S(2)}) async-start(s32[16,312,2]{1,2,0:T(2,128)} %copy.33), calls=%async_computation.1 | async-start | bytes 98304 | tf_op jit(solution)/shard_map/all_to_all | solution.py:85
  67.1 1.0 iota_compare_fusion
  68.1 6.4 %all-to-all-done.1 = s32[16,312,2]{1,2,0:T(2,128)S(1)} async-done(((s32[16,312,2]{1,2,0:T(2,128)}), s32[16,312,2]{1,2,0:T(2,128)S(1)}, u32[]{:S(2)}, u32[]{:S(2)}) %all-to-all-start.1) | async-done | bytes 39968 | tf_op jit(solution)/shard_map/all_to_all | solution.py:85
  74.6 2.2 copy.34
  76.8 3.1 reshape.156
  79.9 19.1 %gather_fusion.1 = f32[9984,128]{1,0:T(8,128)} fusion(f32[2048,128]{1,0:T(8,128)S(1)} %scatter_custom_fusion.1, s32[10240]{0:T(1024)S(1)} %pad_clamp_fusion), kind=kCustom, calls=%fused_computation.2 | custom fusion | bytes 10263552 | tf_op jit(solution)/shard_map/gather | solution.py:88
  99.0 26.1 %select_reduce_fusion = bf16[16,312,128]{2,1,0:T(8,128)(2,1)} fusion(f32[16,312,2,128]{3,2,1,0:T(2,128)} %bitcast.61, pred[16,312,2]{2,1,0:T(8,128)(4,1)S(1)} %iota_compare_fusion), kind=kLoop, calls=%fused_computation.11 | loop fusion | flops 1916928 | bytes 6399744 | tf_op jit(solution)/shard_map/reduce_sum | solution.py:90
  125.1 4.0 %all-to-all-start.2 = ((bf16[16,312,128]{2,1,0:T(8,128)(2,1)}), bf16[16,312,128]{2,1,0:T(8,128)(2,1)S(1)}, u32[]{:S(2)}, u32[]{:S(2)}) async-start(bf16[16,312,128]{2,1,0:T(8,128)(2,1)} %select_reduce_fusion), calls=%async_computation.2 | async-start | bytes 2555904 | tf_op jit(solution)/shard_map/all_to_all | solution.py:89
  129.8 26.3 %all-to-all-done.2 = bf16[16,312,128]{2,1,0:T(8,128)(2,1)S(1)} async-done(((bf16[16,312,128]{2,1,0:T(8,128)(2,1)}), bf16[16,312,128]{2,1,0:T(8,128)(2,1)S(1)}, u32[]{:S(2)}, u32[]{:S(2)}) %all-to-all-start.2) | async-done | bytes 1277984 | tf_op jit(solution)/shard_map/all_to_all | solution.py:89
  156.1 6.5 %gather_fusion.2 = bf16[3328,128]{1,0:T(8,128)(2,1)S(1)} fusion(bf16[4992,128]{1,0:T(8,128)(2,1)S(1)} %bitcast.60, s32[4096]{0:T(1024)S(1)} %pad_clamp_fusion.1), kind=kCustom, calls=%fused_computation.3 | custom fusion | bytes 1717248 | tf_op jit(solution)/shard_map/gather | solution.py:97
  162.6 0.9 reshape.132
  163.7 0.9 copy-done.5
  164.6 6.3 %fusion.13 = (f32[128]{0:T(128)S(1)}, f32[128,3456]{1,0:T(8,128)}) fusion(bf16[128,3456]{1,0:T(8,128)(2,1)} %copy-done.5, f32[3456]{0:T(1024)} %param.27, f32[3456]{0:T(1024)} %reduce.2, bf16[1,512,3456]{2,1,0:T(8,128)(2,1)} %all-gather.5.cloned.1.call-done, bf16[1,3456,512]{2,1,0:T(8,128)(2,1)} %all-gather.3.cloned.1.call-done), kind=kOutput, calls=%fused_computation.27 | convolution fusion | flops 908689280 | bytes 9760256 | tf_op jit(solution)/shard_map/dot_general | solution.py:17
  171.6 2.1 broadcast_multiply_fusion
  173.7 5.8 %fusion.5 = f32[128,3456]{1,0:T(8,128)} fusion(bf16[1,3456,512]{2,1,0:T(8,128)(2,1)S(1)} %copy-done.2, bf16[1,512,3456]{2,1,0:T(8,128)(2,1)} %all-gather.5.cloned.1.call-done, bf16[128,3456]{1,0:T(8,128)(2,1)} %copy-done.5, f32[128]{0:T(128)S(1)} %fusion.43, f32[3456]{0:T(1024)} %param.27), kind=kOutput, calls=%fused_computation.16 | convolution fusion | flops 907804672 | bytes 9746432 | tf_op jit(solution)/shard_map/dot_general | solution.py:34
  179.5 2.7 fusion.14
  182.4 15.1 %scatter_custom_fusion.3 = f32[4992,128]{1,0:T(8,128)} fusion(s32[3328]{0:T(1024)} %copy-done.9, f32[3328,128]{1,0:T(8,128)S(1)} %reshape.198, f32[]{:T(128)} %constant.11.clone.1), kind=kCustom, calls=%fused_computation.32 | custom fusion | bytes 2556416 | tf_op jit(solution)/shard_map/scatter | solution.py:107
  197.4 6.6 %all-to-all-start.3 = ((f32[16,312,128]{2,1,0:T(8,128)}), f32[16,312,128]{2,1,0:T(8,128)}, u32[]{:S(2)}, u32[]{:S(2)}) async-start(f32[16,312,128]{2,1,0:T(8,128)} %bitcast.6), calls=%async_computation.3 | async-start | bytes 5111808 | tf_op jit(solution)/shard_map/all_to_all | solution.py:109
  204.3 2.0 lt.77
  206.3 0.8 copy.35
  207.1 1.8 reshape.133
  209.0 44.9 %all-to-all-done.3 = f32[16,312,128]{2,1,0:T(8,128)} async-done(((f32[16,312,128]{2,1,0:T(8,128)}), f32[16,312,128]{2,1,0:T(8,128)}, u32[]{:S(2)}, u32[]{:S(2)}) %all-to-all-start.3) | async-done | bytes 2555936 | tf_op jit(solution)/shard_map/all_to_all | solution.py:109
  253.9 5.7 %broadcast_in_dim.89 = f32[16,312,2,128]{3,2,1,0:T(2,128)} broadcast(f32[16,312,128]{2,1,0:T(8,128)} %all-to-all-done.3), dimensions={0,1,3} | broadcast | bytes 7667712 | tf_op jit(solution)/shard_map/jit(_where)/broadcast_in_dim | solution.py:111
  259.6 70.0 %scatter_custom_fusion.4 = f32[2048,128]{1,0:T(8,128)} fusion(s32[9984]{0:T(1024)S(1)} %fusion.39, f32[9984,128]{1,0:T(8,128)} %bitcast.62, f32[]{:T(128)} %constant.11.clone.1, pred[9984]{0:T(1024)(128)(4,1)S(1)} %lt.77), kind=kCustom, calls=%fused_computation.9 | custom fusion | flops 2555904 | bytes 6171648 | tf_op jit(solution)/shard_map/scatter-add | solution.py:115
  329.6 18.1 %reduce-scatter.2.cloned.1.call-done = f32[1024,128]{1,0:T(8,128)} async-done(((f32[2048,128]{1,0:T(8,128)}), f32[1024,128]{1,0:T(8,128)}) %reduce-scatter.2.cloned.1.call-update) | async-done | bytes 524304 | tf_op jit(solution)/shard_map/reduce_scatter | solution.py:117
  (75 shorter events, 6.9 us)
Async XLA Ops:
  7.2 49.0 %copy-start = (s32[2048]{0:T(1024)S(1)}, s32[2048]{0:T(1024)}, u32[]{:S(2)}) copy-start(s32[2048]{0:T(1024)} %param.15) | copy-start | bytes 24580
  7.2 0.8 copy-start.10
  7.2 6.7 %copy-start.13 = (s32[128,26]{0,1:T(8,128)S(1)}, s32[128,26]{0,1:T(8,128)}, u32[]{:S(2)}) copy-start(s32[128,26]{0,1:T(8,128)} %param.21) | copy-start | bytes 39940
  7.2 156.5 %all-gather.3.cloned.1.call-start = ((), (), s32[]{:S(2)}) async-start(), calls=%async_computation.5 | async-start | bytes 5308416 | tf_op jit(solution)/shard_map/all_gather | solution.py:102
  7.9 29.2 %copy-start.15 = (s32[256]{0:T(256)S(1)}, s32[256]{0:T(256)}, u32[]{:S(2)}) copy-start(s32[256]{0:T(256)} %param.16) | copy-start | bytes 3076
  8.0 29.2 %copy-start.12 = (s32[128,26,2]{0,2,1:T(2,128)S(1)}, s32[128,26,2]{0,2,1:T(2,128)}, u32[]{:S(2)}) copy-start(s32[128,26,2]{0,2,1:T(2,128)} %param.20) | copy-start | bytes 79876
  14.5 115.2 %copy-start.9 = (s32[3328]{0:T(1024)}, s32[3328]{0:T(1024)S(1)}, u32[]{:S(2)}) copy-start(s32[3328]{0:T(1024)S(1)} %fusion.40) | copy-start | bytes 39940
  28.0 32.1 %all-to-all-start = ((s32[16,1,312]{2,1,0:T(1,128)}), s32[16,1,312]{2,1,0:T(1,128)S(1)}, u32[]{:S(2)}, u32[]{:S(2)}) async-start(s32[16,1,312]{2,1,0:T(1,128)} %all_to_all.15), calls=%async_computation | async-start | bytes 49152 | tf_op jit(solution)/shard_map/all_to_all | solution.py:86
  36.3 128.3 %all-gather.5.cloned.1.call-start = ((), (), s32[]{:S(2)}) async-start(), calls=%async_computation.6 | async-start | bytes 5308416 | tf_op jit(solution)/shard_map/all_gather | solution.py:103
  38.0 20.0 %copy-start.16 = (s32[256]{0:T(256)S(1)}, s32[256]{0:T(256)}, u32[]{:S(2)}) copy-start(s32[256]{0:T(256)} %param.17) | copy-start | bytes 3076
  38.0 20.0 %copy-start.1 = (f32[2048,128]{1,0:T(8,128)S(1)}, f32[2048,128]{1,0:T(8,128)}, u32[]{:S(2)}) copy-start(f32[2048,128]{1,0:T(8,128)} %param.14) | copy-start | bytes 3145732
  38.0 20.0 %copy-start.8 = (f32[256,128]{1,0:T(8,128)S(1)}, f32[256,128]{1,0:T(8,128)}, u32[]{:S(2)}) copy-start(f32[256,128]{1,0:T(8,128)} %param.18) | copy-start | bytes 393220
  60.1 14.4 %all-to-all-start.1 = ((s32[16,312,2]{1,2,0:T(2,128)}), s32[16,312,2]{1,2,0:T(2,128)S(1)}, u32[]{:S(2)}, u32[]{:S(2)}) async-start(s32[16,312,2]{1,2,0:T(2,128)} %copy.33), calls=%async_computation.1 | async-start | bytes 98304 | tf_op jit(solution)/shard_map/all_to_all | solution.py:85
  68.1 30.9 %copy-start.3 = (pred[16,312,2]{2,1,0:T(8,128)(4,1)}, pred[16,312,2]{2,1,0:T(8,128)(4,1)S(1)}, u32[]{:S(2)}) copy-start(pred[16,312,2]{2,1,0:T(8,128)(4,1)S(1)} %iota_compare_fusion) | copy-start | bytes 29956
  74.5 5.4 %copy-start.6 = (s32[16,312,2]{1,2,0:T(2,128)}, s32[16,312,2]{1,2,0:T(2,128)S(1)}, u32[]{:S(2)}) copy-start(s32[16,312,2]{1,2,0:T(2,128)S(1)} %all-to-all-done.1) | copy-start | bytes 119812
  125.1 4.0 %copy-start.14 = (f32[1,3456]{1,0:T(1,128)S(1)}, f32[1,3456]{1,0:T(1,128)}, u32[]{:S(2)}) copy-start(f32[1,3456]{1,0:T(1,128)} %param.26) | copy-start | bytes 41476
  125.1 4.7 %copy-start.11 = (bf16[128,128]{1,0:T(8,128)(2,1)S(1)}, bf16[128,128]{1,0:T(8,128)(2,1)}, u32[]{:S(2)}) copy-start(bf16[128,128]{1,0:T(8,128)(2,1)} %param.22) | copy-start | bytes 98308
  125.1 31.0 %all-to-all-start.2 = ((bf16[16,312,128]{2,1,0:T(8,128)(2,1)}), bf16[16,312,128]{2,1,0:T(8,128)(2,1)S(1)}, u32[]{:S(2)}, u32[]{:S(2)}) async-start(bf16[16,312,128]{2,1,0:T(8,128)(2,1)} %select_reduce_fusion), calls=%async_computation.2 | async-start | bytes 2555904 | tf_op jit(solution)/shard_map/all_to_all | solution.py:89
  163.7 0.9 copy-start.5
  164.6 9.1 %copy-start.2 = (bf16[1,3456,512]{2,1,0:T(8,128)(2,1)S(1)}, bf16[1,3456,512]{2,1,0:T(8,128)(2,1)}, u32[]{:S(2)}) copy-start(bf16[1,3456,512]{2,1,0:T(8,128)(2,1)} %all-gather.3.cloned.1.call-done) | copy-start | bytes 10616836
  170.9 8.6 %copy-start.17 = (f32[128]{0:T(128)}, f32[128]{0:T(128)S(1)}, u32[]{:S(2)}) copy-start(f32[128]{0:T(128)S(1)} %get-tuple-element.2) | copy-start | bytes 1540
  197.4 6.9 %copy-start.4 = (pred[16,312,2]{2,1,0:T(8,128)(4,1)S(1)}, pred[16,312,2]{2,1,0:T(8,128)(4,1)}, u32[]{:S(2)}) copy-start(pred[16,312,2]{2,1,0:T(8,128)(4,1)} %copy-done.3) | copy-start | bytes 29956
  197.4 8.9 %copy-start.7 = (s32[16,312,2]{1,2,0:T(2,128)S(1)}, s32[16,312,2]{1,2,0:T(2,128)}, u32[]{:S(2)}) copy-start(s32[16,312,2]{1,2,0:T(2,128)} %copy-done.6) | copy-start | bytes 119812
  197.4 56.4 %all-to-all-start.3 = ((f32[16,312,128]{2,1,0:T(8,128)}), f32[16,312,128]{2,1,0:T(8,128)}, u32[]{:S(2)}, u32[]{:S(2)}) async-start(f32[16,312,128]{2,1,0:T(8,128)} %bitcast.6), calls=%async_computation.3 | async-start | bytes 5111808 | tf_op jit(solution)/shard_map/all_to_all | solution.py:109
  204.0 143.7 %reduce-scatter.2.cloned.1.call-start = ((), (), s32[]{:S(2)}) async-start(), calls=%async_computation.7 | async-start | bytes 1572864 | tf_op jit(solution)/shard_map/reduce_scatter | solution.py:117
Sparse Core Ops, SparseCore 0:
  9.6 14.8 all-gather.2
  38.7 13.9 all-gather.4
  329.7 17.9 reduce-scatter.1
where the time goes:
time: 354 us
  other arithmetic  111 us (31%)
  waiting for transfers between devices  97.1 us (27%)
  local copies, waits for them, and re-layouts  93.9 us (27%)
  starting transfers between devices  26.2 us (7%)
  between operations  14.2 us (4%)
  matrix products  12.1 us (3%)
    scatter-add x1, other arithmetic, body(): local_grad = jnp.zeros((rows_dev, emb_width), jnp.float32).at[got_rows.re...  70 us
    all_to_all x1, waiting for transfers between devices, body(): lax.all_to_all(send_grad, 'table', split_axis=0, concat_axis=0, tiled=True)  44.9 us
    all_to_all x1, waiting for transfers between devices, body(): lax.all_to_all(jnp.sum(looked_up, axis=2).astype(jnp.bfloat16), 'table',...  26.3 us
    reduce_sum x1, other arithmetic, body(): jnp.sum(looked_up, axis=2).astype(jnp.bfloat16)  26.1 us
    gather x1, local copies, waits for them, and re-layouts, body(): looked_up = jnp.where(live_mask[..., None], updated[asked_rows], 0.0)  19.1 us
    reduce_scatter x1, waiting for transfers between devices, body(): lax.psum_scatter(local_grad, 'dp', scatter_dimension=0, tiled=True)  18.1 us
    scatter x1, local copies, waits for them, and re-layouts, body(): jnp.zeros((peers * capacity, emb_width), jnp.float32).at[position]  15.1 us
    scatter x1, local copies, waits for them, and re-layouts, body(): request_rows = jnp.zeros((peers * capacity, slot_count), jnp.int32).at[po...  14.9 us
  transfers between devices with their start and end apart: 7, of which 4 were waited for; matrix products, arithmetic and copies ran while one was open for 30% of the time, Pallas kernels for 0%

commit v1 on v0

v1 whole, which is shorter than its diff:
```python
import functools

import jax
import jax.numpy as jnp
from jax import lax
from jax.experimental import pallas as pl
from jax.experimental.pallas import tpu as pltpu
from jax.sharding import PartitionSpec as P

loss_scale = 64.0
LANES = 128
F32, BF16, I32 = jnp.float32, jnp.bfloat16, jnp.int32
VMEM = pl.BlockSpec(memory_space=pltpu.VMEM)
SMEM = pl.BlockSpec(memory_space=pltpu.SMEM)
params = pltpu.CompilerParams(vmem_limit_bytes=56 * 1024 * 1024)
NT = (((1,), (1,)), ((), ()))


def dot(a, b, dims=(((1,), (0,)), ((), ()))):
    return lax.dot_general(a, b, dims, preferred_element_type=F32)


def iota(shape, axis):
    return lax.broadcasted_iota(I32, shape, axis)


def round_up(value, step):
    return -(-value // step) * step


def route_kernel(peers, cap, owner_ref, rows_ref, len_ref, pos_ref, req_ref, own_s, a_s, b_s):
    feats, lanes = len_ref.shape
    padded = own_s.shape[0]
    chunks = -(-cap // LANES)
    per = req_ref.shape[0] // peers
    count = peers * per
    own_s[...] = jnp.full(own_s.shape, -1, I32)
    own_s[0:feats, :] = owner_ref[...]
    own = own_s[...]
    hits = [(own == o).astype(F32) for o in range(peers)]
    stacked = jnp.concatenate(hits, axis=0).astype(BF16)
    row, col = iota((lanes, 2 * lanes), 0), iota((lanes, 2 * lanes), 1)
    upper = jnp.where((row < col) | (col >= lanes), 1.0, 0.0).astype(BF16)
    sums = dot(stacked, upper)
    totals = jnp.concatenate(
        [sums[o * padded : (o + 1) * padded, lanes:] for o in range(peers)], axis=1
    ).astype(BF16)
    lower = jnp.where(iota((padded, padded), 1) < iota((padded, padded), 0), 1.0, 0.0).astype(BF16)
    base = dot(lower, totals)
    rank = jnp.zeros((padded, lanes), F32)
    for o in range(peers):
        before = sums[o * padded : (o + 1) * padded, :lanes] + base[:, o * lanes : (o + 1) * lanes]
        rank = rank + hits[o] * before
    rank = rank.astype(I32)
    pos_ref[...] = (own * cap + rank)[0:feats, :]
    first = own * per + lax.shift_right_logical(rank, 7)
    second = first + chunks
    low = rank & (LANES - 1)
    lengths = len_ref[...]
    slots = rows_ref.shape[0] // feats
    ids = [
        jnp.where(lengths > slot, rows_ref[pl.ds(slot, feats, slots), :] + 1, 0)
        for slot in range(slots)
    ]
    at = iota((count, lanes), 0)
    lane_at = iota((LANES, lanes), 0)
    for f in range(feats):
        held = jnp.where(at == first[f : f + 1, :], ids[0][f : f + 1, :], 0)
        held = jnp.where(at == second[f : f + 1, :], ids[1][f : f + 1, :], held)
        span = slice(f * lanes, (f + 1) * lanes)
        a_s[0:count, span] = lax.shift_right_logical(held, 7).astype(F32).astype(BF16)
        a_s[count : 2 * count, span] = (held & 127).astype(F32).astype(BF16)
        b_s[:, span] = jnp.where(lane_at == low[f : f + 1, :], 1.0, 0.0).astype(BF16)
    found = dot(a_s[...], b_s[...], NT)
    req_ref[...] = (found[0:count] * 128.0 + found[count:]).astype(I32)


def update_kernel(local_ref, new_ref, versions_ref, table_ref, values_ref, out_ref, rows_s):
    rows_s[...] = table_ref[...]

    def entry(i, carry):
        at = local_ref[i]

        @pl.when(new_ref[i] > versions_ref[at])
        def _():
            rows_s[pl.ds(at, 1), :] = values_ref[pl.ds(i, 1), :]

        return carry

    lax.fori_loop(0, values_ref.shape[0], entry, 0, unroll=8)
    table = rows_s[...]
    width = table.shape[1]
    high = table.astype(BF16)
    out_ref[:, 0:width] = high
    out_ref[:, width:] = (table - high.astype(F32)).astype(BF16)


def lookup_kernel(peers, cap, ids_ref, table_ref, out_ref):
    rows, double = table_ref.shape
    width = double // 2
    per = ids_ref.shape[0] // peers
    chunks = -(-cap // LANES)

    def source(s, carry):
        block = ids_ref[pl.ds(pl.multiple_of(s * per, 8), per), :].T
        for c in range(chunks):
            n = min(LANES, cap - c * LANES)
            at = iota((n, rows), 1) + 1
            counts = jnp.where(at == block[0:n, c : c + 1], 1.0, 0.0) + jnp.where(
                at == block[0:n, chunks + c : chunks + c + 1], 1.0, 0.0
            )
            both = dot(counts.astype(BF16), table_ref[...])
            start = pl.multiple_of(s * cap + c * LANES, 16)
            out_ref[pl.ds(start, n), :] = (both[:, 0:width] + both[:, width:]).astype(BF16)
        return carry

    lax.fori_loop(0, peers, source, 0)


def dense_kernel(pieces, *refs):
    pos_ref, ans_ref, dense_ref, labels_ref = refs[0:4]
    down = refs[4 : 4 + pieces]
    up = refs[4 + pieces : 4 + 2 * pieces]
    bias_ref, head_ref, logit_ref, send_ref, rows_s, x_s, factor_s, bags_s = refs[4 + 2 * pieces :]
    feats, samples = pos_ref.shape
    width = dense_ref.shape[1]
    slots = ans_ref.shape[0]
    rows_s[...] = ans_ref[...].astype(F32)

    def fetch(f, carry):
        start = f * samples
        for b in range(samples):
            bags_s[pl.ds(start + b, 1), :] = rows_s[pl.ds(pos_ref[f, b], 1), :]
        return carry

    lax.fori_loop(0, feats, fetch, 0)
    x_s[:, 0:width] = dense_ref[...]
    for f in range(feats):
        x_s[:, (f + 1) * width : (f + 2) * width] = bags_s[
            f * samples : (f + 1) * samples, :
        ].astype(BF16)
    rows_s[...] = jnp.zeros(rows_s.shape, F32)
    x = x_s[...]
    crossed = [dot(x, w[...]).astype(BF16) for w in down]
    total = jnp.zeros((samples, width), F32)
    blocks = feats + 1
    for k in range(blocks):
        span = slice(k * width, (k + 1) * width)
        factor = bias_ref[:, span]
        for c, w in zip(crossed, up):
            factor = factor + dot(c, w[:, span])
        factor_s[:, span] = factor
        base = x_s[:, span].astype(F32)
        total = total + (base * factor + base) * head_ref[:, span]
    logits = jnp.sum(total, axis=1, keepdims=True)
    logit_ref[...] = logits
    signal = loss_scale * (jax.nn.sigmoid(logits) - labels_ref[...].astype(F32))
    lifts = []
    for k in range(blocks):
        span = slice(k * width, (k + 1) * width)
        lifts.append(((signal * head_ref[:, span]) * x_s[:, span].astype(F32)).astype(BF16))
    lift = jnp.concatenate(lifts, axis=1)
    back = [dot(lift, w[...], NT).astype(BF16) for w in up]
    for f in range(feats):
        span = slice((f + 1) * width, (f + 2) * width)
        outer = signal * head_ref[:, span]
        grad = outer
        for c, w in zip(back, down):
            grad = grad + dot(c, w[span, :], NT)
        bags_s[f * samples : (f + 1) * samples, :] = grad + outer * factor_s[:, span]

    def place(f, carry):
        start = f * samples
        for b in range(samples):
            rows_s[pl.ds(pos_ref[f, b], 1), :] = bags_s[pl.ds(start + b, 1), :]
        return carry

    lax.fori_loop(0, feats, place, 0)
    send_ref[...] = rows_s[...].astype(BF16)


def scatter_kernel(base_ref, ids_ref, grad_ref, out_ref):
    rows = out_ref.shape[0]
    lines = ids_ref.shape[0] // 2
    step = 4 if lines % 4 == 0 else 1
    at = iota((rows, LANES), 0) + 1 + base_ref[0]
    out_ref[...] = jnp.zeros(out_ref.shape, F32)

    def part(k, carry):
        counts = []
        for j in range(step):
            line = k * step + j
            one = ids_ref[pl.ds(line, 1), :]
            two = ids_ref[pl.ds(lines + line, 1), :]
            counts.append(
                (jnp.where(at == one, 1.0, 0.0) + jnp.where(at == two, 1.0, 0.0)).astype(BF16)
            )
        start = pl.multiple_of(k * (step * LANES), step * LANES)
        out_ref[...] += dot(
            jnp.concatenate(counts, axis=1), grad_ref[pl.ds(start, step * LANES), :]
        )
        return carry

    lax.fori_loop(0, lines // step, part, 0)


def call(kernel, outs, ins, scratch=()):
    return pl.pallas_call(
        kernel,
        out_shape=outs,
        in_specs=ins,
        out_specs=jax.tree.map(lambda _: VMEM, outs),
        scratch_shapes=list(scratch),
        compiler_params=params,
    )


def shape(dims, dtype):
    return jax.ShapeDtypeStruct(dims, dtype)


def body(
    emb_table,
    versions,
    conf_local,
    conf_version,
    conf_values,
    owners,
    row_local,
    lengths,
    dense_out,
    labels,
    cross_down,
    cross_up,
    cross_bias,
    head_weight,
):
    peers, replicas = lax.axis_size("table"), lax.axis_size("dp")
    dp_at = lax.axis_index("dp")
    rows_dev, width = emb_table.shape
    samples, feats, slots = row_local.shape
    cap = round_up(3 * samples * feats // (2 * peers), 16)
    chunks = -(-cap // LANES)
    per = round_up(slots * chunks, 8)
    total = round_up(peers * cap, LANES)
    wide = cross_down.shape[1]
    rank_dev = cross_down.shape[2]

    def shift(x, by):
        if by == 0:
            return x
        return lax.ppermute(x, "dp", [(i, (i + by) % replicas) for i in range(replicas)])

    down = [shift(cross_down[0], by) for by in range(replicas)]
    up = [shift(cross_up[0], by) for by in range(replicas)]

    position, requests = call(
        functools.partial(route_kernel, peers, cap),
        (shape((feats, samples), I32), shape((peers * per, LANES), I32)),
        [VMEM] * 3,
        [
            pltpu.VMEM((round_up(feats, 8), samples), I32),
            pltpu.VMEM((2 * peers * per, feats * samples), BF16),
            pltpu.VMEM((LANES, feats * samples), BF16),
        ],
    )(
        owners.reshape(samples, feats).T,
        row_local.transpose(1, 2, 0).reshape(feats * slots, samples),
        lengths.T,
    )
    asked = lax.all_to_all(
        requests.reshape(peers, per, LANES), "table", split_axis=0, concat_axis=0, tiled=True
    )
    updated = call(
        update_kernel,
        shape((rows_dev, 2 * width), BF16),
        [SMEM] * 3 + [VMEM] * 2,
        [pltpu.VMEM((rows_dev, width), F32)],
    )(conf_local, conf_version, versions, emb_table, conf_values)
    found = call(
        functools.partial(lookup_kernel, peers, cap),
        shape((peers * cap, width), BF16),
        [VMEM] * 2,
    )(asked.reshape(peers * per, LANES), updated)
    answer = lax.all_to_all(
        found.reshape(peers, cap, width), "table", split_axis=0, concat_axis=0, tiled=True
    )
    logits, send = call(
        functools.partial(dense_kernel, replicas),
        (shape((samples, 1), F32), shape((peers * cap, width), BF16)),
        [SMEM] + [VMEM] * (5 + 2 * replicas),
        [
            pltpu.VMEM((peers * cap, width), F32),
            pltpu.VMEM((samples, wide), BF16),
            pltpu.VMEM((samples, wide), F32),
            pltpu.VMEM((samples * feats, width), F32),
        ],
    )(
        position,
        answer.reshape(peers * cap, width),
        dense_out,
        labels.reshape(samples, 1),
        *down,
        *up,
        cross_bias,
        head_weight.reshape(1, wide),
    )
    got = lax.all_to_all(
        send.reshape(peers, cap, width), "table", split_axis=0, concat_axis=0, tiled=True
    ).reshape(peers * cap, width)
    lines = jnp.concatenate(
        [
            asked[:, slot * chunks : (slot + 1) * chunks]
            .reshape(peers, chunks * LANES)[:, :cap]
            .reshape(total // LANES, LANES)
            for slot in range(slots)
        ]
    )
    own_rows = rows_dev // replicas
    grads = None
    for by in range(replicas - 1, -1, -1):
        target = lax.rem(dp_at + by, replicas)
        part = call(
            scatter_kernel, shape((own_rows, width), F32), [SMEM] + [VMEM] * 2
        )((target * own_rows).astype(I32).reshape(1), lines, got)
        part = shift(part, by)
        grads = part if grads is None else grads + part
    return (logits.reshape(samples), grads)


def solution(mesh):
    in_specs = (
        P("table", None),
        P("table"),
        P("table"),
        P("table"),
        P("table", None),
        P(("table", "dp"), None, None),
        P(("table", "dp"), None, None),
        P(("table", "dp"), None),
        P(("table", "dp"), None),
        P(("table", "dp")),
        P(None, None, "dp"),
        P(None, "dp", None),
        P(),
        P(),
    )
    out_specs = (P(("table", "dp")), P(("table", "dp"), None))
    return jax.shard_map(body, mesh=mesh, in_specs=in_specs, out_specs=out_specs, check_vma=False)
```

time: 354 us -> 144 us (0.41)
  other arithmetic: 111 us -> 2.51 us
  local copies, waits for them, and re-layouts: 93.9 us -> 7.04 us
  Pallas kernels: 0 us -> 53.2 us
  waiting for transfers between devices: 97.1 us -> 57.5 us
  between operations: 14.2 us -> 0.73 us
  matrix products: 12.1 us -> 0 us
  starting transfers between devices: 26.2 us -> 20.3 us
    scatter-add x1 -> x0, other arithmetic: 70 us -> none  [body(): local_grad = jnp.zeros((rows_dev, emb_width), jnp.float32).at[got_rows.re...]
    pallas_call x0 -> x6, Pallas kernels: none -> 53.2 us  [the longest x2 15.3 us: body(): call(scatter_kernel, shape((own_rows, width), F32), [SMEM] + [VMEM] * 2)]
    scatter x3 -> x0, local copies, waits for them, and re-layouts: 42.7 us -> none  [the longest x1 15.1 us: body(): jnp.zeros((peers * capacity, emb_width), jnp.float32).at[position]]
    gather x3 -> x0, local copies, waits for them, and re-layouts: 27.3 us -> none  [the longest x1 19.1 us: body(): looked_up = jnp.where(live_mask[..., None], updated[asked_rows], 0.0)]
    reduce_sum x2 -> x0, other arithmetic: 26.3 us -> none  [the longest x1 26.1 us: body(): jnp.sum(looked_up, axis=2).astype(jnp.bfloat16)]
    all_to_all x4 -> x3, waiting for transfers between devices: 77.6 us -> 52.8 us  [the longest x1 28.3 us: body(): lax.all_to_all(send.reshape(peers, cap, width), 'table', split_axis=0, co...]
    reduce_scatter x1 -> x0, waiting for transfers between devices: 18.1 us -> none  [body(): lax.psum_scatter(local_grad, 'dp', scatter_dimension=0, tiled=True)]
    dot_general x2 -> x0, matrix products: 12.1 us -> none  [the longest x1 6.29 us: dense_step(): jnp.dot(crossed, cross_up[cross_index], preferred_element_type=jnp.float32)]
  transfers between devices with their start and end apart: 7 -> 6, of which waited for: 4 -> 5; matrix products, arithmetic and copies ran while one was open for 30% -> 2% of each run, Pallas kernels for 0% -> 9%
where the time goes in v1:
time: 144 us; the launch traced here: 141 us
  waiting for transfers between devices  57.5 us (40%)
  Pallas kernels  53.2 us (37%)
  starting transfers between devices  20.3 us (14%)
  local copies, waits for them, and re-layouts  7.04 us (5%)
  other arithmetic  2.51 us (2%)
    all_to_all x1, waiting for transfers between devices, body(): lax.all_to_all(send.reshape(peers, cap, width), 'table', split_axis=0, co...  28.3 us
    all_to_all x1, waiting for transfers between devices, body(): lax.all_to_all(found.reshape(peers, cap, width), 'table', split_axis=0, c...  22.4 us
    pallas_call x2, Pallas kernels, body(): call(scatter_kernel, shape((own_rows, width), F32), [SMEM] + [VMEM] * 2)  15.3 us
    pallas_call x1, Pallas kernels, body(): call(functools.partial(dense_kernel, replicas), (shape((samples, 1), F32)...  14.7 us
    pallas_call x1, Pallas kernels, body(): call(functools.partial(lookup_kernel, peers, cap), shape((peers * cap, wi...  14.6 us
    all_to_all x1, starting transfers between devices, body(): lax.all_to_all(requests.reshape(peers, per, LANES), 'table', split_axis=0...  8.31 us
    all_to_all x1, starting transfers between devices, body(): lax.all_to_all(send.reshape(peers, cap, width), 'table', split_axis=0, co...  6.43 us
    pallas_call x1, Pallas kernels, body(): call(update_kernel, shape((rows_dev, 2 * width), BF16), [SMEM] * 3 + [VME...  5.47 us
  transfers between devices with their start and end apart: 6, of which 5 were waited for; matrix products, arithmetic and copies ran while one was open for 2% of the time, Pallas kernels for 9%

profile of v1, /device:TPU:0, one launch (start us, length us, event | category | flops | bytes accessed | tf_op | source)
XLA Modules:
  0.0 141.3 jit_solution(5911572705050793059)
XLA Ops:
  0.6 1.3 copy.26
  1.9 1.4 reshape.56.rows_ref
  3.3 3.1 %shard_map.149 = (s32[26,128]{1,0:T(8,128)}, s32[128,128]{1,0:T(8,128)}) custom-call(s32[26,128]{1,0:T(8,128)} %bitcast.43, s32[52,128]{1,0:T(8,128)} %reshape.56.rows_ref, s32[26,128]{1,0:T(8,128)} %bitcast.45), custom_call_target="tpu_custom_call" | custom-call | tf_op jit(solution)/shard_map/pallas_call | solution.py:257
  6.4 8.3 %all-to-all-start = ((s32[16,8,128]{2,1,0:T(8,128)}), s32[16,8,128]{2,1,0:T(8,128)S(1)}, u32[]{:S(2)}, u32[]{:S(2)}) async-start(s32[16,8,128]{2,1,0:T(8,128)} %bitcast.42), calls=%async_computation | async-start | bytes 131072 | tf_op jit(solution)/shard_map/all_to_all | solution.py:271
  14.7 5.5 %shard_map.150.table_ref = bf16[2048,256]{1,0:T(8,128)(2,1)} custom-call(s32[256]{0:T(256)} %local_ref.1, s32[256]{0:T(256)} %new_ref.1, s32[2048]{0:T(1024)} %versions_ref.1, f32[2048,128]{1,0:T(8,128)} %table_ref.1, f32[256,128]{1,0:T(8,128)} %values_ref.1), custom_call_target="tpu_custom_call" | custom-call | tf_op jit(solution)/shard_map/pallas_call | solution.py:274
  20.2 2.1 %all-to-all-done = s32[16,8,128]{2,1,0:T(8,128)S(1)} async-done(((s32[16,8,128]{2,1,0:T(8,128)}), s32[16,8,128]{2,1,0:T(8,128)S(1)}, u32[]{:S(2)}, u32[]{:S(2)}) %all-to-all-start) | async-done | bytes 65568 | tf_op jit(solution)/shard_map/all_to_all | solution.py:271
  22.3 0.6 copy-done.3
  22.9 14.6 %shard_map.151 = bf16[5120,128]{1,0:T(8,128)(2,1)} custom-call(s32[128,128]{1,0:T(8,128)} %bitcast.37, bf16[2048,256]{1,0:T(8,128)(2,1)} %shard_map.150.table_ref), custom_call_target="tpu_custom_call" | custom-call | tf_op jit(solution)/shard_map/pallas_call | solution.py:280
  37.5 5.0 %all-to-all-start.1 = ((bf16[16,320,128]{2,1,0:T(8,128)(2,1)}), bf16[16,320,128]{2,1,0:T(8,128)(2,1)S(1)}, u32[]{:S(2)}, u32[]{:S(2)}) async-start(bf16[16,320,128]{2,1,0:T(8,128)(2,1)} %bitcast.30), calls=%async_computation.1 | async-start | bytes 2621440 | tf_op jit(solution)/shard_map/all_to_all | solution.py:285
  42.5 0.1 collective-permute-start
  42.6 0.5 collective-permute-start.1
  43.1 0.0 copy-done.7
  43.1 0.6 reshape.62.refs_9_
  43.7 0.7 copy.17.refs_3_
  44.4 3.7 %collective-permute-done.refs_5_ = bf16[3456,256]{1,0:T(8,128)(2,1)} collective-permute-done((bf16[3456,256]{1,0:T(8,128)(2,1)S(1)}, bf16[3456,256]{1,0:T(8,128)(2,1)}, u32[]{:S(2)}, u32[]{:S(2)}) %collective-permute-start) | collective-permute-done | bytes 1769504 | tf_op jit(solution)/shard_map/ppermute | solution.py:252
  48.1 1.0 collective-permute-done.1.refs_7_
  49.1 22.4 %all-to-all-done.1 = bf16[16,320,128]{2,1,0:T(8,128)(2,1)S(1)} async-done(((bf16[16,320,128]{2,1,0:T(8,128)(2,1)}), bf16[16,320,128]{2,1,0:T(8,128)(2,1)S(1)}, u32[]{:S(2)}, u32[]{:S(2)}) %all-to-all-start.1) | async-done | bytes 1310752 | tf_op jit(solution)/shard_map/all_to_all | solution.py:285
  71.5 1.1 copy-done.1
  72.6 14.7 %shard_map.152 = (f32[128,1]{1,0:T(8,128)}, bf16[5120,128]{1,0:T(8,128)(2,1)}) custom-call(s32[26,128]{1,0:T(8,128)} %get-tuple-element.6.refs_0_, bf16[5120,128]{1,0:T(8,128)(2,1)} %bitcast.31, bf16[128,128]{1,0:T(8,128)(2,1)} %refs_2_.1, s32[128,1]{1,0:T(8,128)} %copy.17.refs_3_, bf16[3456,256]{1,0:T(8,128)(2,1)} %bitcast.32, ...), custom_call_target="tpu_custom_call" | custom-call | tf_op jit(solution)/shard_map/pallas_call | solution.py:288
  87.3 6.4 %all-to-all-start.2 = ((bf16[16,320,128]{2,1,0:T(8,128)(2,1)}), bf16[16,320,128]{2,1,0:T(8,128)(2,1)S(1)}, u32[]{:S(2)}, u32[]{:S(2)}) async-start(bf16[16,320,128]{2,1,0:T(8,128)(2,1)} %bitcast.36), calls=%async_computation.2 | async-start | bytes 2621440 | tf_op jit(solution)/shard_map/all_to_all | solution.py:308
  93.8 0.0 copy-done.4
  93.8 0.1 reshape.68
  93.9 0.1 reshape.66
  94.0 0.0 copy-start.5
  94.0 28.3 %all-to-all-done.2 = bf16[16,320,128]{2,1,0:T(8,128)(2,1)S(1)} async-done(((bf16[16,320,128]{2,1,0:T(8,128)(2,1)}), bf16[16,320,128]{2,1,0:T(8,128)(2,1)S(1)}, u32[]{:S(2)}, u32[]{:S(2)}) %all-to-all-start.2) | async-done | bytes 1310752 | tf_op jit(solution)/shard_map/all_to_all | solution.py:308
  122.3 1.1 copy-done
  123.4 7.7 %shard_map.153 = f32[1024,128]{1,0:T(8,128)} custom-call(s32[1]{0:T(128)} %bitcast.10.base_ref, s32[80,128]{1,0:T(8,128)} %copy-done.5, bf16[5120,128]{1,0:T(8,128)(2,1)} %bitcast.28), custom_call_target="tpu_custom_call" | custom-call | tf_op jit(solution)/shard_map/pallas_call | solution.py:323
  131.1 0.0 collective-permute-start.2
  131.1 0.6 reduce
  131.7 7.7 %shard_map.154 = f32[1024,128]{1,0:T(8,128)} custom-call(s32[1]{0:T(128)} %bitcast.13.base_ref, s32[80,128]{1,0:T(8,128)} %copy-done.5, bf16[5120,128]{1,0:T(8,128)(2,1)} %bitcast.29), custom_call_target="tpu_custom_call" | custom-call | tf_op jit(solution)/shard_map/pallas_call | solution.py:323
  139.4 0.0 collective-permute-done.2
  139.4 1.9 %add.7 = f32[1024,128]{1,0:T(8,128)} add(f32[1024,128]{1,0:T(8,128)S(1)} %collective-permute-done.2, f32[1024,128]{1,0:T(8,128)} %shard_map.154) | non-fusion elementwise | flops 131072 | bytes 1572864 | tf_op jit(solution)/shard_map/add | solution.py:327
  (17 shorter events, 0.0 us)
Async XLA Ops:
  6.4 15.9 %all-to-all-start = ((s32[16,8,128]{2,1,0:T(8,128)}), s32[16,8,128]{2,1,0:T(8,128)S(1)}, u32[]{:S(2)}, u32[]{:S(2)}) async-start(s32[16,8,128]{2,1,0:T(8,128)} %bitcast.42), calls=%async_computation | async-start | bytes 131072 | tf_op jit(solution)/shard_map/all_to_all | solution.py:271
  22.2 0.6 copy-start.3
  37.5 5.0 %copy-start.2 = (bf16[1,3456,256]{2,1,0:T(8,128)(2,1)S(1)}, bf16[1,3456,256]{2,1,0:T(8,128)(2,1)}, u32[]{:S(2)}) copy-start(bf16[1,3456,256]{2,1,0:T(8,128)(2,1)} %param.24) | copy-start | bytes 5308420
  37.5 5.6 %copy-start.7 = (f32[3456]{0:T(1024)S(1)}, f32[3456]{0:T(1024)}, u32[]{:S(2)}) copy-start(f32[3456]{0:T(1024)} %param.27) | copy-start | bytes 41476
  37.5 6.2 %copy-start.8 = (s32[128]{0:T(128)S(1)}, s32[128]{0:T(128)}, u32[]{:S(2)}) copy-start(s32[128]{0:T(128)} %param.23) | copy-start | bytes 1540
  37.5 34.0 %all-to-all-start.1 = ((bf16[16,320,128]{2,1,0:T(8,128)(2,1)}), bf16[16,320,128]{2,1,0:T(8,128)(2,1)S(1)}, u32[]{:S(2)}, u32[]{:S(2)}) async-start(bf16[16,320,128]{2,1,0:T(8,128)(2,1)} %bitcast.30), calls=%async_computation.1 | async-start | bytes 2621440 | tf_op jit(solution)/shard_map/all_to_all | solution.py:285
  42.5 5.6 %collective-permute-start = (bf16[3456,256]{1,0:T(8,128)(2,1)S(1)}, bf16[3456,256]{1,0:T(8,128)(2,1)}, u32[]{:S(2)}, u32[]{:S(2)}) collective-permute-start(bf16[3456,256]{1,0:T(8,128)(2,1)S(1)} %bitcast.33), channel_id=1, source_target_pairs={{0,1},{1,0},{2,3},{3,2},{4,5},{5,4},{6,7},{7,6},{8,9},{9,8},{10,11... | collective-permute-start | bytes 5308424 | tf_op jit(solution)/shard_map/ppermute | solution.py:252
  42.6 6.5 %collective-permute-start.1 = (bf16[256,3456]{1,0:T(8,128)(2,1)}, bf16[256,3456]{1,0:T(8,128)(2,1)}, u32[]{:S(2)}, u32[]{:S(2)}) collective-permute-start(bf16[256,3456]{1,0:T(8,128)(2,1)} %bitcast.34), channel_id=1, source_target_pairs={{0,1},{1,0},{2,3},{3,2},{4,5},{5,4},{6,7},{7,6},{8,9},{9,8},{10,11... | collective-permute-start | bytes 5308424 | tf_op jit(solution)/shard_map/ppermute | solution.py:252
  71.5 1.1 copy-start.1
  87.3 6.5 %copy-start.4 = (s32[16,8,128]{2,1,0:T(8,128)S(1)}, s32[16,8,128]{2,1,0:T(8,128)}, u32[]{:S(2)}) copy-start(s32[16,8,128]{2,1,0:T(8,128)} %copy-done.3) | copy-start | bytes 196612
  87.3 35.0 %all-to-all-start.2 = ((bf16[16,320,128]{2,1,0:T(8,128)(2,1)}), bf16[16,320,128]{2,1,0:T(8,128)(2,1)S(1)}, u32[]{:S(2)}, u32[]{:S(2)}) async-start(bf16[16,320,128]{2,1,0:T(8,128)(2,1)} %bitcast.36), calls=%async_computation.2 | async-start | bytes 2621440 | tf_op jit(solution)/shard_map/all_to_all | solution.py:308
  93.8 37.3 %copy-start.6 = (f32[128,1]{1,0:T(8,128)S(1)}, f32[128,1]{1,0:T(8,128)}, u32[]{:S(2)}) copy-start(f32[128,1]{1,0:T(8,128)} %get-tuple-element.8) | copy-start | bytes 1540
  94.0 28.3 %copy-start.5 = (s32[80,128]{1,0:T(8,128)}, s32[80,128]{1,0:T(8,128)S(1)}, u32[]{:S(2)}) copy-start(s32[80,128]{1,0:T(8,128)S(1)} %constant_dynamic-update-slice_fusion.ids_ref) | copy-start | bytes 122884
  122.3 1.1 copy-start
  131.1 8.3 %collective-permute-start.2 = (f32[1024,128]{1,0:T(8,128)}, f32[1024,128]{1,0:T(8,128)S(1)}, u32[]{:S(2)}, u32[]{:S(2)}) collective-permute-start(f32[1024,128]{1,0:T(8,128)} %shard_map.153), channel_id=1, source_target_pairs={{0,1},{1,0},{2,3},{3,2},{4,5},{5,4},{6,7},{7,6},{8,9},{9,8},{10,11... | collective-permute-start | bytes 1572872 | tf_op jit(solution)/shard_map/ppermute | solution.py:252

commit v2 on v1

v2 whole, which is shorter than its diff:
```python
import functools

import jax
import jax.numpy as jnp
from jax import lax
from jax.experimental import pallas as pl
from jax.experimental.pallas import tpu as pltpu
from jax.sharding import PartitionSpec as P

loss_scale = 64.0
LANES = 128
F32, BF16, I32, I16 = jnp.float32, jnp.bfloat16, jnp.int32, jnp.int16
VMEM = pl.BlockSpec(memory_space=pltpu.VMEM)
SMEM = pl.BlockSpec(memory_space=pltpu.SMEM)
ANY = pl.BlockSpec(memory_space=pl.ANY)
params = pltpu.CompilerParams(vmem_limit_bytes=36 * 1024 * 1024)
NT = (((1,), (1,)), ((), ()))


def dot(a, b, dims=(((1,), (0,)), ((), ()))):
    return lax.dot_general(a, b, dims, preferred_element_type=F32)


def iota(shape, axis):
    return lax.broadcasted_iota(I32, shape, axis)


def round_up(value, step):
    return -(-value // step) * step


def route_kernel(
    peers, cap, owner_ref, rows_ref, len_ref, pos_ref, req_ref, own_s, one_s, two_s, a_s, b_s
):
    feats, lanes = len_ref.shape
    padded = own_s.shape[0]
    chunks = -(-cap // LANES)
    half = peers // 2
    per = req_ref.shape[0] // peers
    count = peers * per
    own_s[...] = jnp.full(own_s.shape, -1, I32)
    for f in range(feats):
        own_s[f : f + 1, :] = owner_ref[f]
        one_s[f : f + 1, :] = rows_ref[f, 0:1, :]
        two_s[f : f + 1, :] = rows_ref[f, 1:2, :]
    own = own_s[...]
    hits = [(own == o).astype(F32) for o in range(peers)]
    stacked = jnp.concatenate(hits, axis=0).astype(BF16)
    row, col = iota((lanes, 2 * lanes), 0), iota((lanes, 2 * lanes), 1)
    upper = jnp.where((row < col) | (col >= lanes), 1.0, 0.0).astype(BF16)
    sums = dot(stacked, upper)
    totals = jnp.concatenate(
        [sums[o * padded : (o + 1) * padded, lanes:] for o in range(peers)], axis=1
    ).astype(BF16)
    lower = jnp.where(iota((padded, padded), 1) < iota((padded, padded), 0), 1.0, 0.0).astype(BF16)
    base = dot(lower, totals)
    rank = jnp.zeros((padded, lanes), F32)
    for o in range(peers):
        before = sums[o * padded : (o + 1) * padded, :lanes] + base[:, o * lanes : (o + 1) * lanes]
        rank = rank + hits[o] * before
    rank = rank.astype(I32)
    far = own >= half
    column = jnp.where(far, own - half, own)
    side = (lax.axis_index("table") >= half).astype(I32)
    mirrored = jnp.where(far, 1 - side, side)
    place = jnp.where(own < 0, -8, column * 2 + mirrored)
    pos_ref[...] = (place * cap + rank)[0:feats, :]
    first = place * per + lax.shift_right_logical(rank, 7)
    second = first + chunks
    low = rank & (LANES - 1)
    lengths = len_ref[...]
    one = jnp.where(lengths > 0, one_s[0:feats, :] + 1, 0)
    two = jnp.where(lengths > 1, two_s[0:feats, :] + 1, 0)
    at = iota((count, lanes), 0)
    lane_at = iota((LANES, lanes), 0)
    for f in range(feats):
        held = jnp.where(at == first[f : f + 1, :], one[f : f + 1, :], 0)
        held = jnp.where(at == second[f : f + 1, :], two[f : f + 1, :], held)
        span = slice(f * lanes, (f + 1) * lanes)
        a_s[0:count, span] = lax.shift_right_logical(held, 7).astype(F32).astype(BF16)
        a_s[count : 2 * count, span] = (held & 127).astype(F32).astype(BF16)
        b_s[:, span] = jnp.where(lane_at == low[f : f + 1, :], 1.0, 0.0).astype(BF16)
    found = dot(a_s[...], b_s[...], NT)
    req_ref[...] = (found[0:count] * 128.0 + found[count:]).astype(I32)


def update_kernel(
    after_ref, local_ref, new_ref, versions_ref, table_ref, values_ref, table_out_ref, part_ref, rows_s
):
    del after_ref
    held_rows, width = table_ref.shape
    rows_s[0:held_rows, :] = table_ref[...]

    def entry(i, carry):
        at = local_ref[i]
        to = jnp.where(new_ref[i] > versions_ref[at], at, held_rows)
        rows_s[pl.ds(to, 1), :] = values_ref[pl.ds(i, 1), :]
        return carry

    lax.fori_loop(0, values_ref.shape[0], entry, 0, unroll=8)
    table = rows_s[0:held_rows, :]
    high = table.astype(BF16)
    table_out_ref[:, 0:width] = high
    table_out_ref[:, width:] = (table - high.astype(F32)).astype(BF16)
    own_rows = part_ref.shape[0]
    start = pl.multiple_of(lax.axis_index("dp") * own_rows, own_rows)
    part_ref[...] = rows_s[pl.ds(start, own_rows), :].astype(BF16)


def lookup_kernel(kind, peers, cap, ids_ref, *refs):
    out_ref, count_s, found_s, sems = refs[-4:]
    tables = refs[:-4] if kind == 0 else refs[1:-4]
    width = out_ref.shape[1]
    per = ids_ref.shape[0] // (2 * peers)
    chunks = -(-cap // LANES)
    group = count_s.shape[1] // cap
    one, zero = jnp.ones((), BF16), jnp.zeros((), BF16)
    pieces = len(tables)
    at_dp = lax.axis_index("dp")
    bases = [lax.rem(at_dp + pieces - p, pieces) * tables[p].shape[0] for p in range(pieces)]

    def count(i):
        for g in range(group):
            start = ((i * group + g) * 2 + kind) * per
            block = ids_ref[start : start + per, :].T
            for c in range(chunks):
                n = min(LANES, cap - c * LANES)
                at = g * cap + c * LANES
                a = jnp.broadcast_to(block[0:n, c : c + 1], (n, LANES))
                b = jnp.broadcast_to(block[0:n, chunks + c : chunks + c + 1], (n, LANES))
                column = 0
                for p, table in enumerate(tables):
                    a16 = (a - bases[p]).astype(I16)
                    b16 = (b - bases[p]).astype(I16)
                    for k in range(0, table.shape[0], LANES):
                        size = min(LANES, table.shape[0] - k)
                        row = (iota((n, size), 1) + (1 + k)).astype(I16)
                        count_s[i % 2, at : at + n, column : column + size] = jnp.where(
                            a16[:, :size] == row, one, zero
                        ) + jnp.where(b16[:, :size] == row, one, zero)
                        column += size

    def multiply(i):
        total = None
        column = 0
        for table in tables:
            rows, span = table.shape
            both = dot(count_s[i % 2, :, column : column + rows], table[...])
            if span > width:
                both = both[:, 0:width] + both[:, width:]
            total = both if total is None else total + both
            column += rows
        found_s[i * group * cap : (i + 1) * group * cap, :] = total.astype(BF16)

    def move(source):
        return pltpu.make_async_copy(
            found_s.at[source * cap : (source + 1) * cap, :],
            out_ref.at[(2 * source + kind) * cap : (2 * source + kind + 1) * cap, :],
            sems.at[source],
        )

    steps = peers // group
    count(0)
    for i in range(steps):
        if i + 1 < steps:
            count(i + 1)
        multiply(i)
        for source in range(i * group, (i + 1) * group):
            move(source).start()
    for source in range(peers):
        move(source).wait()


def dense_kernel(pieces, *refs):
    pos_ref, answer_ref, dense_ref, labels_ref = refs[0:4]
    (
        bias_ref, head_ref, logit_ref, send_ref, rows_s, x_s, factor_s, bags_s, down_s, up_s, sems,
    ) = refs[4 + 2 * pieces :]
    loads = []
    for p in range(pieces):
        loads.append(pltpu.make_async_copy(refs[4 + p], down_s.at[p], sems.at[p]))
    for p in range(pieces):
        loads.append(pltpu.make_async_copy(refs[4 + pieces + p], up_s.at[p], sems.at[pieces + p]))
    for load in loads:
        load.start()
    down = [down_s.at[p] for p in range(pieces)]
    up = [up_s.at[p] for p in range(pieces)]
    feats, samples = pos_ref.shape
    width = dense_ref.shape[1]
    rows_s[...] = answer_ref[...].astype(F32)

    def fetch(f, carry):
        start = f * samples
        for b in range(samples):
            bags_s[pl.ds(start + b, 1), :] = rows_s[pl.ds(pos_ref[f, b], 1), :]
        return carry

    lax.fori_loop(0, feats, fetch, 0)
    x_s[:, 0:width] = dense_ref[...]
    for f in range(feats):
        x_s[:, (f + 1) * width : (f + 2) * width] = bags_s[
            f * samples : (f + 1) * samples, :
        ].astype(BF16)
    rows_s[...] = jnp.zeros(rows_s.shape, F32)
    for load in loads:
        load.wait()
    x = x_s[...]
    crossed = [dot(x, w[...]).astype(BF16) for w in down]
    total = jnp.zeros((samples, width), F32)
    blocks = feats + 1
    for k in range(blocks):
        span = slice(k * width, (k + 1) * width)
        factor = bias_ref[:, span]
        for c, w in zip(crossed, up):
            factor = factor + dot(c, w[:, span])
        factor_s[:, span] = factor
        base = x_s[:, span].astype(F32)
        total = total + (base * factor + base) * head_ref[:, span]
    logits = jnp.sum(total, axis=1, keepdims=True)
    logit_ref[...] = jnp.broadcast_to(logits, (samples, samples)).T[0:1, :]
    labels = jnp.broadcast_to(labels_ref[...].astype(F32), (samples, samples)).T[:, 0:1]
    signal = loss_scale * (jax.nn.sigmoid(logits) - labels)
    lifts = []
    for k in range(blocks):
        span = slice(k * width, (k + 1) * width)
        lifts.append(((signal * head_ref[:, span]) * x_s[:, span].astype(F32)).astype(BF16))
    lift = jnp.concatenate(lifts, axis=1)
    back = [dot(lift, w[...], NT).astype(BF16) for w in up]
    for f in range(feats):
        span = slice((f + 1) * width, (f + 2) * width)
        outer = signal * head_ref[:, span]
        grad = outer
        for c, w in zip(back, down):
            grad = grad + dot(c, w[span, :], NT)
        bags_s[f * samples : (f + 1) * samples, :] = grad + outer * factor_s[:, span]

    def place(f, carry):
        start = f * samples
        for b in range(samples):
            rows_s[pl.ds(pos_ref[f, b], 1), :] = bags_s[pl.ds(start + b, 1), :]
        return carry

    lax.fori_loop(0, feats, place, 0)
    send_ref[...] = rows_s[...].astype(BF16)


def scatter_kernel(cap, kind, by, after_ref, ids_ref, grad_ref, *refs):
    del after_ref
    out_ref, bags_s = refs[-2:]
    rows = out_ref.shape[0]
    first = lax.rem(lax.axis_index("dp") + by, lax.axis_size("dp")) * rows
    tile = min(rows, 512)
    lines = ids_ref.shape[0] // 2
    step = 4 if lines % 4 == 0 else 1
    one, zero = jnp.ones((), BF16), jnp.zeros((), BF16)
    at = (iota((tile, LANES), 0) + 1).astype(I16)
    for source in range(bags_s.shape[0] // cap):
        start = (2 * source + kind) * cap
        bags_s[source * cap : (source + 1) * cap, :] = grad_ref[start : start + cap, :]

    def part(r, carry):
        base = first + r * tile
        here = pl.ds(pl.multiple_of(r * tile, tile), tile)
        total = jnp.zeros((tile, LANES), F32) if len(refs) == 2 else refs[0][here, :]
        for k in range(0, lines, step):
            counts = []
            for line in range(k, k + step):
                a = jnp.broadcast_to(ids_ref[line : line + 1, :] - base, (tile, LANES)).astype(I16)
                b = jnp.broadcast_to(
                    ids_ref[lines + line : lines + line + 1, :] - base, (tile, LANES)
                ).astype(I16)
                counts.append(jnp.where(a == at, one, zero) + jnp.where(b == at, one, zero))
            total = total + dot(
                jnp.concatenate(counts, axis=1), bags_s[k * LANES : (k + step) * LANES, :]
            )
        out_ref[here, :] = total.astype(out_ref.dtype)
        return carry

    lax.fori_loop(0, rows // tile, part, 0)


def call(kernel, outs, ins, scratch=()):
    return pl.pallas_call(
        kernel,
        out_shape=outs,
        in_specs=ins,
        out_specs=jax.tree.map(lambda _: VMEM, outs),
        scratch_shapes=list(scratch),
        compiler_params=params,
    )


def in_hbm(x):
    return pltpu.with_memory_space_constraint(x, pltpu.HBM)


def in_vmem(x):
    return pltpu.with_memory_space_constraint(x, pltpu.VMEM)


def shape(dims, dtype):
    return jax.ShapeDtypeStruct(dims, dtype)


def body(
    emb_table,
    versions,
    conf_local,
    conf_version,
    conf_values,
    owners,
    row_local,
    lengths,
    dense_out,
    labels,
    cross_down,
    cross_up,
    cross_bias,
    head_weight,
):
    peers, replicas = lax.axis_size("table"), lax.axis_size("dp")
    half = peers // 2
    groups = [list(range(half)), list(range(half, peers))]
    rows_dev, width = emb_table.shape
    samples, feats, slots = row_local.shape
    cap = round_up(3 * samples * feats // (2 * peers), 16)
    chunks = -(-cap // LANES)
    per = round_up(slots * chunks, 8)
    lines_half = half * cap // LANES
    wide = cross_down.shape[1]
    own_rows = rows_dev // replicas

    def shift(x, by):
        if by == 0:
            return x
        return lax.ppermute(x, "dp", [(i, (i + by) % replicas) for i in range(replicas)])

    def across(x):
        return lax.ppermute(x, "table", [(i, (i + half) % peers) for i in range(peers)])

    def exchange(x):
        return lax.all_to_all(
            x, "table", split_axis=0, concat_axis=0, axis_index_groups=groups, tiled=True
        )

    down = [shift(cross_down[0], by) for by in range(replicas)]
    up = [shift(cross_up[0], by) for by in range(replicas)]

    position, requests = call(
        functools.partial(route_kernel, peers, cap),
        (shape((feats, samples), I32), shape((peers * per, LANES), I32)),
        [VMEM] * 3,
        [pltpu.VMEM((round_up(feats, 8), samples), I32)] * 3
        + [
            pltpu.VMEM((2 * peers * per, feats * samples), BF16),
            pltpu.VMEM((LANES, feats * samples), BF16),
        ],
    )(*map(in_hbm, (owners.transpose(1, 2, 0), row_local.transpose(1, 2, 0), lengths.T)))
    asked = exchange(requests.reshape(half, 2 * per, LANES)).reshape(2 * half * per, LANES)
    table, part = call(
        update_kernel,
        (shape((rows_dev, 2 * width), BF16), shape((own_rows, width), BF16)),
        [ANY] + [SMEM] * 3 + [VMEM] * 2,
        [pltpu.VMEM((rows_dev + 8, width), F32)],
    )(requests, *map(in_hbm, (conf_local, conf_version, versions, emb_table, conf_values)))
    part = across(part)
    part, asked = lax.optimization_barrier((part, asked))
    mirror = [shift(part, by) for by in range(replicas)]

    group = max(g for g in range(1, half + 1) if half % g == 0 and g * cap <= 2 * 320)

    def lookup(kind, tables, filled=()):
        rows = sum(t.shape[0] for t in tables)
        return pl.pallas_call(
            functools.partial(lookup_kernel, kind, half, cap),
            out_shape=shape((peers * cap, width), BF16),
            in_specs=[VMEM] + [ANY] * len(filled) + [VMEM] * len(tables),
            out_specs=ANY,
            scratch_shapes=[
                pltpu.VMEM((2, group * cap, rows), BF16),
                pltpu.VMEM((half * cap, width), BF16),
                pltpu.SemaphoreType.DMA((half,)),
            ],
            input_output_aliases={1: 0} if filled else {},
            compiler_params=params,
        )(asked, *filled, *tables)

    found = lookup(0, [table])
    found = lookup(1, mirror, (found,))
    answer = exchange(found.reshape(half, 2 * cap, width)).reshape(peers * cap, width)
    answer = in_vmem(answer)

    logits, send = call(
        functools.partial(dense_kernel, replicas),
        (shape((1, samples), F32), shape((peers * cap, width), BF16)),
        [SMEM] + [VMEM] * 3 + [ANY] * (2 * replicas) + [VMEM] * 2,
        [
            pltpu.VMEM((peers * cap, width), F32),
            pltpu.VMEM((samples, wide), BF16),
            pltpu.VMEM((samples, wide), F32),
            pltpu.VMEM((samples * feats, width), F32),
            pltpu.VMEM((replicas,) + down[0].shape, BF16),
            pltpu.VMEM((replicas,) + up[0].shape, BF16),
            pltpu.SemaphoreType.DMA((2 * replicas,)),
        ],
    )(
        position,
        answer,
        dense_out,
        labels.reshape(1, samples),
        *map(in_hbm, down),
        *map(in_hbm, up),
        cross_bias,
        head_weight.reshape(1, wide),
    )
    asked = asked.reshape(half, 2, per, LANES)
    got = exchange(send.reshape(half, 2 * cap, width)).reshape(peers * cap, width)
    got = in_vmem(got)

    def scatter(kind, by, after, init=()):
        lines = jnp.concatenate(
            [
                asked[:, kind, slot * chunks : (slot + 1) * chunks]
                .reshape(half, chunks * LANES)[:, :cap]
                .reshape(lines_half, LANES)
                for slot in range(slots)
            ]
        )
        return call(
            functools.partial(scatter_kernel, cap, kind, by),
            shape((own_rows, width), F32),
            [ANY] + [VMEM] * (2 + len(init)),
            [pltpu.VMEM((half * cap, width), BF16)],
        )(after, lines, got, *init)

    last = asked
    returned, total = None, None
    for by in range(1, replicas):
        last = scatter(1, by, last)
        part = shift(last, by)
        returned = part if returned is None else returned + part
    last = scatter(1, 0, last)
    last = (last if returned is None else returned + last).astype(BF16)
    returned = across(last)
    for by in range(1, replicas):
        last = scatter(0, by, last)
        part = shift(last, by)
        total = part if total is None else total + part
    total = scatter(0, 0, last, () if total is None else (total,))
    grads = total + returned.astype(F32)
    return (logits.reshape(samples), grads)


def solution(mesh):
    in_specs = (
        P("table", None),
        P("table"),
        P("table"),
        P("table"),
        P("table", None),
        P(("table", "dp"), None, None),
        P(("table", "dp"), None, None),
        P(("table", "dp"), None),
        P(("table", "dp"), None),
        P(("table", "dp")),
        P(None, None, "dp"),
        P(None, "dp", None),
        P(),
        P(),
    )
    out_specs = (P(("table", "dp")), P(("table", "dp"), None))
    return jax.shard_map(body, mesh=mesh, in_specs=in_specs, out_specs=out_specs, check_vma=False)
```

time: 144 us -> 113 us (0.78); the launches traced: 141 us -> 113 us
  Pallas kernels: 53.2 us -> 35 us
  blocking collectives: 0 us -> 14.1 us
  waiting for transfers between devices: 57.5 us -> 45.9 us
  starting transfers between devices: 20.3 us -> 14.8 us
  local copies, waits for them, and re-layouts: 7.04 us -> 1.59 us
  other arithmetic: 2.51 us -> 0.91 us
    all_to_all x3 -> x2, waiting for transfers between devices: 52.8 us -> 28.5 us  [exchange(): lax.all_to_all(x, 'table', split_axis=0, concat_axis=0, axis_index_groups...]
    pallas_call x5 -> x8, Pallas kernels: 50.1 us -> 32.6 us  [the longest x1 12.1 us: body(): call(functools.partial(dense_kernel, replicas), (shape((1, samples), F32)...]
    all_to_all x0 -> x1, blocking collectives: none -> 14.1 us  [exchange(): lax.all_to_all(x, 'table', split_axis=0, concat_axis=0, axis_index_groups...]
    ppermute x0 -> x2, waiting for transfers between devices: none -> 11.5 us  [across(): lax.ppermute(x, 'table', [(i, (i + half) % peers) for i in range(peers)])]
    all_to_all x3 -> x2, starting transfers between devices: 19.7 us -> 8.77 us  [exchange(): lax.all_to_all(x, 'table', split_axis=0, concat_axis=0, axis_index_groups...]
    ppermute x0 -> x2, starting transfers between devices: none -> 4.74 us  [across(): lax.ppermute(x, 'table', [(i, (i + half) % peers) for i in range(peers)])]
    unnamed x22 -> x13, local copies, waits for them, and re-layouts: 4.16 us -> 1.28 us
    reshape x4, local copies, waits for them, and re-layouts: 2.26 us -> 0.29 us  [scatter(): lines = jnp.concatenate([asked[:, kind, slot * chunks:(slot + 1) * chunks...]
  transfers between devices with their start and end apart: 6 -> 9, of which waited for: 5 -> 5; matrix products, arithmetic and copies ran while one was open for 2% -> 0% of each run, Pallas kernels for 9% -> 8%
where the time goes in v2:
time: 113 us
  waiting for transfers between devices  45.9 us (41%)
  Pallas kernels  35 us (31%)
  starting transfers between devices  14.8 us (13%)
  blocking collectives  14.1 us (12%)
  local copies, waits for them, and re-layouts  1.59 us (1%)
    all_to_all x2, waiting for transfers between devices, exchange(): lax.all_to_all(x, 'table', split_axis=0, concat_axis=0, axis_index_groups...  28.5 us
    all_to_all x1, blocking collectives, exchange(): lax.all_to_all(x, 'table', split_axis=0, concat_axis=0, axis_index_groups...  14.1 us
    pallas_call x1, Pallas kernels, body(): call(functools.partial(dense_kernel, replicas), (shape((1, samples), F32)...  12.1 us
    ppermute x2, waiting for transfers between devices, across(): lax.ppermute(x, 'table', [(i, (i + half) % peers) for i in range(peers)])  11.5 us
    pallas_call x2, Pallas kernels, lookup(): pl.pallas_call(functools.partial(lookup_kernel, kind, half, cap), out_sha...  11.3 us
    all_to_all x2, starting transfers between devices, exchange(): lax.all_to_all(x, 'table', split_axis=0, concat_axis=0, axis_index_groups...  8.77 us
    pallas_call x4, Pallas kernels, scatter(): call(functools.partial(scatter_kernel, cap, kind, by), shape((own_rows, w...  6.97 us
    ppermute x5, waiting for transfers between devices, shift(): lax.ppermute(x, 'dp', [(i, (i + by) % replicas) for i in range(replicas)])  5.87 us
  transfers between devices with their start and end apart: 9, of which 5 were waited for; matrix products, arithmetic and copies ran while one was open for 0% of the time, Pallas kernels for 8%

profile of v2, /device:TPU:0, one launch (start us, length us, event | category | flops | bytes accessed | tf_op | source)
XLA Modules:
  0.0 113.1 jit_solution(13231496481707433928)
XLA Ops:
  0.6 2.4 %shard_map.149 = (s32[26,128]{1,0:T(8,128)S(1)}, s32[128,128]{1,0:T(8,128)S(1)}) custom-call(s32[26,1,128]{2,1,0:T(1,128)} %bitcast.59, s32[26,2,128]{2,1,0:T(2,128)} %bitcast.57, s32[26,128]{1,0:T(8,128)} %bitcast.58), custom_call_target="tpu_custom_call" | custom-call | tf_op jit(solution)/shard_map/pallas_call | solution.py:349
  3.1 2.2 %shard_map.150 = (bf16[2048,256]{1,0:T(8,128)(2,1)S(1)}, bf16[1024,128]{1,0:T(8,128)(2,1)S(1)}) custom-call(s32[128,128]{1,0:T(8,128)S(1)} %get-tuple-element.11.after_ref, s32[256]{0:T(256)} %local_ref.1, s32[256]{0:T(256)} %new_ref.1, s32[2048]{0:T(1024)} %versions_ref.1, f32[2048,128]{1,0:T(8,128)} %table_ref.1, f32[256,128]{1,0:T(8,128)} %values_ref.1), custom_call_target="tpu_custom_call" | custom-call | tf_op jit(solution)/shard_map/pallas_call | solution.py:360
  5.3 4.1 %collective-permute-start = (bf16[1024,128]{1,0:T(8,128)(2,1)S(1)}, bf16[1024,128]{1,0:T(8,128)(2,1)S(1)}, u32[]{:S(2)}, u32[]{:S(2)}) collective-permute-start(bf16[1024,128]{1,0:T(8,128)(2,1)S(1)} %get-tuple-element.12), channel_id=1, source_target_pairs={{0,16},{2,18},{4,20},{6,22},{8,24},{10,26},{12,28},{14,30},{16,0},... | collective-permute-start | bytes 786440 | tf_op jit(solution)/shard_map/ppermute | solution.py:339
  9.4 14.1 %all_to_all.15 = s32[8,16,128]{2,1,0:T(8,128)S(1)} all-to-all(s32[8,16,128]{2,1,0:T(8,128)S(1)} %bitcast.47), channel_id=1, replica_groups={{0,2,4,6,8,10,12,14},{16,18,20,22,24,26,28,30},{1,3,5,7,9,11,13,15},{17..., dimensions={0} | all-to-all | bytes 131072 | tf_op jit(solution)/shard_map/all_to_all | solution.py:342
  23.5 5.3 %shard_map.151.refs_0_ = bf16[5120,128]{1,0:T(8,128)(2,1)} custom-call(s32[128,128]{1,0:T(8,128)S(1)} %bitcast.43, bf16[2048,256]{1,0:T(8,128)(2,1)S(1)} %get-tuple-element.14.refs_0_), custom_call_target="tpu_custom_call" | custom-call | tf_op jit(solution)/shard_map/pallas_call | solution.py:374
  28.9 6.0 %shard_map.152 = bf16[5120,128]{1,0:T(8,128)(2,1)} custom-call(s32[128,128]{1,0:T(8,128)S(1)} %bitcast.44, bf16[5120,128]{1,0:T(8,128)(2,1)} %shard_map.151.refs_0_, bf16[1024,128]{1,0:T(8,128)(2,1)S(1)} %collective-permute-done.refs_1_, bf16[1024,128]{1,0:T(8,128)(2,1)S(1)} %collective-permute-done.1.refs_2_), custom_call_target="tpu_custom_call", output_to_operand_aliasing={{}: (1, {})} | custom-call | tf_op jit(solution)/shard_map/pallas_call | solution.py:374
  34.9 0.0 copy-start
  34.9 0.0 copy-start.1
  34.9 3.9 %all-to-all-start.1 = ((bf16[8,640,128]{2,1,0:T(8,128)(2,1)}), bf16[8,640,128]{2,1,0:T(8,128)(2,1)S(1)}, u32[]{:S(2)}, u32[]{:S(2)}) async-start(bf16[8,640,128]{2,1,0:T(8,128)(2,1)} %bitcast.5), calls=%async_computation.1 | async-start | bytes 2621440 | tf_op jit(solution)/shard_map/all_to_all | solution.py:342
  38.8 0.6 collective-permute-start.2
  39.4 0.1 collective-permute-start.3
  39.5 5.0 %collective-permute-done.2.refs_5_ = bf16[3456,256]{1,0:T(8,128)(2,1)S(1)} collective-permute-done((bf16[3456,256]{1,0:T(8,128)(2,1)S(1)}, bf16[3456,256]{1,0:T(8,128)(2,1)S(1)}, u32[]{:S(2)}, u32[]{:S(2)}) %collective-permute-start.2) | collective-permute-done | bytes 1769504 | tf_op jit(solution)/shard_map/ppermute | solution.py:336
  44.5 1.2 %copy-done.4 = bf16[3456,256]{1,0:T(8,128)(2,1)} copy-done((bf16[3456,256]{1,0:T(8,128)(2,1)}, bf16[3456,256]{1,0:T(8,128)(2,1)S(1)}, u32[]{:S(2)}) %copy-start.4) | copy-done | bytes 1769496
  45.7 11.2 %all-to-all-done.1 = bf16[8,640,128]{2,1,0:T(8,128)(2,1)S(1)} async-done(((bf16[8,640,128]{2,1,0:T(8,128)(2,1)}), bf16[8,640,128]{2,1,0:T(8,128)(2,1)S(1)}, u32[]{:S(2)}, u32[]{:S(2)}) %all-to-all-start.1) | async-done | bytes 1310752 | tf_op jit(solution)/shard_map/all_to_all | solution.py:342
  56.9 12.1 %shard_map.153 = (f32[1,128]{1,0:T(1,128)}, bf16[5120,128]{1,0:T(8,128)(2,1)}) custom-call(s32[26,128]{1,0:T(8,128)S(1)} %get-tuple-element.10.refs_0_, bf16[5120,128]{1,0:T(8,128)(2,1)S(1)} %bitcast.42, bf16[128,128]{1,0:T(8,128)(2,1)S(1)} %copy-done, s32[1,128]{1,0:T(1,128)S(1)} %bitcast.48, bf16[3456,256]{1,0:T(8,128)(2,1)} %bitcast.49, ...), custom_call_target="tpu_custom_call" | custom-call | tf_op jit(solution)/shard_map/pallas_call | solution.py:393
  69.0 4.9 %all-to-all-start.2 = ((bf16[8,640,128]{2,1,0:T(8,128)(2,1)}), bf16[8,640,128]{2,1,0:T(8,128)(2,1)S(1)}, u32[]{:S(2)}, u32[]{:S(2)}) async-start(bf16[8,640,128]{2,1,0:T(8,128)(2,1)} %bitcast.12), calls=%async_computation.2 | async-start | bytes 2621440 | tf_op jit(solution)/shard_map/all_to_all | solution.py:342
  73.9 0.1 reshape.59
  74.0 0.1 reshape.58
  74.1 17.3 %all-to-all-done.2 = bf16[8,640,128]{2,1,0:T(8,128)(2,1)S(1)} async-done(((bf16[8,640,128]{2,1,0:T(8,128)(2,1)}), bf16[8,640,128]{2,1,0:T(8,128)(2,1)S(1)}, u32[]{:S(2)}, u32[]{:S(2)}) %all-to-all-start.2) | async-done | bytes 1310752 | tf_op jit(solution)/shard_map/all_to_all | solution.py:342
  91.3 1.7 %shard_map.154.after_ref = f32[1024,128]{1,0:T(8,128)S(1)} custom-call(s32[8,2,8,128]{3,2,1,0:T(8,128)S(1)} %bitcast.46, s32[40,128]{1,0:T(8,128)S(1)} %pad_add_fusion.ids_ref, bf16[5120,128]{1,0:T(8,128)(2,1)S(1)} %bitcast.38), custom_call_target="tpu_custom_call" | custom-call | tf_op jit(solution)/shard_map/pallas_call | solution.py:429
  93.1 0.1 collective-permute-start.4
  93.2 0.1 reshape.63
  93.3 0.1 reshape.62
  93.3 1.7 %shard_map.155 = f32[1024,128]{1,0:T(8,128)S(1)} custom-call(f32[1024,128]{1,0:T(8,128)S(1)} %shard_map.154.after_ref, s32[40,128]{1,0:T(8,128)S(1)} %pad_add_fusion.ids_ref, bf16[5120,128]{1,0:T(8,128)(2,1)S(1)} %bitcast.39), custom_call_target="tpu_custom_call" | custom-call | tf_op jit(solution)/shard_map/pallas_call | solution.py:429
  95.1 0.1 add_convert_fusion.after_ref
  95.2 1.7 %shard_map.156.after_ref = f32[1024,128]{1,0:T(8,128)S(1)} custom-call(bf16[1024,128]{1,0:T(8,128)(2,1)S(1)} %add_convert_fusion.after_ref, s32[40,128]{1,0:T(8,128)S(1)} %pad_add_fusion.1.ids_ref, bf16[5120,128]{1,0:T(8,128)(2,1)S(1)} %bitcast.40), custom_call_target="tpu_custom_call" | custom-call | tf_op jit(solution)/shard_map/pallas_call | solution.py:429
  96.9 0.6 collective-permute-start.5
  97.5 0.6 collective-permute-start.6
  98.1 0.9 collective-permute-done.5.refs_0_
  99.0 1.7 %shard_map.157 = f32[1024,128]{1,0:T(8,128)S(1)} custom-call(f32[1024,128]{1,0:T(8,128)S(1)} %shard_map.156.after_ref, s32[40,128]{1,0:T(8,128)S(1)} %pad_add_fusion.1.ids_ref, bf16[5120,128]{1,0:T(8,128)(2,1)S(1)} %bitcast.41, f32[1024,128]{1,0:T(8,128)S(1)} %collective-permute-done.5.refs_0_), custom_call_target="tpu_custom_call" | custom-call | tf_op jit(solution)/shard_map/pallas_call | solution.py:429
  100.8 11.5 %collective-permute-done.6 = bf16[1024,128]{1,0:T(8,128)(2,1)S(1)} collective-permute-done((bf16[1024,128]{1,0:T(8,128)(2,1)S(1)}, bf16[1024,128]{1,0:T(8,128)(2,1)S(1)}, u32[]{:S(2)}, u32[]{:S(2)}) %collective-permute-start.6) | collective-permute-done | bytes 262176 | tf_op jit(solution)/shard_map/ppermute | solution.py:339
  112.3 0.8 convert_add_fusion
  (20 shorter events, 0.1 us)
Async XLA Ops:
  5.3 18.2 %collective-permute-start = (bf16[1024,128]{1,0:T(8,128)(2,1)S(1)}, bf16[1024,128]{1,0:T(8,128)(2,1)S(1)}, u32[]{:S(2)}, u32[]{:S(2)}) collective-permute-start(bf16[1024,128]{1,0:T(8,128)(2,1)S(1)} %get-tuple-element.12), channel_id=1, source_target_pairs={{0,16},{2,18},{4,20},{6,22},{8,24},{10,26},{12,28},{14,30},{16,0},... | collective-permute-start | bytes 786440 | tf_op jit(solution)/shard_map/ppermute | solution.py:339
  23.5 5.4 %collective-permute-start.1 = (bf16[1024,128]{1,0:T(8,128)(2,1)S(1)}, bf16[1024,128]{1,0:T(8,128)(2,1)S(1)}, u32[]{:S(2)}, u32[]{:S(2)}) collective-permute-start(bf16[1024,128]{1,0:T(8,128)(2,1)S(1)} %collective-permute-done.refs_1_), channel_id=1, source_target_pairs={{0,1},{1,0},{2,3},{3,2},{4,5},{5,4},{6,7},{7,6},{8,9},{9,8},{10,11... | collective-permute-start | bytes 786440 | tf_op jit(solution)/shard_map/ppermute | solution.py:336
  34.9 4.0 %copy-start.3 = (bf16[1,3456,256]{2,1,0:T(8,128)(2,1)S(1)}, bf16[1,3456,256]{2,1,0:T(8,128)(2,1)}, u32[]{:S(2)}) copy-start(bf16[1,3456,256]{2,1,0:T(8,128)(2,1)} %param.24) | copy-start | bytes 5308420
  34.9 4.6 %copy-start.5 = (f32[3456]{0:T(1024)S(1)}, f32[3456]{0:T(1024)}, u32[]{:S(2)}) copy-start(f32[3456]{0:T(1024)} %param.27) | copy-start | bytes 41476
  34.9 22.0 %copy-start = (bf16[128,128]{1,0:T(8,128)(2,1)S(1)}, bf16[128,128]{1,0:T(8,128)(2,1)}, u32[]{:S(2)}) copy-start(bf16[128,128]{1,0:T(8,128)(2,1)} %refs_2_.1) | copy-start | bytes 98308
  34.9 22.0 %copy-start.1 = (f32[1,3456]{1,0:T(1,128)S(1)}, f32[1,3456]{1,0:T(1,128)}, u32[]{:S(2)}) copy-start(f32[1,3456]{1,0:T(1,128)} %refs_8_.1) | copy-start | bytes 41476
  34.9 22.0 %copy-start.2 = (s32[128]{0:T(128)S(1)}, s32[128]{0:T(128)}, u32[]{:S(2)}) copy-start(s32[128]{0:T(128)} %param.23) | copy-start | bytes 1540
  34.9 22.0 %all-to-all-start.1 = ((bf16[8,640,128]{2,1,0:T(8,128)(2,1)}), bf16[8,640,128]{2,1,0:T(8,128)(2,1)S(1)}, u32[]{:S(2)}, u32[]{:S(2)}) async-start(bf16[8,640,128]{2,1,0:T(8,128)(2,1)} %bitcast.5), calls=%async_computation.1 | async-start | bytes 2621440 | tf_op jit(solution)/shard_map/all_to_all | solution.py:342
  38.8 5.6 %collective-permute-start.2 = (bf16[3456,256]{1,0:T(8,128)(2,1)S(1)}, bf16[3456,256]{1,0:T(8,128)(2,1)S(1)}, u32[]{:S(2)}, u32[]{:S(2)}) collective-permute-start(bf16[3456,256]{1,0:T(8,128)(2,1)S(1)} %bitcast.50), channel_id=1, source_target_pairs={{0,1},{1,0},{2,3},{3,2},{4,5},{5,4},{6,7},{7,6},{8,9},{9,8},{10,11... | collective-permute-start | bytes 5308424 | tf_op jit(solution)/shard_map/ppermute | solution.py:336
  39.4 6.3 %collective-permute-start.3 = (bf16[256,3456]{1,0:T(8,128)(2,1)}, bf16[256,3456]{1,0:T(8,128)(2,1)}, u32[]{:S(2)}, u32[]{:S(2)}) collective-permute-start(bf16[256,3456]{1,0:T(8,128)(2,1)} %bitcast.51), channel_id=1, source_target_pairs={{0,1},{1,0},{2,3},{3,2},{4,5},{5,4},{6,7},{7,6},{8,9},{9,8},{10,11... | collective-permute-start | bytes 5308424 | tf_op jit(solution)/shard_map/ppermute | solution.py:336
  44.5 1.2 %copy-start.4 = (bf16[3456,256]{1,0:T(8,128)(2,1)}, bf16[3456,256]{1,0:T(8,128)(2,1)S(1)}, u32[]{:S(2)}) copy-start(bf16[3456,256]{1,0:T(8,128)(2,1)S(1)} %collective-permute-done.2.refs_5_) | copy-start | bytes 5308420
  69.0 22.3 %all-to-all-start.2 = ((bf16[8,640,128]{2,1,0:T(8,128)(2,1)}), bf16[8,640,128]{2,1,0:T(8,128)(2,1)S(1)}, u32[]{:S(2)}, u32[]{:S(2)}) async-start(bf16[8,640,128]{2,1,0:T(8,128)(2,1)} %bitcast.12), calls=%async_computation.2 | async-start | bytes 2621440 | tf_op jit(solution)/shard_map/all_to_all | solution.py:342
  93.1 2.0 %collective-permute-start.4 = (f32[1024,128]{1,0:T(8,128)S(1)}, f32[1024,128]{1,0:T(8,128)S(1)}, u32[]{:S(2)}, u32[]{:S(2)}) collective-permute-start(f32[1024,128]{1,0:T(8,128)S(1)} %shard_map.154.after_ref), channel_id=1, source_target_pairs={{0,1},{1,0},{2,3},{3,2},{4,5},{5,4},{6,7},{7,6},{8,9},{9,8},{10,11... | collective-permute-start | bytes 1572872 | tf_op jit(solution)/shard_map/ppermute | solution.py:336
  96.9 2.1 %collective-permute-start.5 = (f32[1024,128]{1,0:T(8,128)S(1)}, f32[1024,128]{1,0:T(8,128)S(1)}, u32[]{:S(2)}, u32[]{:S(2)}) collective-permute-start(f32[1024,128]{1,0:T(8,128)S(1)} %shard_map.156.after_ref), channel_id=1, source_target_pairs={{0,1},{1,0},{2,3},{3,2},{4,5},{5,4},{6,7},{7,6},{8,9},{9,8},{10,11... | collective-permute-start | bytes 1572872 | tf_op jit(solution)/shard_map/ppermute | solution.py:336
  97.5 14.8 %collective-permute-start.6 = (bf16[1024,128]{1,0:T(8,128)(2,1)S(1)}, bf16[1024,128]{1,0:T(8,128)(2,1)S(1)}, u32[]{:S(2)}, u32[]{:S(2)}) collective-permute-start(bf16[1024,128]{1,0:T(8,128)(2,1)S(1)} %add_convert_fusion.after_ref), channel_id=1, source_target_pairs={{0,16},{2,18},{4,20},{6,22},{8,24},{10,26},{12,28},{14,30},{16,0},... | collective-permute-start | bytes 786440 | tf_op jit(solution)/shard_map/ppermute | solution.py:339

commit v3 on v2

v3 whole, which is shorter than its diff:
```python
import functools

import jax
import jax.numpy as jnp
from jax import lax
from jax.experimental import pallas as pl
from jax.experimental.pallas import tpu as pltpu
from jax.sharding import PartitionSpec as P

loss_scale = 64.0
LANES = 128
F32, BF16, I32, I16 = jnp.float32, jnp.bfloat16, jnp.int32, jnp.int16
VMEM = pl.BlockSpec(memory_space=pltpu.VMEM)
SMEM = pl.BlockSpec(memory_space=pltpu.SMEM)
ANY = pl.BlockSpec(memory_space=pl.ANY)
params = pltpu.CompilerParams(vmem_limit_bytes=36 * 1024 * 1024)
NT = (((1,), (1,)), ((), ()))


def dot(a, b, dims=(((1,), (0,)), ((), ()))):
    return lax.dot_general(a, b, dims, preferred_element_type=F32)


def iota(shape, axis):
    return lax.broadcasted_iota(I32, shape, axis)


def round_up(value, step):
    return -(-value // step) * step


def route_kernel(
    peers, cap, after_ref, owner_ref, rows_ref, len_ref, pos_ref, req_ref, own_s, one_s, two_s, a_s, b_s
):
    del after_ref
    feats, lanes = len_ref.shape
    padded = own_s.shape[0]
    chunks = -(-cap // LANES)
    half = peers // 2
    per = req_ref.shape[0] // peers
    count = peers * per
    own_s[...] = jnp.full(own_s.shape, -1, I32)
    for f in range(feats):
        own_s[f : f + 1, :] = owner_ref[f]
        one_s[f : f + 1, :] = rows_ref[f, 0:1, :]
        two_s[f : f + 1, :] = rows_ref[f, 1:2, :]
    own = own_s[...]
    hits = [(own == o).astype(F32) for o in range(peers)]
    stacked = jnp.concatenate(hits, axis=0).astype(BF16)
    row, col = iota((lanes, 2 * lanes), 0), iota((lanes, 2 * lanes), 1)
    upper = jnp.where((row < col) | (col >= lanes), 1.0, 0.0).astype(BF16)
    sums = dot(stacked, upper)
    totals = jnp.concatenate(
        [sums[o * padded : (o + 1) * padded, lanes:] for o in range(peers)], axis=1
    ).astype(BF16)
    lower = jnp.where(iota((padded, padded), 1) < iota((padded, padded), 0), 1.0, 0.0).astype(BF16)
    base = dot(lower, totals)
    rank = jnp.zeros((padded, lanes), F32)
    for o in range(peers):
        before = sums[o * padded : (o + 1) * padded, :lanes] + base[:, o * lanes : (o + 1) * lanes]
        rank = rank + hits[o] * before
    rank = rank.astype(I32)
    far = own >= half
    column = jnp.where(far, own - half, own)
    side = (lax.axis_index("table") >= half).astype(I32)
    mirrored = jnp.where(far, 1 - side, side)
    place = jnp.where(own < 0, -8, column * 2 + mirrored)
    pos_ref[...] = (place * cap + rank)[0:feats, :]
    first = place * per + lax.shift_right_logical(rank, 7)
    second = first + chunks
    low = rank & (LANES - 1)
    lengths = len_ref[...]
    one = jnp.where(lengths > 0, one_s[0:feats, :] + 1, 0)
    two = jnp.where(lengths > 1, two_s[0:feats, :] + 1, 0)
    at = iota((count, lanes), 0)
    lane_at = iota((LANES, lanes), 0)
    for f in range(feats):
        held = jnp.where(at == first[f : f + 1, :], one[f : f + 1, :], 0)
        held = jnp.where(at == second[f : f + 1, :], two[f : f + 1, :], held)
        span = slice(f * lanes, (f + 1) * lanes)
        a_s[0:count, span] = lax.shift_right_logical(held, 7).astype(F32).astype(BF16)
        a_s[count : 2 * count, span] = (held & 127).astype(F32).astype(BF16)
        b_s[:, span] = jnp.where(lane_at == low[f : f + 1, :], 1.0, 0.0).astype(BF16)
    found = dot(a_s[...], b_s[...], NT)
    req_ref[...] = (found[0:count] * 128.0 + found[count:]).astype(I32)


def update_kernel(
    local_ref, new_ref, versions_ref, table_ref, values_ref, table_out_ref, part_ref, rows_s
):
    held_rows, width = table_ref.shape
    rows_s[0:held_rows, :] = table_ref[...]

    def entry(i, carry):
        at = local_ref[i]
        to = jnp.where(new_ref[i] > versions_ref[at], at, held_rows)
        rows_s[pl.ds(to, 1), :] = values_ref[pl.ds(i, 1), :]
        return carry

    lax.fori_loop(0, values_ref.shape[0], entry, 0, unroll=8)
    table = rows_s[0:held_rows, :]
    high = table.astype(BF16)
    table_out_ref[:, 0:width] = high
    table_out_ref[:, width:] = (table - high.astype(F32)).astype(BF16)
    own_rows = part_ref.shape[0]
    start = pl.multiple_of(lax.axis_index("dp") * own_rows, own_rows)
    part_ref[...] = rows_s[pl.ds(start, own_rows), :].astype(BF16)


def lookup_kernel(peers, cap, partners, pieces, after_ref, ids_ref, table_ref, *refs):
    del after_ref
    mirror, outs, count_s = refs[:pieces], refs[pieces:-1], refs[-1]
    width = outs[0].shape[1]
    per = ids_ref.shape[0] // (2 * peers)
    chunks = -(-cap // LANES)
    one, zero = jnp.ones((), BF16), jnp.zeros((), BF16)
    at_dp = lax.axis_index("dp")
    at_table = lax.rem(lax.axis_index("table"), peers)
    own_rows = mirror[0].shape[0]
    bases = [lax.rem(at_dp + pieces - p, pieces) * own_rows for p in range(pieces)]
    spans = [[(0, table_ref.shape[0])], [(base, own_rows) for base in bases]]

    def count(kind):
        for g, partner in enumerate(partners):
            start = ((at_table ^ partner) * 2 + kind) * per
            block = ids_ref[pl.ds(pl.multiple_of(start, 8), per), :].T
            for c in range(chunks):
                n = min(LANES, cap - c * LANES)
                at = g * cap + c * LANES
                a = jnp.broadcast_to(block[0:n, c : c + 1], (n, LANES))
                b = jnp.broadcast_to(block[0:n, chunks + c : chunks + c + 1], (n, LANES))
                column = 0
                for base, rows in spans[kind]:
                    a16, b16 = (a - base).astype(I16), (b - base).astype(I16)
                    for k in range(0, rows, LANES):
                        size = min(LANES, rows - k)
                        row = (iota((n, size), 1) + (1 + k)).astype(I16)
                        count_s[kind, at : at + n, column : column + size] = jnp.where(
                            a16[:, :size] == row, one, zero
                        ) + jnp.where(b16[:, :size] == row, one, zero)
                        column += size

    def give(kind, found):
        for g, out in enumerate(outs):
            out[kind * cap : (kind + 1) * cap, :] = found[g * cap : (g + 1) * cap, :].astype(BF16)

    count(0)
    count(1)
    both = dot(count_s[0], table_ref[...])
    give(0, both[:, 0:width] + both[:, width:])
    found = dot(count_s[1, :, 0:own_rows], mirror[0][...])
    for p in range(1, pieces):
        found = found + dot(count_s[1, :, p * own_rows : (p + 1) * own_rows], mirror[p][...])
    give(1, found)


def dense_kernel(pieces, partners, cap, *refs):
    answers, refs = refs[:partners], refs[partners:]
    pos_ref, dense_ref, labels_ref = refs[0:3]
    bias_ref, head_ref, logit_ref = refs[3 + 2 * pieces : 6 + 2 * pieces]
    send_ref, rows_s, x_s, factor_s, bags_s, down_s, up_s, sems = refs[6 + 2 * pieces :]
    at_table = lax.rem(lax.axis_index("table"), partners)
    load_down = pltpu.make_async_copy(refs[3], down_s, sems.at[0])
    load_up = pltpu.make_async_copy(refs[3 + pieces], up_s, sems.at[1])
    load_down.start()
    load_up.start()
    down = (down_s,) + refs[4 : 3 + pieces]
    up = (up_s,) + refs[4 + pieces : 3 + 2 * pieces]
    feats, samples = pos_ref.shape
    width = dense_ref.shape[1]
    for p, answer in enumerate(answers):
        at = pl.multiple_of((at_table ^ p) * 2 * cap, 16)
        rows_s[pl.ds(at, 2 * cap), :] = answer[...].astype(F32)

    def fetch(f, carry):
        start = f * samples
        for b in range(samples):
            bags_s[pl.ds(start + b, 1), :] = rows_s[pl.ds(pos_ref[f, b], 1), :]
        return carry

    lax.fori_loop(0, feats, fetch, 0)
    x_s[:, 0:width] = dense_ref[...]
    for f in range(feats):
        x_s[:, (f + 1) * width : (f + 2) * width] = bags_s[
            f * samples : (f + 1) * samples, :
        ].astype(BF16)
    rows_s[...] = jnp.zeros(rows_s.shape, F32)
    load_down.wait()
    x = x_s[...]
    crossed = [dot(x, w[...]).astype(BF16) for w in down]
    load_up.wait()
    total = jnp.zeros((samples, width), F32)
    blocks = feats + 1
    for k in range(blocks):
        span = slice(k * width, (k + 1) * width)
        factor = bias_ref[:, span]
        for c, w in zip(crossed, up):
            factor = factor + dot(c, w[:, span])
        factor_s[:, span] = factor
        base = x_s[:, span].astype(F32)
        total = total + (base * factor + base) * head_ref[:, span]
    logits = jnp.sum(total, axis=1, keepdims=True)
    logit_ref[...] = jnp.broadcast_to(logits, (samples, samples)).T[0:1, :]
    labels = jnp.broadcast_to(labels_ref[...].astype(F32), (samples, samples)).T[:, 0:1]
    signal = loss_scale * (jax.nn.sigmoid(logits) - labels)
    lifts = []
    for k in range(blocks):
        span = slice(k * width, (k + 1) * width)
        lifts.append(((signal * head_ref[:, span]) * x_s[:, span].astype(F32)).astype(BF16))
    lift = jnp.concatenate(lifts, axis=1)
    back = [dot(lift, w[...], NT).astype(BF16) for w in up]
    for f in range(feats):
        span = slice((f + 1) * width, (f + 2) * width)
        outer = signal * head_ref[:, span]
        grad = outer
        for c, w in zip(back, down):
            grad = grad + dot(c, w[span, :], NT)
        bags_s[f * samples : (f + 1) * samples, :] = grad + outer * factor_s[:, span]

    def place(f, carry):
        start = f * samples
        for b in range(samples):
            rows_s[pl.ds(pos_ref[f, b], 1), :] = bags_s[pl.ds(start + b, 1), :]
        return carry

    lax.fori_loop(0, feats, place, 0)
    send_ref[...] = rows_s[...].astype(BF16)


def scatter_kernel(cap, kind, by, replicas, after_ref, *refs):
    del after_ref
    ids, grads, (out_ref, bags_s) = refs[:replicas], refs[replicas:-2], refs[-2:]
    rows = out_ref.shape[0]
    tile = min(rows, 512)
    each = ids[0].shape[0] // 2
    slots = each * LANES
    step = 4 if each % 4 == 0 else 1
    one, zero = jnp.ones((), BF16), jnp.zeros((), BF16)
    at = (iota((tile, LANES), 0) + 1).astype(I16)
    for r, grad in enumerate(grads):
        for source in range(slots // cap):
            start = (2 * source + kind) * cap
            to = r * slots + source * cap
            bags_s[to : to + cap, :] = grad[start : start + cap, :]
    first = lax.rem(lax.axis_index("dp") + by, lax.axis_size("dp")) * rows
    for start in range(0, rows, tile):
        base = first + start
        total = jnp.zeros((tile, LANES), F32)
        for r, lines in enumerate(ids):
            for k in range(0, each, step):
                counts = []
                for line in range(k, k + step):
                    a = lines[line : line + 1, :] - base
                    b = lines[each + line : each + line + 1, :] - base
                    a = jnp.broadcast_to(a, (tile, LANES)).astype(I16)
                    b = jnp.broadcast_to(b, (tile, LANES)).astype(I16)
                    counts.append(jnp.where(a == at, one, zero) + jnp.where(b == at, one, zero))
                here = r * slots + k * LANES
                total = total + dot(
                    jnp.concatenate(counts, axis=1), bags_s[here : here + step * LANES, :]
                )
        out_ref[start : start + tile, :] = total


def call(kernel, outs, ins, scratch=(), flops=0, moved=0):
    cost = pl.CostEstimate(flops=flops, bytes_accessed=moved, transcendentals=0)
    return pl.pallas_call(
        kernel,
        out_shape=outs,
        in_specs=ins,
        out_specs=jax.tree.map(lambda _: VMEM, outs),
        scratch_shapes=list(scratch),
        compiler_params=params,
        cost_estimate=cost,
    )


def in_hbm(x):
    return pltpu.with_memory_space_constraint(x, pltpu.HBM)


def in_vmem(x):
    return pltpu.with_memory_space_constraint(x, pltpu.VMEM)


def shape(dims, dtype):
    return jax.ShapeDtypeStruct(dims, dtype)


def body(
    emb_table,
    versions,
    conf_local,
    conf_version,
    conf_values,
    owners,
    row_local,
    lengths,
    dense_out,
    labels,
    cross_down,
    cross_up,
    cross_bias,
    head_weight,
):
    peers, replicas = lax.axis_size("table"), lax.axis_size("dp")
    half = peers // 2
    groups = [list(range(half)), list(range(half, peers))]
    rows_dev, width = emb_table.shape
    samples, feats, slots = row_local.shape
    cap = round_up(3 * samples * feats // (2 * peers), 16)
    chunks = -(-cap // LANES)
    per = round_up(slots * chunks, 8)
    lines_half = half * cap // LANES
    wide = cross_down.shape[1]
    own_rows = rows_dev // replicas

    def shift(x, by):
        if by == 0:
            return x
        return lax.ppermute(x, "dp", [(i, (i + by) % replicas) for i in range(replicas)])

    def across(x):
        return lax.ppermute(x, "table", [(i, (i + half) % peers) for i in range(peers)])

    def exchange(x):
        return lax.all_to_all(
            x, "table", split_axis=0, concat_axis=0, axis_index_groups=groups, tiled=True
        )

    down = [shift(cross_down[0], by) for by in range(replicas)]
    up = [shift(cross_up[0], by) for by in range(replicas)]

    table, part = call(
        update_kernel,
        (shape((rows_dev, 2 * width), BF16), shape((own_rows, width), BF16)),
        [SMEM] * 3 + [VMEM] * 2,
        [pltpu.VMEM((rows_dev + 8, width), F32)],
    )(*map(in_hbm, (conf_local, conf_version, versions, emb_table, conf_values)))
    position, requests = call(
        functools.partial(route_kernel, peers, cap),
        (shape((feats, samples), I32), shape((peers * per, LANES), I32)),
        [ANY] + [VMEM] * 3,
        [pltpu.VMEM((round_up(feats, 8), samples), I32)] * 3
        + [
            pltpu.VMEM((2 * peers * per, feats * samples), BF16),
            pltpu.VMEM((LANES, feats * samples), BF16),
        ],
    )(part, *map(in_hbm, (owners.transpose(1, 2, 0), row_local.transpose(1, 2, 0), lengths.T)))
    asked = exchange(requests.reshape(half, 2 * per, LANES)).reshape(2 * half * per, LANES)
    part = across(part)
    part, asked = lax.optimization_barrier((part, asked))
    mirror = [shift(part, by) for by in range(replicas)]

    def meet(x, partner):
        if partner == 0:
            return x
        return lax.ppermute(x, "table", [(i, i ^ partner) for i in range(peers)])

    steps = 4 if half % 8 == 0 else 1
    pairs = [(i, half - 1 - i) for i in range(half // 2, half)]
    group = len(pairs) // steps
    answers = [None] * half
    after = [asked, asked]
    for start in range(len(pairs) - group, -1, -group):
        partners = [p for pair in pairs[start : start + group] for p in pair]
        found = call(
            functools.partial(lookup_kernel, half, cap, partners, replicas),
            tuple(shape((2 * cap, width), BF16) for _ in partners),
            [ANY] + [VMEM] * (2 + replicas),
            [pltpu.VMEM((2, 2 * group * cap, rows_dev), BF16)],
        )(after[-2], asked, table, *mirror)
        for partner, sums in zip(partners, found):
            answers[partner] = meet(sums, partner)
        after.append(answers[partners[0]])

    logits, send = call(
        functools.partial(dense_kernel, replicas, half, cap),
        (shape((1, samples), F32), shape((peers * cap, width), BF16)),
        [VMEM] * half + [SMEM] + [VMEM] * 2 + ([ANY] + [VMEM] * (replicas - 1)) * 2 + [VMEM] * 2,
        [
            pltpu.VMEM((peers * cap, width), F32),
            pltpu.VMEM((samples, wide), BF16),
            pltpu.VMEM((samples, wide), F32),
            pltpu.VMEM((samples * feats, width), F32),
            pltpu.VMEM(down[0].shape, BF16),
            pltpu.VMEM(up[0].shape, BF16),
            pltpu.SemaphoreType.DMA((2,)),
        ],
    )(
        *map(in_vmem, answers),
        position,
        dense_out,
        labels.reshape(1, samples),
        in_hbm(down[0]),
        *map(in_vmem, down[1:]),
        in_hbm(up[0]),
        *map(in_vmem, up[1:]),
        cross_bias,
        head_weight.reshape(1, wide),
    )
    ids = asked.reshape(half, 2, per, LANES)
    got = in_vmem(exchange(send.reshape(half, 2 * cap, width)).reshape(peers * cap, width))

    def lines_of(kind):
        return jnp.concatenate(
            [
                ids[:, kind, slot * chunks : (slot + 1) * chunks]
                .reshape(half, chunks * LANES)[:, :cap]
                .reshape(lines_half, LANES)
                for slot in range(slots)
            ]
        )

    def scatter(kind, by, after, lines, grads):
        return call(
            functools.partial(scatter_kernel, cap, kind, by, len(lines)),
            shape((own_rows, width), F32),
            [ANY] + [VMEM] * (2 * len(lines)),
            [pltpu.VMEM((len(lines) * half * cap, width), BF16)],
        )(after, *lines, *grads)

    mirror_lines, native_lines = lines_of(1), lines_of(0)
    last, parts = asked, []
    for by in range(1, replicas):
        last = scatter(1, by, last, [mirror_lines], [got])
        parts.append(shift(last, by))
    own = scatter(1, 0, last, [mirror_lines], [got])
    mirrored = functools.reduce(jnp.add, [own] + parts).astype(BF16)
    returned = across(mirrored)
    every_line = [shift(native_lines, by) for by in range(replicas)]
    every_got = [in_vmem(shift(got, by)) for by in range(replicas)]
    grads = scatter(0, 0, mirrored, every_line, every_got) + returned.astype(F32)
    return (logits.reshape(samples), grads)


def solution(mesh):
    in_specs = (
        P("table", None),
        P("table"),
        P("table"),
        P("table"),
        P("table", None),
        P(("table", "dp"), None, None),
        P(("table", "dp"), None, None),
        P(("table", "dp"), None),
        P(("table", "dp"), None),
        P(("table", "dp")),
        P(None, None, "dp"),
        P(None, "dp", None),
        P(),
        P(),
    )
    out_specs = (P(("table", "dp")), P(("table", "dp"), None))
    return jax.shard_map(body, mesh=mesh, in_specs=in_specs, out_specs=out_specs, check_vma=False)
```

time: 113 us -> 104 us (0.920)
  waiting for transfers between devices: 45.9 us -> 35 us
  starting transfers between devices: 14.8 us -> 21.5 us
  Pallas kernels: 35 us -> 32.5 us
  blocking collectives: 14.1 us -> 12.3 us
  local copies, waits for them, and re-layouts: 1.59 us -> 0.34 us
    all_to_all x2 -> x1, waiting for transfers between devices: 28.5 us -> 16.9 us  [exchange(): lax.all_to_all(x, 'table', split_axis=0, concat_axis=0, axis_index_groups...]
    ppermute x0 -> x7, starting transfers between devices: none -> 9.35 us  [meet(): return lax.ppermute(x, 'table', [(i, i ^ partner) for i in range(peers)])]
    ppermute x0 -> x7, waiting for transfers between devices: none -> 7.35 us  [meet(): return lax.ppermute(x, 'table', [(i, i ^ partner) for i in range(peers)])]
    all_to_all x2 -> x1, starting transfers between devices: 8.77 us -> 3.81 us  [exchange(): lax.all_to_all(x, 'table', split_axis=0, concat_axis=0, axis_index_groups...]
    ppermute x2, waiting for transfers between devices: 11.5 us -> 8.1 us  [across(): lax.ppermute(x, 'table', [(i, (i + half) % peers) for i in range(peers)])]
    ppermute x5 -> x6, waiting for transfers between devices: 5.87 us -> 2.67 us  [shift(): lax.ppermute(x, 'dp', [(i, (i + by) % replicas) for i in range(replicas)])]
    pallas_call x7 -> x8, Pallas kernels: 30.4 us -> 27.8 us  [the longest x1 12.4 us: body(): call(functools.partial(dense_kernel, replicas, half, cap), (shape((1, sam...]
    ppermute x2, starting transfers between devices: 4.74 us -> 7.02 us  [across(): lax.ppermute(x, 'table', [(i, (i + half) % peers) for i in range(peers)])]
  transfers between devices with their start and end apart: 9 -> 16, of which waited for: 5 -> 9; matrix products, arithmetic and copies ran while one was open for 0% -> 0% of each run, Pallas kernels for 8% -> 19%
where the time goes in v3:
time: 104 us; the launch traced here: 103 us
  waiting for transfers between devices  35 us (34%)
  Pallas kernels  32.5 us (31%)
  starting transfers between devices  21.5 us (21%)
  blocking collectives  12.3 us (12%)
    all_to_all x1, waiting for transfers between devices, exchange(): lax.all_to_all(x, 'table', split_axis=0, concat_axis=0, axis_index_groups...  16.9 us
    pallas_call x1, Pallas kernels, body(): call(functools.partial(dense_kernel, replicas, half, cap), (shape((1, sam...  12.4 us
    all_to_all x1, blocking collectives, exchange(): lax.all_to_all(x, 'table', split_axis=0, concat_axis=0, axis_index_groups...  12.3 us
    pallas_call x4, Pallas kernels, body(): call(functools.partial(lookup_kernel, half, cap, partners, replicas), tup...  9.51 us
    ppermute x7, starting transfers between devices, meet(): return lax.ppermute(x, 'table', [(i, i ^ partner) for i in range(peers)])  9.35 us
    ppermute x2, waiting for transfers between devices, across(): lax.ppermute(x, 'table', [(i, (i + half) % peers) for i in range(peers)])  8.1 us
    ppermute x7, waiting for transfers between devices, meet(): return lax.ppermute(x, 'table', [(i, i ^ partner) for i in range(peers)])  7.35 us
    ppermute x2, starting transfers between devices, across(): lax.ppermute(x, 'table', [(i, (i + half) % peers) for i in range(peers)])  7.02 us
  transfers between devices with their start and end apart: 16, of which 9 were waited for; matrix products, arithmetic and copies ran while one was open for 0% of the time, Pallas kernels for 19%

profile of v3, /device:TPU:0, one launch (start us, length us, event | category | flops | bytes accessed | tf_op | source)
XLA Modules:
  0.0 103.3 jit_solution(7015171540474207600)
XLA Ops:
  0.6 0.5 collective-permute-start.10
  1.2 2.2 %shard_map.149 = (bf16[2048,256]{1,0:T(8,128)(2,1)S(1)}, bf16[1024,128]{1,0:T(8,128)(2,1)S(1)}) custom-call(s32[256]{0:T(256)} %local_ref.1, s32[256]{0:T(256)} %new_ref.1, s32[2048]{0:T(1024)} %versions_ref.1, f32[2048,128]{1,0:T(8,128)} %table_ref.1, f32[256,128]{1,0:T(8,128)} %values_ref.1), custom_call_target="tpu_custom_call" | custom-call | tf_op jit(solution)/shard_map/pallas_call | solution.py:334
  3.4 4.1 %collective-permute-start = (bf16[1024,128]{1,0:T(8,128)(2,1)S(1)}, bf16[1024,128]{1,0:T(8,128)(2,1)S(1)}, u32[]{:S(2)}, u32[]{:S(2)}) collective-permute-start(bf16[1024,128]{1,0:T(8,128)(2,1)S(1)} %get-tuple-element.18.after_ref), channel_id=1, source_target_pairs={{0,16},{2,18},{4,20},{6,22},{8,24},{10,26},{12,28},{14,30},{16,0},... | collective-permute-start | bytes 786440 | tf_op jit(solution)/shard_map/ppermute | solution.py:324
  7.5 2.4 %shard_map.150 = (s32[26,128]{1,0:T(8,128)S(1)}, s32[128,128]{1,0:T(8,128)S(1)}) custom-call(bf16[1024,128]{1,0:T(8,128)(2,1)S(1)} %get-tuple-element.18.after_ref, s32[26,1,128]{2,1,0:T(1,128)} %bitcast.48, s32[26,2,128]{2,1,0:T(2,128)} %bitcast.46, s32[26,128]{1,0:T(8,128)} %bitcast.47), custom_call_target="tpu_custom_call" | custom-call | tf_op jit(solution)/shard_map/pallas_call | solution.py:340
  10.0 12.3 %all_to_all.10 = s32[8,16,128]{2,1,0:T(8,128)S(1)} all-to-all(s32[8,16,128]{2,1,0:T(8,128)S(1)} %bitcast.36), channel_id=1, replica_groups={{0,2,4,6,8,10,12,14},{16,18,20,22,24,26,28,30},{1,3,5,7,9,11,13,15},{17..., dimensions={0} | all-to-all | bytes 131072 | tf_op jit(solution)/shard_map/all_to_all | solution.py:327
  22.2 1.5 %collective-permute-done.1.refs_1_ = bf16[1024,128]{1,0:T(8,128)(2,1)S(1)} collective-permute-done((bf16[1024,128]{1,0:T(8,128)(2,1)S(1)}, bf16[1024,128]{1,0:T(8,128)(2,1)S(1)}, u32[]{:S(2)}, u32[]{:S(2)}) %collective-permute-start.1) | collective-permute-done | bytes 262176 | tf_op jit(solution)/shard_map/ppermute | solution.py:321
  23.8 2.4 %shard_map.152 = (bf16[640,128]{1,0:T(8,128)(2,1)S(1)}, bf16[640,128]{1,0:T(8,128)(2,1)S(1)}) custom-call(s32[128,128]{1,0:T(8,128)S(1)} %bitcast.28, s32[128,128]{1,0:T(8,128)S(1)} %bitcast.29, bf16[2048,256]{1,0:T(8,128)(2,1)S(1)} %get-tuple-element.21.table_ref, bf16[1024,128]{1,0:T(8,128)(2,1)S(1)} %collective-permute-done.refs_0_, ...), custom_call_target="tpu_custom_call" | custom-call | tf_op jit(solution)/shard_map/pallas_call | solution.py:367
  26.2 2.4 %shard_map.151 = (bf16[640,128]{1,0:T(8,128)(2,1)S(1)}, bf16[640,128]{1,0:T(8,128)(2,1)S(1)}) custom-call(s32[128,128]{1,0:T(8,128)S(1)} %bitcast.30, s32[128,128]{1,0:T(8,128)S(1)} %bitcast.31, bf16[2048,256]{1,0:T(8,128)(2,1)S(1)} %get-tuple-element.21.table_ref, bf16[1024,128]{1,0:T(8,128)(2,1)S(1)} %collective-permute-done.refs_0_, ...), custom_call_target="tpu_custom_call" | custom-call | tf_op jit(solution)/shard_map/pallas_call | solution.py:367
  28.6 2.8 %collective-permute-start.3 = (bf16[640,128]{1,0:T(8,128)(2,1)S(1)}, bf16[640,128]{1,0:T(8,128)(2,1)S(1)}, u32[]{:S(2)}, u32[]{:S(2)}) collective-permute-start(bf16[640,128]{1,0:T(8,128)(2,1)S(1)} %get-tuple-element.25), channel_id=1, source_target_pairs={{0,14},{2,12},{4,10},{6,8},{8,6},{10,4},{12,2},{14,0},{16,30},{18,... | collective-permute-start | bytes 491528 | tf_op jit(solution)/shard_map/ppermute | solution.py:358
  31.4 1.7 %collective-permute-start.2 = (bf16[640,128]{1,0:T(8,128)(2,1)S(1)}, bf16[640,128]{1,0:T(8,128)(2,1)S(1)}, u32[]{:S(2)}, u32[]{:S(2)}) collective-permute-start(bf16[640,128]{1,0:T(8,128)(2,1)S(1)} %get-tuple-element.24), channel_id=1, source_target_pairs={{0,2},{2,0},{4,6},{6,4},{8,10},{10,8},{12,14},{14,12},{16,18},{18,... | collective-permute-start | bytes 491528 | tf_op jit(solution)/shard_map/ppermute | solution.py:358
  33.1 1.5 %collective-permute-done.5.after_ref.refs_6_ = bf16[640,128]{1,0:T(8,128)(2,1)S(1)} collective-permute-done((bf16[640,128]{1,0:T(8,128)(2,1)S(1)}, bf16[640,128]{1,0:T(8,128)(2,1)S(1)}, u32[]{:S(2)}, u32[]{:S(2)}) %collective-permute-start.5) | collective-permute-done | bytes 163872 | tf_op jit(solution)/shard_map/ppermute | solution.py:358
  34.6 2.4 %shard_map.154 = (bf16[640,128]{1,0:T(8,128)(2,1)S(1)}, bf16[640,128]{1,0:T(8,128)(2,1)S(1)}) custom-call(bf16[640,128]{1,0:T(8,128)(2,1)S(1)} %collective-permute-done.5.after_ref.refs_6_, s32[128,128]{1,0:T(8,128)S(1)} %bitcast.32, bf16[2048,256]{1,0:T(8,128)(2,1)S(1)} %get-tuple-element.21.table_ref, bf16[1024,128]{1,0:T(8,128)(2,1)S(1)} %collective-permute-done.refs_0_, ...), custom_call_target="tpu_custom_call" | custom-call | tf_op jit(solution)/shard_map/pallas_call | solution.py:367
  37.1 0.1 collective-permute-done.3.after_ref.refs_7_
  37.2 1.3 %collective-permute-start.7 = (bf16[640,128]{1,0:T(8,128)(2,1)S(1)}, bf16[640,128]{1,0:T(8,128)(2,1)S(1)}, u32[]{:S(2)}, u32[]{:S(2)}) collective-permute-start(bf16[640,128]{1,0:T(8,128)(2,1)S(1)} %get-tuple-element.29), channel_id=1, source_target_pairs={{0,8},{2,10},{4,12},{6,14},{8,0},{10,2},{12,4},{14,6},{16,24},{18,... | collective-permute-start | bytes 491528 | tf_op jit(solution)/shard_map/ppermute | solution.py:358
  38.5 2.4 %shard_map.153 = (bf16[640,128]{1,0:T(8,128)(2,1)S(1)}, bf16[640,128]{1,0:T(8,128)(2,1)S(1)}) custom-call(bf16[640,128]{1,0:T(8,128)(2,1)S(1)} %collective-permute-done.3.after_ref.refs_7_, s32[128,128]{1,0:T(8,128)S(1)} %bitcast.33, bf16[2048,256]{1,0:T(8,128)(2,1)S(1)} %get-tuple-element.21.table_ref, bf16[1024,128]{1,0:T(8,128)(2,1)S(1)} %collective-permute-done.refs_0_, ...), custom_call_target="tpu_custom_call" | custom-call | tf_op jit(solution)/shard_map/pallas_call | solution.py:367
  40.9 1.6 %collective-permute-start.4 = (bf16[640,128]{1,0:T(8,128)(2,1)S(1)}, bf16[640,128]{1,0:T(8,128)(2,1)S(1)}, u32[]{:S(2)}, u32[]{:S(2)}) collective-permute-start(bf16[640,128]{1,0:T(8,128)(2,1)S(1)} %get-tuple-element.26), channel_id=1, source_target_pairs={{0,4},{2,6},{4,0},{6,2},{8,12},{10,14},{12,8},{14,10},{16,20},{18,... | collective-permute-start | bytes 491528 | tf_op jit(solution)/shard_map/ppermute | solution.py:358
  42.5 1.4 %collective-permute-done.6.refs_3_ = bf16[640,128]{1,0:T(8,128)(2,1)S(1)} collective-permute-done((bf16[640,128]{1,0:T(8,128)(2,1)S(1)}, bf16[640,128]{1,0:T(8,128)(2,1)S(1)}, u32[]{:S(2)}, u32[]{:S(2)}) %collective-permute-start.6) | collective-permute-done | bytes 163872 | tf_op jit(solution)/shard_map/ppermute | solution.py:358
  43.8 1.8 %collective-permute-start.8 = (bf16[640,128]{1,0:T(8,128)(2,1)S(1)}, bf16[640,128]{1,0:T(8,128)(2,1)S(1)}, u32[]{:S(2)}, u32[]{:S(2)}) collective-permute-start(bf16[640,128]{1,0:T(8,128)(2,1)S(1)} %get-tuple-element.30), channel_id=1, source_target_pairs={{0,10},{2,8},{4,14},{6,12},{8,2},{10,0},{12,6},{14,4},{16,26},{18,... | collective-permute-start | bytes 491528 | tf_op jit(solution)/shard_map/ppermute | solution.py:358
  45.7 1.6 %collective-permute-done.4.refs_2_ = bf16[640,128]{1,0:T(8,128)(2,1)S(1)} collective-permute-done((bf16[640,128]{1,0:T(8,128)(2,1)S(1)}, bf16[640,128]{1,0:T(8,128)(2,1)S(1)}, u32[]{:S(2)}, u32[]{:S(2)}) %collective-permute-start.4) | collective-permute-done | bytes 163872 | tf_op jit(solution)/shard_map/ppermute | solution.py:358
  47.2 2.8 %collective-permute-done.8.refs_5_ = bf16[640,128]{1,0:T(8,128)(2,1)S(1)} collective-permute-done((bf16[640,128]{1,0:T(8,128)(2,1)S(1)}, bf16[640,128]{1,0:T(8,128)(2,1)S(1)}, u32[]{:S(2)}, u32[]{:S(2)}) %collective-permute-start.8) | collective-permute-done | bytes 163872 | tf_op jit(solution)/shard_map/ppermute | solution.py:358
  50.1 12.4 %shard_map.155 = (f32[1,128]{1,0:T(1,128)}, bf16[5120,128]{1,0:T(8,128)(2,1)}) custom-call(bf16[640,128]{1,0:T(8,128)(2,1)S(1)} %get-tuple-element.23.refs_0_, bf16[640,128]{1,0:T(8,128)(2,1)S(1)} %collective-permute-done.2.refs_1_, bf16[640,128]{1,0:T(8,128)(2,1)S(1)} %collective-permute-done.4.refs_2_, ...), custom_call_target="tpu_custom_call" | custom-call | tf_op jit(solution)/shard_map/pallas_call | solution.py:377
  62.5 3.8 %all-to-all-start.1 = ((bf16[8,640,128]{2,1,0:T(8,128)(2,1)}), bf16[8,640,128]{2,1,0:T(8,128)(2,1)S(1)}, u32[]{:S(2)}, u32[]{:S(2)}) async-start(bf16[8,640,128]{2,1,0:T(8,128)(2,1)} %bitcast.12), calls=%async_computation.1 | async-start | bytes 2621440 | tf_op jit(solution)/shard_map/all_to_all | solution.py:327
  66.3 16.9 %all-to-all-done.1 = bf16[8,640,128]{2,1,0:T(8,128)(2,1)S(1)} async-done(((bf16[8,640,128]{2,1,0:T(8,128)(2,1)}), bf16[8,640,128]{2,1,0:T(8,128)(2,1)S(1)}, u32[]{:S(2)}, u32[]{:S(2)}) %all-to-all-start.1) | async-done | bytes 1310752 | tf_op jit(solution)/shard_map/all_to_all | solution.py:327
  83.3 1.5 %shard_map.156.after_ref = f32[1024,128]{1,0:T(8,128)S(1)} custom-call(s32[128,128]{1,0:T(8,128)S(1)} %bitcast.35, s32[40,128]{1,0:T(8,128)S(1)} %pad_add_fusion.refs_0_, bf16[5120,128]{1,0:T(8,128)(2,1)S(1)} %bitcast.25), custom_call_target="tpu_custom_call" | custom-call | tf_op jit(solution)/shard_map/pallas_call | solution.py:416
  84.9 0.6 collective-permute-start.11
  85.4 1.5 %shard_map.157 = f32[1024,128]{1,0:T(8,128)S(1)} custom-call(f32[1024,128]{1,0:T(8,128)S(1)} %shard_map.156.after_ref, s32[40,128]{1,0:T(8,128)S(1)} %pad_add_fusion.refs_0_, bf16[5120,128]{1,0:T(8,128)(2,1)S(1)} %bitcast.26), custom_call_target="tpu_custom_call" | custom-call | tf_op jit(solution)/shard_map/pallas_call | solution.py:416
  87.1 2.9 %collective-permute-start.14 = (bf16[1024,128]{1,0:T(8,128)(2,1)S(1)}, bf16[1024,128]{1,0:T(8,128)(2,1)S(1)}, u32[]{:S(2)}, u32[]{:S(2)}) collective-permute-start(bf16[1024,128]{1,0:T(8,128)(2,1)S(1)} %add_convert_fusion.after_ref), channel_id=1, source_target_pairs={{0,16},{2,18},{4,20},{6,22},{8,24},{10,26},{12,28},{14,30},{16,0},... | collective-permute-start | bytes 786440 | tf_op jit(solution)/shard_map/ppermute | solution.py:324
  90.2 0.1 collective-permute-start.12
  90.3 1.1 %collective-permute-done.12.refs_1_ = s32[40,128]{1,0:T(8,128)S(1)} collective-permute-done((s32[40,128]{1,0:T(8,128)S(1)}, s32[40,128]{1,0:T(8,128)S(1)}, u32[]{:S(2)}, u32[]{:S(2)}) %collective-permute-start.12) | collective-permute-done | bytes 20512 | tf_op jit(solution)/shard_map/ppermute | solution.py:321
  91.4 2.9 %shard_map.158 = f32[1024,128]{1,0:T(8,128)S(1)} custom-call(bf16[1024,128]{1,0:T(8,128)(2,1)S(1)} %add_convert_fusion.after_ref, s32[40,128]{1,0:T(8,128)S(1)} %pad_add_fusion.1.refs_0_, s32[40,128]{1,0:T(8,128)S(1)} %collective-permute-done.12.refs_1_, bf16[5120,128]{1,0:T(8,128)(2,1)S(1)} %bitcast.27, bf16[5120,128]{1,0:T(8,128)(2,1)S(1)} %collective-permute-done.13.refs_3_), custom_call_target="tpu_custom_call" | custom-call | tf_op jit(solution)/shard_map/pallas_call | solution.py:416
  94.4 8.1 %collective-permute-done.14 = bf16[1024,128]{1,0:T(8,128)(2,1)S(1)} collective-permute-done((bf16[1024,128]{1,0:T(8,128)(2,1)S(1)}, bf16[1024,128]{1,0:T(8,128)(2,1)S(1)}, u32[]{:S(2)}, u32[]{:S(2)}) %collective-permute-start.14) | collective-permute-done | bytes 262176 | tf_op jit(solution)/shard_map/ppermute | solution.py:324
  102.5 0.8 convert_add_fusion
  (31 shorter events, 0.7 us)
Async XLA Ops:
  0.6 49.4 %collective-permute-start.10 = (bf16[256,3456]{1,0:T(8,128)(2,1)}, bf16[256,3456]{1,0:T(8,128)(2,1)S(1)}, u32[]{:S(2)}, u32[]{:S(2)}) collective-permute-start(bf16[256,3456]{1,0:T(8,128)(2,1)} %bitcast.40), channel_id=1, source_target_pairs={{0,1},{1,0},{2,3},{3,2},{4,5},{5,4},{6,7},{7,6},{8,9},{9,8},{10,11... | collective-permute-start | bytes 5308424 | tf_op jit(solution)/shard_map/ppermute | solution.py:321
  1.1 48.9 %collective-permute-start.9 = (bf16[3456,256]{1,0:T(8,128)(2,1)}, bf16[3456,256]{1,0:T(8,128)(2,1)S(1)}, u32[]{:S(2)}, u32[]{:S(2)}) collective-permute-start(bf16[3456,256]{1,0:T(8,128)(2,1)} %bitcast.38), channel_id=1, source_target_pairs={{0,1},{1,0},{2,3},{3,2},{4,5},{5,4},{6,7},{7,6},{8,9},{9,8},{10,11... | collective-permute-start | bytes 5308424 | tf_op jit(solution)/shard_map/ppermute | solution.py:321
  3.4 18.8 %collective-permute-start = (bf16[1024,128]{1,0:T(8,128)(2,1)S(1)}, bf16[1024,128]{1,0:T(8,128)(2,1)S(1)}, u32[]{:S(2)}, u32[]{:S(2)}) collective-permute-start(bf16[1024,128]{1,0:T(8,128)(2,1)S(1)} %get-tuple-element.18.after_ref), channel_id=1, source_target_pairs={{0,16},{2,18},{4,20},{6,22},{8,24},{10,26},{12,28},{14,30},{16,0},... | collective-permute-start | bytes 786440 | tf_op jit(solution)/shard_map/ppermute | solution.py:324
  22.2 1.5 %collective-permute-start.1 = (bf16[1024,128]{1,0:T(8,128)(2,1)S(1)}, bf16[1024,128]{1,0:T(8,128)(2,1)S(1)}, u32[]{:S(2)}, u32[]{:S(2)}) collective-permute-start(bf16[1024,128]{1,0:T(8,128)(2,1)S(1)} %collective-permute-done.refs_0_), channel_id=1, source_target_pairs={{0,1},{1,0},{2,3},{3,2},{4,5},{5,4},{6,7},{7,6},{8,9},{9,8},{10,11... | collective-permute-start | bytes 786440 | tf_op jit(solution)/shard_map/ppermute | solution.py:321
  26.1 8.5 %collective-permute-start.5 = (bf16[640,128]{1,0:T(8,128)(2,1)S(1)}, bf16[640,128]{1,0:T(8,128)(2,1)S(1)}, u32[]{:S(2)}, u32[]{:S(2)}) collective-permute-start(bf16[640,128]{1,0:T(8,128)(2,1)S(1)} %get-tuple-element.27), channel_id=1, source_target_pairs={{0,12},{2,14},{4,8},{6,10},{8,4},{10,6},{12,0},{14,2},{16,28},{18,... | collective-permute-start | bytes 491528 | tf_op jit(solution)/shard_map/ppermute | solution.py:358
  28.6 8.6 %collective-permute-start.3 = (bf16[640,128]{1,0:T(8,128)(2,1)S(1)}, bf16[640,128]{1,0:T(8,128)(2,1)S(1)}, u32[]{:S(2)}, u32[]{:S(2)}) collective-permute-start(bf16[640,128]{1,0:T(8,128)(2,1)S(1)} %get-tuple-element.25), channel_id=1, source_target_pairs={{0,14},{2,12},{4,10},{6,8},{8,6},{10,4},{12,2},{14,0},{16,30},{18,... | collective-permute-start | bytes 491528 | tf_op jit(solution)/shard_map/ppermute | solution.py:358
  31.4 14.2 %copy-start.3 = (f32[3456]{0:T(1024)S(1)}, f32[3456]{0:T(1024)}, u32[]{:S(2)}) copy-start(f32[3456]{0:T(1024)} %param.27) | copy-start | bytes 41476
  31.4 18.6 %copy-start = (bf16[128,128]{1,0:T(8,128)(2,1)S(1)}, bf16[128,128]{1,0:T(8,128)(2,1)}, u32[]{:S(2)}) copy-start(bf16[128,128]{1,0:T(8,128)(2,1)} %refs_9_.1) | copy-start | bytes 98308
  31.4 18.7 %copy-start.1 = (f32[1,3456]{1,0:T(1,128)S(1)}, f32[1,3456]{1,0:T(1,128)}, u32[]{:S(2)}) copy-start(f32[1,3456]{1,0:T(1,128)} %refs_15_.1) | copy-start | bytes 41476
  31.4 18.7 %copy-start.2 = (s32[128]{0:T(128)S(1)}, s32[128]{0:T(128)}, u32[]{:S(2)}) copy-start(s32[128]{0:T(128)} %param.23) | copy-start | bytes 1540
  31.4 9.5 %collective-permute-start.2 = (bf16[640,128]{1,0:T(8,128)(2,1)S(1)}, bf16[640,128]{1,0:T(8,128)(2,1)S(1)}, u32[]{:S(2)}, u32[]{:S(2)}) collective-permute-start(bf16[640,128]{1,0:T(8,128)(2,1)S(1)} %get-tuple-element.24), channel_id=1, source_target_pairs={{0,2},{2,0},{4,6},{6,4},{8,10},{10,8},{12,14},{14,12},{16,18},{18,... | collective-permute-start | bytes 491528 | tf_op jit(solution)/shard_map/ppermute | solution.py:358
  37.0 6.8 %collective-permute-start.6 = (bf16[640,128]{1,0:T(8,128)(2,1)S(1)}, bf16[640,128]{1,0:T(8,128)(2,1)S(1)}, u32[]{:S(2)}, u32[]{:S(2)}) collective-permute-start(bf16[640,128]{1,0:T(8,128)(2,1)S(1)} %get-tuple-element.28), channel_id=1, source_target_pairs={{0,6},{2,4},{4,2},{6,0},{8,14},{10,12},{12,10},{14,8},{16,22},{18,... | collective-permute-start | bytes 491528 | tf_op jit(solution)/shard_map/ppermute | solution.py:358
  37.2 8.5 %collective-permute-start.7 = (bf16[640,128]{1,0:T(8,128)(2,1)S(1)}, bf16[640,128]{1,0:T(8,128)(2,1)S(1)}, u32[]{:S(2)}, u32[]{:S(2)}) collective-permute-start(bf16[640,128]{1,0:T(8,128)(2,1)S(1)} %get-tuple-element.29), channel_id=1, source_target_pairs={{0,8},{2,10},{4,12},{6,14},{8,0},{10,2},{12,4},{14,6},{16,24},{18,... | collective-permute-start | bytes 491528 | tf_op jit(solution)/shard_map/ppermute | solution.py:358
  40.9 6.4 %collective-permute-start.4 = (bf16[640,128]{1,0:T(8,128)(2,1)S(1)}, bf16[640,128]{1,0:T(8,128)(2,1)S(1)}, u32[]{:S(2)}, u32[]{:S(2)}) collective-permute-start(bf16[640,128]{1,0:T(8,128)(2,1)S(1)} %get-tuple-element.26), channel_id=1, source_target_pairs={{0,4},{2,6},{4,0},{6,2},{8,12},{10,14},{12,8},{14,10},{16,20},{18,... | collective-permute-start | bytes 491528 | tf_op jit(solution)/shard_map/ppermute | solution.py:358
  43.8 6.2 %collective-permute-start.8 = (bf16[640,128]{1,0:T(8,128)(2,1)S(1)}, bf16[640,128]{1,0:T(8,128)(2,1)S(1)}, u32[]{:S(2)}, u32[]{:S(2)}) collective-permute-start(bf16[640,128]{1,0:T(8,128)(2,1)S(1)} %get-tuple-element.30), channel_id=1, source_target_pairs={{0,10},{2,8},{4,14},{6,12},{8,2},{10,0},{12,6},{14,4},{16,26},{18,... | collective-permute-start | bytes 491528 | tf_op jit(solution)/shard_map/ppermute | solution.py:358
  62.5 20.7 %all-to-all-start.1 = ((bf16[8,640,128]{2,1,0:T(8,128)(2,1)}), bf16[8,640,128]{2,1,0:T(8,128)(2,1)S(1)}, u32[]{:S(2)}, u32[]{:S(2)}) async-start(bf16[8,640,128]{2,1,0:T(8,128)(2,1)} %bitcast.12), calls=%async_computation.1 | async-start | bytes 2621440 | tf_op jit(solution)/shard_map/all_to_all | solution.py:327
  83.2 8.3 %collective-permute-start.13 = (bf16[5120,128]{1,0:T(8,128)(2,1)S(1)}, bf16[5120,128]{1,0:T(8,128)(2,1)S(1)}, u32[]{:S(2)}, u32[]{:S(2)}) collective-permute-start(bf16[5120,128]{1,0:T(8,128)(2,1)S(1)} %bitcast.24), channel_id=1, source_target_pairs={{0,1},{1,0},{2,3},{3,2},{4,5},{5,4},{6,7},{7,6},{8,9},{9,8},{10,11... | collective-permute-start | bytes 3932168 | tf_op jit(solution)/shard_map/ppermute | solution.py:321
  84.9 2.1 %collective-permute-start.11 = (f32[1024,128]{1,0:T(8,128)S(1)}, f32[1024,128]{1,0:T(8,128)S(1)}, u32[]{:S(2)}, u32[]{:S(2)}) collective-permute-start(f32[1024,128]{1,0:T(8,128)S(1)} %shard_map.156.after_ref), channel_id=1, source_target_pairs={{0,1},{1,0},{2,3},{3,2},{4,5},{5,4},{6,7},{7,6},{8,9},{9,8},{10,11... | collective-permute-start | bytes 1572872 | tf_op jit(solution)/shard_map/ppermute | solution.py:321
  87.1 15.4 %collective-permute-start.14 = (bf16[1024,128]{1,0:T(8,128)(2,1)S(1)}, bf16[1024,128]{1,0:T(8,128)(2,1)S(1)}, u32[]{:S(2)}, u32[]{:S(2)}) collective-permute-start(bf16[1024,128]{1,0:T(8,128)(2,1)S(1)} %add_convert_fusion.after_ref), channel_id=1, source_target_pairs={{0,16},{2,18},{4,20},{6,22},{8,24},{10,26},{12,28},{14,30},{16,0},... | collective-permute-start | bytes 786440 | tf_op jit(solution)/shard_map/ppermute | solution.py:324
  90.2 1.3 %collective-permute-start.12 = (s32[40,128]{1,0:T(8,128)S(1)}, s32[40,128]{1,0:T(8,128)S(1)}, u32[]{:S(2)}, u32[]{:S(2)}) collective-permute-start(s32[40,128]{1,0:T(8,128)S(1)} %pad_add_fusion.1.refs_0_), channel_id=1, source_target_pairs={{0,1},{1,0},{2,3},{3,2},{4,5},{5,4},{6,7},{7,6},{8,9},{9,8},{10,11... | collective-permute-start | bytes 61448 | tf_op jit(solution)/shard_map/ppermute | solution.py:321

commit v4 on v3

--- a/solution.py
+++ b/solution.py
@@ -65,7 +65,7 @@
     side = (lax.axis_index("table") >= half).astype(I32)
     mirrored = jnp.where(far, 1 - side, side)
     place = jnp.where(own < 0, -8, column * 2 + mirrored)
-    pos_ref[...] = (place * cap + rank)[0:feats, :]
+    pos_ref[...] = ((mirrored * half + column) * cap + rank)[0:feats, :]
     first = place * per + lax.shift_right_logical(rank, 7)
     second = first + chunks
     low = rank & (LANES - 1)
@@ -158,7 +158,9 @@
     answers, refs = refs[:partners], refs[partners:]
     pos_ref, dense_ref, labels_ref = refs[0:3]
     bias_ref, head_ref, logit_ref = refs[3 + 2 * pieces : 6 + 2 * pieces]
-    send_ref, rows_s, x_s, factor_s, bags_s, down_s, up_s, sems = refs[6 + 2 * pieces :]
+    native_ref, mirror_ref, rows_s, x_s, factor_s, bags_s, down_s, up_s, sems = refs[
+        6 + 2 * pieces :
+    ]
     at_table = lax.rem(lax.axis_index("table"), partners)
     load_down = pltpu.make_async_copy(refs[3], down_s, sems.at[0])
     load_up = pltpu.make_async_copy(refs[3 + pieces], up_s, sems.at[1])
@@ -169,8 +171,9 @@
     feats, samples = pos_ref.shape
     width = dense_ref.shape[1]
     for p, answer in enumerate(answers):
-        at = pl.multiple_of((at_table ^ p) * 2 * cap, 16)
-        rows_s[pl.ds(at, 2 * cap), :] = answer[...].astype(F32)
+        for kind in range(2):
+            at = pl.multiple_of((kind * partners + (at_table ^ p)) * cap, 16)
+            rows_s[pl.ds(at, cap), :] = answer[kind * cap : (kind + 1) * cap, :].astype(F32)
 
     def fetch(f, carry):
         start = f * samples
@@ -184,7 +187,6 @@
         x_s[:, (f + 1) * width : (f + 2) * width] = bags_s[
             f * samples : (f + 1) * samples, :
         ].astype(BF16)
-    rows_s[...] = jnp.zeros(rows_s.shape, F32)
     load_down.wait()
     x = x_s[...]
     crossed = [dot(x, w[...]).astype(BF16) for w in down]
@@ -224,10 +226,11 @@
         return carry
 
     lax.fori_loop(0, feats, place, 0)
-    send_ref[...] = rows_s[...].astype(BF16)
-
-
-def scatter_kernel(cap, kind, by, replicas, after_ref, *refs):
+    native_ref[...] = rows_s[0 : partners * cap, :].astype(BF16)
+    mirror_ref[...] = rows_s[partners * cap :, :].astype(BF16)
+
+
+def scatter_kernel(by, replicas, after_ref, *refs):
     del after_ref
     ids, grads, (out_ref, bags_s) = refs[:replicas], refs[replicas:-2], refs[-2:]
     rows = out_ref.shape[0]
@@ -237,11 +240,10 @@
     step = 4 if each % 4 == 0 else 1
     one, zero = jnp.ones((), BF16), jnp.zeros((), BF16)
     at = (iota((tile, LANES), 0) + 1).astype(I16)
-    for r, grad in enumerate(grads):
-        for source in range(slots // cap):
-            start = (2 * source + kind) * cap
-            to = r * slots + source * cap
-            bags_s[to : to + cap, :] = grad[start : start + cap, :]
+    start = 0
+    for grad in grads:
+        bags_s[start : start + grad.shape[0], :] = grad[...]
+        start += grad.shape[0]
     first = lax.rem(lax.axis_index("dp") + by, lax.axis_size("dp")) * rows
     for start in range(0, rows, tile):
         base = first + start
@@ -262,7 +264,7 @@
         out_ref[start : start + tile, :] = total
 
 
-def call(kernel, outs, ins, scratch=(), flops=0, moved=0):
+def call(kernel, outs, ins, scratch=(), flops=1024, moved=1024):
     cost = pl.CostEstimate(flops=flops, bytes_accessed=moved, transcendentals=0)
     return pl.pallas_call(
         kernel,
@@ -328,8 +330,6 @@
             x, "table", split_axis=0, concat_axis=0, axis_index_groups=groups, tiled=True
         )
 
-    down = [shift(cross_down[0], by) for by in range(replicas)]
-    up = [shift(cross_up[0], by) for by in range(replicas)]
 
     table, part = call(
         update_kernel,
@@ -347,10 +347,13 @@
             pltpu.VMEM((LANES, feats * samples), BF16),
         ],
     )(part, *map(in_hbm, (owners.transpose(1, 2, 0), row_local.transpose(1, 2, 0), lengths.T)))
+    down = [shift(cross_down[0], by) for by in range(replicas)]
+    up = [shift(cross_up[0], by) for by in range(replicas)]
     asked = exchange(requests.reshape(half, 2 * per, LANES)).reshape(2 * half * per, LANES)
     part = across(part)
     part, asked = lax.optimization_barrier((part, asked))
     mirror = [shift(part, by) for by in range(replicas)]
+    asked, down, up = lax.optimization_barrier((asked, down, up))
 
     def meet(x, partner):
         if partner == 0:
@@ -374,9 +377,9 @@
             answers[partner] = meet(sums, partner)
         after.append(answers[partners[0]])
 
-    logits, send = call(
+    logits, to_native, to_mirror = call(
         functools.partial(dense_kernel, replicas, half, cap),
-        (shape((1, samples), F32), shape((peers * cap, width), BF16)),
+        (shape((1, samples), F32),) + (shape((half * cap, width), BF16),) * 2,
         [VMEM] * half + [SMEM] + [VMEM] * 2 + ([ANY] + [VMEM] * (replicas - 1)) * 2 + [VMEM] * 2,
         [
             pltpu.VMEM((peers * cap, width), F32),
@@ -400,7 +403,11 @@
         head_weight.reshape(1, wide),
     )
     ids = asked.reshape(half, 2, per, LANES)
-    got = in_vmem(exchange(send.reshape(half, 2 * cap, width)).reshape(peers * cap, width))
+    got_mirror = exchange(to_mirror.reshape(half, cap, width)).reshape(half * cap, width)
+    got_mirror, to_native = lax.optimization_barrier((got_mirror, to_native))
+    got_native = exchange(to_native.reshape(half, cap, width)).reshape(half * cap, width)
+    whole_native = got_native
+    got_mirror, got_native = in_vmem(got_mirror), in_vmem(got_native)
 
     def lines_of(kind):
         return jnp.concatenate(
@@ -412,25 +419,30 @@
             ]
         )
 
-    def scatter(kind, by, after, lines, grads):
+    def scatter(by, after, lines, grads):
         return call(
-            functools.partial(scatter_kernel, cap, kind, by, len(lines)),
+            functools.partial(scatter_kernel, by, len(lines)),
             shape((own_rows, width), F32),
-            [ANY] + [VMEM] * (2 * len(lines)),
+            [ANY] + [VMEM] * (len(lines) + len(grads)),
             [pltpu.VMEM((len(lines) * half * cap, width), BF16)],
         )(after, *lines, *grads)
 
     mirror_lines, native_lines = lines_of(1), lines_of(0)
     last, parts = asked, []
     for by in range(1, replicas):
-        last = scatter(1, by, last, [mirror_lines], [got])
+        last = scatter(by, last, [mirror_lines], [got_mirror])
         parts.append(shift(last, by))
-    own = scatter(1, 0, last, [mirror_lines], [got])
+    own = scatter(0, last, [mirror_lines], [got_mirror])
     mirrored = functools.reduce(jnp.add, [own] + parts).astype(BF16)
     returned = across(mirrored)
     every_line = [shift(native_lines, by) for by in range(replicas)]
-    every_got = [in_vmem(shift(got, by)) for by in range(replicas)]
-    grads = scatter(0, 0, mirrored, every_line, every_got) + returned.astype(F32)
+    pieces = 4 if half * cap % 64 == 0 else 1
+    size = half * cap // pieces
+    every_got = [got_native]
+    for by in range(1, replicas):
+        for i in range(pieces):
+            every_got.append(in_vmem(shift(whole_native[i * size : (i + 1) * size], by)))
+    grads = scatter(0, mirrored, every_line, every_got) + returned.astype(F32)
     return (logits.reshape(samples), grads)
 
 

time: 104 us -> 98 us (0.942)
  waiting for transfers between devices: 35 us -> 17.4 us
  blocking collectives: 12.3 us -> 23.9 us
    all_to_all x1, waiting for transfers between devices: 16.9 us -> 1.37 us  [exchange(): lax.all_to_all(x, 'table', split_axis=0, concat_axis=0, axis_index_groups...]
    all_to_all x1 -> x2, blocking collectives: 12.3 us -> 23.9 us  [exchange(): lax.all_to_all(x, 'table', split_axis=0, concat_axis=0, axis_index_groups...]
    ppermute x2, waiting for transfers between devices: 8.1 us -> 5.65 us  [across(): lax.ppermute(x, 'table', [(i, (i + half) % peers) for i in range(peers)])]
    ppermute x6 -> x9, starting transfers between devices: 1.31 us -> 2.31 us  [shift(): lax.ppermute(x, 'dp', [(i, (i + by) % replicas) for i in range(replicas)])]
    ppermute x6 -> x9, waiting for transfers between devices: 2.67 us -> 2.64 us  [shift(): lax.ppermute(x, 'dp', [(i, (i + by) % replicas) for i in range(replicas)])]
  transfers between devices with their start and end apart: 16 -> 19, of which waited for: 9 -> 10; matrix products, arithmetic and copies ran while one was open for 0% -> 0% of each run, Pallas kernels for 19% -> 18%
where the time goes in v4:
time: 98 us; the launch traced here: 97.6 us
  Pallas kernels  32 us (33%)
  blocking collectives  23.9 us (24%)
  starting transfers between devices  22.2 us (23%)
  waiting for transfers between devices  17.4 us (18%)
    all_to_all x2, blocking collectives, exchange(): lax.all_to_all(x, 'table', split_axis=0, concat_axis=0, axis_index_groups...  23.9 us
    pallas_call x1, Pallas kernels, body(): call(functools.partial(dense_kernel, replicas, half, cap), (shape((1, sam...  11.9 us
    ppermute x7, starting transfers between devices, meet(): return lax.ppermute(x, 'table', [(i, i ^ partner) for i in range(peers)])  9.66 us
    pallas_call x4, Pallas kernels, body(): call(functools.partial(lookup_kernel, half, cap, partners, replicas), tup...  9.5 us
    ppermute x7, waiting for transfers between devices, meet(): return lax.ppermute(x, 'table', [(i, i ^ partner) for i in range(peers)])  7.72 us
    ppermute x2, starting transfers between devices, across(): lax.ppermute(x, 'table', [(i, (i + half) % peers) for i in range(peers)])  6.7 us
    pallas_call x3, Pallas kernels, scatter(): call(functools.partial(scatter_kernel, by, len(lines)), shape((own_rows,...  5.97 us
    ppermute x2, waiting for transfers between devices, across(): lax.ppermute(x, 'table', [(i, (i + half) % peers) for i in range(peers)])  5.65 us
  transfers between devices with their start and end apart: 19, of which 10 were waited for; matrix products, arithmetic and copies ran while one was open for 0% of the time, Pallas kernels for 18%

profile of v4, /device:TPU:0, one launch (start us, length us, event | category | flops | bytes accessed | tf_op | source)
XLA Modules:
  0.0 97.6 jit_solution(10851338572496961107)
XLA Ops:
  0.6 0.5 collective-permute-start.1
  1.2 2.2 %shard_map.149 = (bf16[2048,256]{1,0:T(8,128)(2,1)S(1)}, bf16[1024,128]{1,0:T(8,128)(2,1)S(1)}) custom-call(s32[256]{0:T(256)} %local_ref.1, s32[256]{0:T(256)} %new_ref.1, s32[2048]{0:T(1024)} %versions_ref.1, f32[2048,128]{1,0:T(8,128)} %table_ref.1, f32[256,128]{1,0:T(8,128)} %values_ref.1), custom_call_target="tpu_custom_call" | custom-call | flops 1024 | bytes 1024 | tf_op jit(solution)/shard_map/pallas_call | solution.py:334
  3.4 4.1 %collective-permute-start = (bf16[1024,128]{1,0:T(8,128)(2,1)S(1)}, bf16[1024,128]{1,0:T(8,128)(2,1)S(1)}, u32[]{:S(2)}, u32[]{:S(2)}) collective-permute-start(bf16[1024,128]{1,0:T(8,128)(2,1)S(1)} %get-tuple-element.26.after_ref), channel_id=1, source_target_pairs={{0,16},{2,18},{4,20},{6,22},{8,24},{10,26},{12,28},{14,30},{16,0},... | collective-permute-start | bytes 786440 | tf_op jit(solution)/shard_map/ppermute | solution.py:326
  7.5 2.4 %shard_map.150 = (s32[26,128]{1,0:T(8,128)S(1)}, s32[128,128]{1,0:T(8,128)S(1)}) custom-call(bf16[1024,128]{1,0:T(8,128)(2,1)S(1)} %get-tuple-element.26.after_ref, s32[26,1,128]{2,1,0:T(1,128)} %bitcast.58, s32[26,2,128]{2,1,0:T(2,128)} %bitcast.56, s32[26,128]{1,0:T(8,128)} %bitcast.57), custom_call_target="tpu_custom_call" | custom-call | flops 1024 | bytes 1024 | tf_op jit(solution)/shard_map/pallas_call | solution.py:340
  10.0 12.3 %all_to_all.15 = s32[8,16,128]{2,1,0:T(8,128)S(1)} all-to-all(s32[8,16,128]{2,1,0:T(8,128)S(1)} %bitcast.42), channel_id=1, replica_groups={{0,2,4,6,8,10,12,14},{16,18,20,22,24,26,28,30},{1,3,5,7,9,11,13,15},{17..., dimensions={0} | all-to-all | bytes 131072 | tf_op jit(solution)/shard_map/all_to_all | solution.py:329
  22.2 1.5 %collective-permute-done.3.refs_1_ = bf16[1024,128]{1,0:T(8,128)(2,1)S(1)} collective-permute-done((bf16[1024,128]{1,0:T(8,128)(2,1)S(1)}, bf16[1024,128]{1,0:T(8,128)(2,1)S(1)}, u32[]{:S(2)}, u32[]{:S(2)}) %collective-permute-start.3) | collective-permute-done | bytes 262176 | tf_op jit(solution)/shard_map/ppermute | solution.py:323
  23.8 2.4 %shard_map.151 = (bf16[640,128]{1,0:T(8,128)(2,1)S(1)}, bf16[640,128]{1,0:T(8,128)(2,1)S(1)}) custom-call(s32[128,128]{1,0:T(8,128)S(1)} %bitcast.33, s32[128,128]{1,0:T(8,128)S(1)} %bitcast.34, bf16[2048,256]{1,0:T(8,128)(2,1)S(1)} %get-tuple-element.30.table_ref, bf16[1024,128]{1,0:T(8,128)(2,1)S(1)} %collective-permute-done.refs_0_, ...), custom_call_target="tpu_custom_call" | custom-call | flops 1024 | bytes 1024 | tf_op jit(solution)/shard_map/pallas_call | solution.py:370
  26.3 2.4 %shard_map.152 = (bf16[640,128]{1,0:T(8,128)(2,1)S(1)}, bf16[640,128]{1,0:T(8,128)(2,1)S(1)}) custom-call(s32[128,128]{1,0:T(8,128)S(1)} %bitcast.35, s32[128,128]{1,0:T(8,128)S(1)} %bitcast.36, bf16[2048,256]{1,0:T(8,128)(2,1)S(1)} %get-tuple-element.30.table_ref, bf16[1024,128]{1,0:T(8,128)(2,1)S(1)} %collective-permute-done.refs_0_, ...), custom_call_target="tpu_custom_call" | custom-call | flops 1024 | bytes 1024 | tf_op jit(solution)/shard_map/pallas_call | solution.py:370
  28.7 2.7 %collective-permute-start.7 = (bf16[640,128]{1,0:T(8,128)(2,1)S(1)}, bf16[640,128]{1,0:T(8,128)(2,1)S(1)}, u32[]{:S(2)}, u32[]{:S(2)}) collective-permute-start(bf16[640,128]{1,0:T(8,128)(2,1)S(1)} %get-tuple-element.36), channel_id=1, source_target_pairs={{0,12},{2,14},{4,8},{6,10},{8,4},{10,6},{12,0},{14,2},{16,28},{18,... | collective-permute-start | bytes 491528 | tf_op jit(solution)/shard_map/ppermute | solution.py:361
  31.4 1.7 %collective-permute-start.4 = (bf16[640,128]{1,0:T(8,128)(2,1)S(1)}, bf16[640,128]{1,0:T(8,128)(2,1)S(1)}, u32[]{:S(2)}, u32[]{:S(2)}) collective-permute-start(bf16[640,128]{1,0:T(8,128)(2,1)S(1)} %get-tuple-element.33), channel_id=1, source_target_pairs={{0,2},{2,0},{4,6},{6,4},{8,10},{10,8},{12,14},{14,12},{16,18},{18,... | collective-permute-start | bytes 491528 | tf_op jit(solution)/shard_map/ppermute | solution.py:361
  33.1 2.7 %collective-permute-done.5.after_ref.refs_7_ = bf16[640,128]{1,0:T(8,128)(2,1)S(1)} collective-permute-done((bf16[640,128]{1,0:T(8,128)(2,1)S(1)}, bf16[640,128]{1,0:T(8,128)(2,1)S(1)}, u32[]{:S(2)}, u32[]{:S(2)}) %collective-permute-start.5) | collective-permute-done | bytes 163872 | tf_op jit(solution)/shard_map/ppermute | solution.py:361
  35.8 2.4 %shard_map.153 = (bf16[640,128]{1,0:T(8,128)(2,1)S(1)}, bf16[640,128]{1,0:T(8,128)(2,1)S(1)}) custom-call(bf16[640,128]{1,0:T(8,128)(2,1)S(1)} %collective-permute-done.5.after_ref.refs_7_, s32[128,128]{1,0:T(8,128)S(1)} %bitcast.37, bf16[2048,256]{1,0:T(8,128)(2,1)S(1)} %get-tuple-element.30.table_ref, bf16[1024,128]{1,0:T(8,128)(2,1)S(1)} %collective-permute-done.refs_0_, ...), custom_call_target="tpu_custom_call" | custom-call | flops 1024 | bytes 1024 | tf_op jit(solution)/shard_map/pallas_call | solution.py:370
  38.2 0.5 collective-permute-start.6
  38.7 2.4 %shard_map.154 = (bf16[640,128]{1,0:T(8,128)(2,1)S(1)}, bf16[640,128]{1,0:T(8,128)(2,1)S(1)}) custom-call(bf16[640,128]{1,0:T(8,128)(2,1)S(1)} %collective-permute-done.7.after_ref.refs_6_, s32[128,128]{1,0:T(8,128)S(1)} %bitcast.38, bf16[2048,256]{1,0:T(8,128)(2,1)S(1)} %get-tuple-element.30.table_ref, bf16[1024,128]{1,0:T(8,128)(2,1)S(1)} %collective-permute-done.refs_0_, ...), custom_call_target="tpu_custom_call" | custom-call | flops 1024 | bytes 1024 | tf_op jit(solution)/shard_map/pallas_call | solution.py:370
  41.1 0.7 collective-permute-start.8
  41.8 0.6 collective-permute-start.9
  42.4 3.3 %collective-permute-start.10 = (bf16[640,128]{1,0:T(8,128)(2,1)S(1)}, bf16[640,128]{1,0:T(8,128)(2,1)S(1)}, u32[]{:S(2)}, u32[]{:S(2)}) collective-permute-start(bf16[640,128]{1,0:T(8,128)(2,1)S(1)} %get-tuple-element.39), channel_id=1, source_target_pairs={{0,10},{2,8},{4,14},{6,12},{8,2},{10,0},{12,6},{14,4},{16,26},{18,... | collective-permute-start | bytes 491528 | tf_op jit(solution)/shard_map/ppermute | solution.py:361
  45.7 3.4 %collective-permute-done.8.refs_3_ = bf16[640,128]{1,0:T(8,128)(2,1)S(1)} collective-permute-done((bf16[640,128]{1,0:T(8,128)(2,1)S(1)}, bf16[640,128]{1,0:T(8,128)(2,1)S(1)}, u32[]{:S(2)}, u32[]{:S(2)}) %collective-permute-start.8) | collective-permute-done | bytes 163872 | tf_op jit(solution)/shard_map/ppermute | solution.py:361
  49.1 1.6 %collective-permute-done.10.refs_5_ = bf16[640,128]{1,0:T(8,128)(2,1)S(1)} collective-permute-done((bf16[640,128]{1,0:T(8,128)(2,1)S(1)}, bf16[640,128]{1,0:T(8,128)(2,1)S(1)}, u32[]{:S(2)}, u32[]{:S(2)}) %collective-permute-start.10) | collective-permute-done | bytes 163872 | tf_op jit(solution)/shard_map/ppermute | solution.py:361
  50.7 11.9 %shard_map.155 = (f32[1,128]{1,0:T(1,128)}, bf16[2560,128]{1,0:T(8,128)(2,1)}, bf16[2560,128]{1,0:T(8,128)(2,1)S(1)}) custom-call(bf16[640,128]{1,0:T(8,128)(2,1)S(1)} %get-tuple-element.32.refs_0_, bf16[640,128]{1,0:T(8,128)(2,1)S(1)} %collective-permute-done.4.refs_1_, bf16[640,128]{1,0:T(8,128)(2,1)S(1)} %collective-permute-done.6.refs_2_, ...), custom_call_target="tpu_custom_call" | custom-call | flops 1024 | bytes 1024 | tf_op jit(solution)/shard_map/pallas_call | solution.py:380
  62.6 11.6 %all_to_all.16 = bf16[8,320,128]{2,1,0:T(8,128)(2,1)S(1)} all-to-all(bf16[8,320,128]{2,1,0:T(8,128)(2,1)S(1)} %bitcast.41), channel_id=1, replica_groups={{0,2,4,6,8,10,12,14},{16,18,20,22,24,26,28,30},{1,3,5,7,9,11,13,15},{17..., dimensions={0} | all-to-all | bytes 1310720 | tf_op jit(solution)/shard_map/all_to_all | solution.py:329
  74.2 3.5 %all-to-all-start.2 = ((bf16[8,320,128]{2,1,0:T(8,128)(2,1)}), bf16[8,320,128]{2,1,0:T(8,128)(2,1)S(1)}, u32[]{:S(2)}, u32[]{:S(2)}) async-start(bf16[8,320,128]{2,1,0:T(8,128)(2,1)} %bitcast.16), calls=%async_computation.2 | async-start | bytes 1310720 | tf_op jit(solution)/shard_map/all_to_all | solution.py:329
  78.0 1.5 %shard_map.156.after_ref = f32[1024,128]{1,0:T(8,128)S(1)} custom-call(s32[128,128]{1,0:T(8,128)S(1)} %bitcast.40, s32[40,128]{1,0:T(8,128)S(1)} %pad_add_fusion.refs_0_, bf16[2560,128]{1,0:T(8,128)(2,1)S(1)} %bitcast.31), custom_call_target="tpu_custom_call" | custom-call | flops 1024 | bytes 1024 | tf_op jit(solution)/shard_map/pallas_call | solution.py:423
  79.8 0.6 collective-permute-start.12
  80.3 1.5 %shard_map.157 = f32[1024,128]{1,0:T(8,128)S(1)} custom-call(f32[1024,128]{1,0:T(8,128)S(1)} %shard_map.156.after_ref, s32[40,128]{1,0:T(8,128)S(1)} %pad_add_fusion.refs_0_, bf16[2560,128]{1,0:T(8,128)(2,1)S(1)} %bitcast.32), custom_call_target="tpu_custom_call" | custom-call | flops 1024 | bytes 1024 | tf_op jit(solution)/shard_map/pallas_call | solution.py:423
  81.9 2.6 %collective-permute-start.17 = (bf16[1024,128]{1,0:T(8,128)(2,1)S(1)}, bf16[1024,128]{1,0:T(8,128)(2,1)S(1)}, u32[]{:S(2)}, u32[]{:S(2)}) collective-permute-start(bf16[1024,128]{1,0:T(8,128)(2,1)S(1)} %add_convert_fusion.after_ref), channel_id=1, source_target_pairs={{0,16},{2,18},{4,20},{6,22},{8,24},{10,26},{12,28},{14,30},{16,0},... | collective-permute-start | bytes 786440 | tf_op jit(solution)/shard_map/ppermute | solution.py:326
  84.6 1.4 %all-to-all-done.2 = bf16[8,320,128]{2,1,0:T(8,128)(2,1)S(1)} async-done(((bf16[8,320,128]{2,1,0:T(8,128)(2,1)}), bf16[8,320,128]{2,1,0:T(8,128)(2,1)S(1)}, u32[]{:S(2)}, u32[]{:S(2)}) %all-to-all-start.2) | async-done | bytes 655392 | tf_op jit(solution)/shard_map/all_to_all | solution.py:329
  86.1 0.5 collective-permute-start.14
  86.6 0.4 collective-permute-start.16
  88.2 2.9 %shard_map.158 = f32[1024,128]{1,0:T(8,128)S(1)} custom-call(bf16[1024,128]{1,0:T(8,128)(2,1)S(1)} %add_convert_fusion.after_ref, s32[40,128]{1,0:T(8,128)S(1)} %pad_add_fusion.1.refs_0_, s32[40,128]{1,0:T(8,128)S(1)} %collective-permute-done.12.refs_1_, bf16[2560,128]{1,0:T(8,128)(2,1)S(1)} %bitcast.30, ...), custom_call_target="tpu_custom_call" | custom-call | flops 1024 | bytes 1024 | tf_op jit(solution)/shard_map/pallas_call | solution.py:423
  91.1 5.7 %collective-permute-done.17 = bf16[1024,128]{1,0:T(8,128)(2,1)S(1)} collective-permute-done((bf16[1024,128]{1,0:T(8,128)(2,1)S(1)}, bf16[1024,128]{1,0:T(8,128)(2,1)S(1)}, u32[]{:S(2)}, u32[]{:S(2)}) %collective-permute-start.17) | collective-permute-done | bytes 262176 | tf_op jit(solution)/shard_map/ppermute | solution.py:326
  96.7 0.9 convert_add_fusion
  (39 shorter events, 2.1 us)
Async XLA Ops:
  0.6 21.6 %collective-permute-start.1 = (bf16[3456,256]{1,0:T(8,128)(2,1)}, bf16[3456,256]{1,0:T(8,128)(2,1)S(1)}, u32[]{:S(2)}, u32[]{:S(2)}) collective-permute-start(bf16[3456,256]{1,0:T(8,128)(2,1)} %bitcast.44), channel_id=1, source_target_pairs={{0,1},{1,0},{2,3},{3,2},{4,5},{5,4},{6,7},{7,6},{8,9},{9,8},{10,11... | collective-permute-start | bytes 5308424 | tf_op jit(solution)/shard_map/ppermute | solution.py:323
  1.1 21.1 %collective-permute-start.2 = (bf16[256,3456]{1,0:T(8,128)(2,1)}, bf16[256,3456]{1,0:T(8,128)(2,1)S(1)}, u32[]{:S(2)}, u32[]{:S(2)}) collective-permute-start(bf16[256,3456]{1,0:T(8,128)(2,1)} %bitcast.46), channel_id=1, source_target_pairs={{0,1},{1,0},{2,3},{3,2},{4,5},{5,4},{6,7},{7,6},{8,9},{9,8},{10,11... | collective-permute-start | bytes 5308424 | tf_op jit(solution)/shard_map/ppermute | solution.py:323
  3.4 18.8 %collective-permute-start = (bf16[1024,128]{1,0:T(8,128)(2,1)S(1)}, bf16[1024,128]{1,0:T(8,128)(2,1)S(1)}, u32[]{:S(2)}, u32[]{:S(2)}) collective-permute-start(bf16[1024,128]{1,0:T(8,128)(2,1)S(1)} %get-tuple-element.26.after_ref), channel_id=1, source_target_pairs={{0,16},{2,18},{4,20},{6,22},{8,24},{10,26},{12,28},{14,30},{16,0},... | collective-permute-start | bytes 786440 | tf_op jit(solution)/shard_map/ppermute | solution.py:326
  22.2 1.5 %collective-permute-start.3 = (bf16[1024,128]{1,0:T(8,128)(2,1)S(1)}, bf16[1024,128]{1,0:T(8,128)(2,1)S(1)}, u32[]{:S(2)}, u32[]{:S(2)}) collective-permute-start(bf16[1024,128]{1,0:T(8,128)(2,1)S(1)} %collective-permute-done.refs_0_), channel_id=1, source_target_pairs={{0,1},{1,0},{2,3},{3,2},{4,5},{5,4},{6,7},{7,6},{8,9},{9,8},{10,11... | collective-permute-start | bytes 786440 | tf_op jit(solution)/shard_map/ppermute | solution.py:323
  26.1 9.7 %collective-permute-start.5 = (bf16[640,128]{1,0:T(8,128)(2,1)S(1)}, bf16[640,128]{1,0:T(8,128)(2,1)S(1)}, u32[]{:S(2)}, u32[]{:S(2)}) collective-permute-start(bf16[640,128]{1,0:T(8,128)(2,1)S(1)} %get-tuple-element.34), channel_id=1, source_target_pairs={{0,14},{2,12},{4,10},{6,8},{8,6},{10,4},{12,2},{14,0},{16,30},{18,... | collective-permute-start | bytes 491528 | tf_op jit(solution)/shard_map/ppermute | solution.py:361
  28.7 10.0 %collective-permute-start.7 = (bf16[640,128]{1,0:T(8,128)(2,1)S(1)}, bf16[640,128]{1,0:T(8,128)(2,1)S(1)}, u32[]{:S(2)}, u32[]{:S(2)}) collective-permute-start(bf16[640,128]{1,0:T(8,128)(2,1)S(1)} %get-tuple-element.36), channel_id=1, source_target_pairs={{0,12},{2,14},{4,8},{6,10},{8,4},{10,6},{12,0},{14,2},{16,28},{18,... | collective-permute-start | bytes 491528 | tf_op jit(solution)/shard_map/ppermute | solution.py:361
  31.4 14.3 %copy-start.3 = (f32[3456]{0:T(1024)S(1)}, f32[3456]{0:T(1024)}, u32[]{:S(2)}) copy-start(f32[3456]{0:T(1024)} %param.27) | copy-start | bytes 41476
  31.4 19.3 %copy-start = (bf16[128,128]{1,0:T(8,128)(2,1)S(1)}, bf16[128,128]{1,0:T(8,128)(2,1)}, u32[]{:S(2)}) copy-start(bf16[128,128]{1,0:T(8,128)(2,1)} %refs_9_.1) | copy-start | bytes 98308
  31.4 19.3 %copy-start.1 = (f32[1,3456]{1,0:T(1,128)S(1)}, f32[1,3456]{1,0:T(1,128)}, u32[]{:S(2)}) copy-start(f32[1,3456]{1,0:T(1,128)} %refs_15_.1) | copy-start | bytes 41476
  31.4 19.3 %copy-start.2 = (s32[128]{0:T(128)S(1)}, s32[128]{0:T(128)}, u32[]{:S(2)}) copy-start(s32[128]{0:T(128)} %param.23) | copy-start | bytes 1540
  31.4 14.3 %collective-permute-start.4 = (bf16[640,128]{1,0:T(8,128)(2,1)S(1)}, bf16[640,128]{1,0:T(8,128)(2,1)S(1)}, u32[]{:S(2)}, u32[]{:S(2)}) collective-permute-start(bf16[640,128]{1,0:T(8,128)(2,1)S(1)} %get-tuple-element.33), channel_id=1, source_target_pairs={{0,2},{2,0},{4,6},{6,4},{8,10},{10,8},{12,14},{14,12},{16,18},{18,... | collective-permute-start | bytes 491528 | tf_op jit(solution)/shard_map/ppermute | solution.py:361
  38.2 7.5 %collective-permute-start.6 = (bf16[640,128]{1,0:T(8,128)(2,1)S(1)}, bf16[640,128]{1,0:T(8,128)(2,1)S(1)}, u32[]{:S(2)}, u32[]{:S(2)}) collective-permute-start(bf16[640,128]{1,0:T(8,128)(2,1)S(1)} %get-tuple-element.35), channel_id=1, source_target_pairs={{0,4},{2,6},{4,0},{6,2},{8,12},{10,14},{12,8},{14,10},{16,20},{18,... | collective-permute-start | bytes 491528 | tf_op jit(solution)/shard_map/ppermute | solution.py:361
  41.1 8.0 %collective-permute-start.8 = (bf16[640,128]{1,0:T(8,128)(2,1)S(1)}, bf16[640,128]{1,0:T(8,128)(2,1)S(1)}, u32[]{:S(2)}, u32[]{:S(2)}) collective-permute-start(bf16[640,128]{1,0:T(8,128)(2,1)S(1)} %get-tuple-element.37), channel_id=1, source_target_pairs={{0,6},{2,4},{4,2},{6,0},{8,14},{10,12},{12,10},{14,8},{16,22},{18,... | collective-permute-start | bytes 491528 | tf_op jit(solution)/shard_map/ppermute | solution.py:361
  41.8 7.3 %collective-permute-start.9 = (bf16[640,128]{1,0:T(8,128)(2,1)S(1)}, bf16[640,128]{1,0:T(8,128)(2,1)S(1)}, u32[]{:S(2)}, u32[]{:S(2)}) collective-permute-start(bf16[640,128]{1,0:T(8,128)(2,1)S(1)} %get-tuple-element.38), channel_id=1, source_target_pairs={{0,8},{2,10},{4,12},{6,14},{8,0},{10,2},{12,4},{14,6},{16,24},{18,... | collective-permute-start | bytes 491528 | tf_op jit(solution)/shard_map/ppermute | solution.py:361
  42.4 8.4 %collective-permute-start.10 = (bf16[640,128]{1,0:T(8,128)(2,1)S(1)}, bf16[640,128]{1,0:T(8,128)(2,1)S(1)}, u32[]{:S(2)}, u32[]{:S(2)}) collective-permute-start(bf16[640,128]{1,0:T(8,128)(2,1)S(1)} %get-tuple-element.39), channel_id=1, source_target_pairs={{0,10},{2,8},{4,14},{6,12},{8,2},{10,0},{12,6},{14,4},{16,26},{18,... | collective-permute-start | bytes 491528 | tf_op jit(solution)/shard_map/ppermute | solution.py:361
  74.2 11.7 %all-to-all-start.2 = ((bf16[8,320,128]{2,1,0:T(8,128)(2,1)}), bf16[8,320,128]{2,1,0:T(8,128)(2,1)S(1)}, u32[]{:S(2)}, u32[]{:S(2)}) async-start(bf16[8,320,128]{2,1,0:T(8,128)(2,1)} %bitcast.16), calls=%async_computation.2 | async-start | bytes 1310720 | tf_op jit(solution)/shard_map/all_to_all | solution.py:329
  79.5 2.3 %collective-permute-start.11 = (f32[1024,128]{1,0:T(8,128)S(1)}, f32[1024,128]{1,0:T(8,128)S(1)}, u32[]{:S(2)}, u32[]{:S(2)}) collective-permute-start(f32[1024,128]{1,0:T(8,128)S(1)} %shard_map.156.after_ref), channel_id=1, source_target_pairs={{0,1},{1,0},{2,3},{3,2},{4,5},{5,4},{6,7},{7,6},{8,9},{9,8},{10,11... | collective-permute-start | bytes 1572872 | tf_op jit(solution)/shard_map/ppermute | solution.py:323
  79.8 6.9 %collective-permute-start.12 = (s32[40,128]{1,0:T(8,128)S(1)}, s32[40,128]{1,0:T(8,128)S(1)}, u32[]{:S(2)}, u32[]{:S(2)}) collective-permute-start(s32[40,128]{1,0:T(8,128)S(1)} %pad_add_fusion.1.refs_0_), channel_id=1, source_target_pairs={{0,1},{1,0},{2,3},{3,2},{4,5},{5,4},{6,7},{7,6},{8,9},{9,8},{10,11... | collective-permute-start | bytes 61448 | tf_op jit(solution)/shard_map/ppermute | solution.py:323
  81.9 14.8 %collective-permute-start.17 = (bf16[1024,128]{1,0:T(8,128)(2,1)S(1)}, bf16[1024,128]{1,0:T(8,128)(2,1)S(1)}, u32[]{:S(2)}, u32[]{:S(2)}) collective-permute-start(bf16[1024,128]{1,0:T(8,128)(2,1)S(1)} %add_convert_fusion.after_ref), channel_id=1, source_target_pairs={{0,16},{2,18},{4,20},{6,22},{8,24},{10,26},{12,28},{14,30},{16,0},... | collective-permute-start | bytes 786440 | tf_op jit(solution)/shard_map/ppermute | solution.py:326
  86.0 1.5 %collective-permute-start.13 = (bf16[640,128]{1,0:T(8,128)(2,1)S(1)}, bf16[640,128]{1,0:T(8,128)(2,1)S(1)}, u32[]{:S(2)}, u32[]{:S(2)}) collective-permute-start(bf16[640,128]{1,0:T(8,128)(2,1)S(1)} %bitcast.51), channel_id=1, source_target_pairs={{0,1},{1,0},{2,3},{3,2},{4,5},{5,4},{6,7},{7,6},{8,9},{9,8},{10,11... | collective-permute-start | bytes 491528 | tf_op jit(solution)/shard_map/ppermute | solution.py:323
  86.1 1.6 %collective-permute-start.14 = (bf16[640,128]{1,0:T(8,128)(2,1)S(1)}, bf16[640,128]{1,0:T(8,128)(2,1)S(1)}, u32[]{:S(2)}, u32[]{:S(2)}) collective-permute-start(bf16[640,128]{1,0:T(8,128)(2,1)S(1)} %bitcast.50), channel_id=1, source_target_pairs={{0,1},{1,0},{2,3},{3,2},{4,5},{5,4},{6,7},{7,6},{8,9},{9,8},{10,11... | collective-permute-start | bytes 491528 | tf_op jit(solution)/shard_map/ppermute | solution.py:323
  86.5 1.4 %collective-permute-start.15 = (bf16[640,128]{1,0:T(8,128)(2,1)S(1)}, bf16[640,128]{1,0:T(8,128)(2,1)S(1)}, u32[]{:S(2)}, u32[]{:S(2)}) collective-permute-start(bf16[640,128]{1,0:T(8,128)(2,1)S(1)} %bitcast.49), channel_id=1, source_target_pairs={{0,1},{1,0},{2,3},{3,2},{4,5},{5,4},{6,7},{7,6},{8,9},{9,8},{10,11... | collective-permute-start | bytes 491528 | tf_op jit(solution)/shard_map/ppermute | solution.py:323
  86.6 1.5 %collective-permute-start.16 = (bf16[640,128]{1,0:T(8,128)(2,1)S(1)}, bf16[640,128]{1,0:T(8,128)(2,1)S(1)}, u32[]{:S(2)}, u32[]{:S(2)}) collective-permute-start(bf16[640,128]{1,0:T(8,128)(2,1)S(1)} %bitcast.48), channel_id=1, source_target_pairs={{0,1},{1,0},{2,3},{3,2},{4,5},{5,4},{6,7},{7,6},{8,9},{9,8},{10,11... | collective-permute-start | bytes 491528 | tf_op jit(solution)/shard_map/ppermute | solution.py:323

commit v5 on v4

--- a/solution.py
+++ b/solution.py
@@ -192,32 +192,37 @@
     crossed = [dot(x, w[...]).astype(BF16) for w in down]
     load_up.wait()
     total = jnp.zeros((samples, width), F32)
-    blocks = feats + 1
-    for k in range(blocks):
-        span = slice(k * width, (k + 1) * width)
+    wide = x_s.shape[1]
+    step = 2 * width
+    spans = [slice(k, min(k + step, wide)) for k in range(0, wide, step)]
+    for span in spans:
         factor = bias_ref[:, span]
         for c, w in zip(crossed, up):
             factor = factor + dot(c, w[:, span])
         factor_s[:, span] = factor
         base = x_s[:, span].astype(F32)
-        total = total + (base * factor + base) * head_ref[:, span]
+        terms = (base * factor + base) * head_ref[:, span]
+        for k in range(0, terms.shape[1], width):
+            total = total + terms[:, k : k + width]
     logits = jnp.sum(total, axis=1, keepdims=True)
     logit_ref[...] = jnp.broadcast_to(logits, (samples, samples)).T[0:1, :]
     labels = jnp.broadcast_to(labels_ref[...].astype(F32), (samples, samples)).T[:, 0:1]
     signal = loss_scale * (jax.nn.sigmoid(logits) - labels)
     lifts = []
-    for k in range(blocks):
-        span = slice(k * width, (k + 1) * width)
+    for span in spans:
         lifts.append(((signal * head_ref[:, span]) * x_s[:, span].astype(F32)).astype(BF16))
     lift = jnp.concatenate(lifts, axis=1)
     back = [dot(lift, w[...], NT).astype(BF16) for w in up]
-    for f in range(feats):
-        span = slice((f + 1) * width, (f + 2) * width)
+    for start in range(width, wide, step):
+        span = slice(start, min(start + step, wide))
         outer = signal * head_ref[:, span]
         grad = outer
         for c, w in zip(back, down):
             grad = grad + dot(c, w[span, :], NT)
-        bags_s[f * samples : (f + 1) * samples, :] = grad + outer * factor_s[:, span]
+        grad = grad + outer * factor_s[:, span]
+        for k in range(0, grad.shape[1], width):
+            f = (start + k) // width - 1
+            bags_s[f * samples : (f + 1) * samples, :] = grad[:, k : k + width]
 
     def place(f, carry):
         start = f * samples
@@ -364,7 +369,7 @@
     pairs = [(i, half - 1 - i) for i in range(half // 2, half)]
     group = len(pairs) // steps
     answers = [None] * half
-    after = [asked, asked]
+    after = [asked, asked, asked]
     for start in range(len(pairs) - group, -1, -group):
         partners = [p for pair in pairs[start : start + group] for p in pair]
         found = call(
@@ -372,7 +377,7 @@
             tuple(shape((2 * cap, width), BF16) for _ in partners),
             [ANY] + [VMEM] * (2 + replicas),
             [pltpu.VMEM((2, 2 * group * cap, rows_dev), BF16)],
-        )(after[-2], asked, table, *mirror)
+        )(after[-3], asked, table, *mirror)
         for partner, sums in zip(partners, found):
             answers[partner] = meet(sums, partner)
         after.append(answers[partners[0]])

time: 98 us -> 94.2 us (0.961)
  waiting for transfers between devices: 17.4 us -> 12.8 us
    ppermute x7, waiting for transfers between devices: 7.72 us -> 3.26 us  [meet(): return lax.ppermute(x, 'table', [(i, i ^ partner) for i in range(peers)])]
  transfers between devices with their start and end apart: 19 -> 19, of which waited for: 10 -> 9; matrix products, arithmetic and copies ran while one was open for 0% -> 0% of each run, Pallas kernels for 18% -> 19%
where the time goes in v5:
time: 94.2 us; the launch traced here: 93.8 us
  Pallas kernels  31.7 us (34%)
  blocking collectives  24.6 us (26%)
  starting transfers between devices  22.5 us (24%)
  waiting for transfers between devices  12.8 us (14%)
    all_to_all x2, blocking collectives, exchange(): lax.all_to_all(x, 'table', split_axis=0, concat_axis=0, axis_index_groups...  24.6 us
    pallas_call x1, Pallas kernels, body(): call(functools.partial(dense_kernel, replicas, half, cap), (shape((1, sam...  11.6 us
    ppermute x7, starting transfers between devices, meet(): return lax.ppermute(x, 'table', [(i, i ^ partner) for i in range(peers)])  9.59 us
    pallas_call x4, Pallas kernels, body(): call(functools.partial(lookup_kernel, half, cap, partners, replicas), tup...  9.5 us
    ppermute x2, starting transfers between devices, across(): lax.ppermute(x, 'table', [(i, (i + half) % peers) for i in range(peers)])  7.09 us
    pallas_call x3, Pallas kernels, scatter(): call(functools.partial(scatter_kernel, by, len(lines)), shape((own_rows,...  5.97 us
    ppermute x2, waiting for transfers between devices, across(): lax.ppermute(x, 'table', [(i, (i + half) % peers) for i in range(peers)])  5.96 us
    all_to_all x1, starting transfers between devices, exchange(): lax.all_to_all(x, 'table', split_axis=0, concat_axis=0, axis_index_groups...  3.54 us
  transfers between devices with their start and end apart: 19, of which 9 were waited for; matrix products, arithmetic and copies ran while one was open for 0% of the time, Pallas kernels for 19%

profile of v5, /device:TPU:0, one launch (start us, length us, event | category | flops | bytes accessed | tf_op | source)
XLA Modules:
  0.0 93.8 jit_solution(15628781897910685683)
XLA Ops:
  0.6 0.5 collective-permute-start.1
  1.2 2.2 %shard_map.149 = (bf16[2048,256]{1,0:T(8,128)(2,1)S(1)}, bf16[1024,128]{1,0:T(8,128)(2,1)S(1)}) custom-call(s32[256]{0:T(256)} %local_ref.1, s32[256]{0:T(256)} %new_ref.1, s32[2048]{0:T(1024)} %versions_ref.1, f32[2048,128]{1,0:T(8,128)} %table_ref.1, f32[256,128]{1,0:T(8,128)} %values_ref.1), custom_call_target="tpu_custom_call" | custom-call | flops 1024 | bytes 1024 | tf_op jit(solution)/shard_map/pallas_call | solution.py:339
  3.4 4.1 %collective-permute-start = (bf16[1024,128]{1,0:T(8,128)(2,1)S(1)}, bf16[1024,128]{1,0:T(8,128)(2,1)S(1)}, u32[]{:S(2)}, u32[]{:S(2)}) collective-permute-start(bf16[1024,128]{1,0:T(8,128)(2,1)S(1)} %get-tuple-element.26.after_ref), channel_id=1, source_target_pairs={{0,16},{2,18},{4,20},{6,22},{8,24},{10,26},{12,28},{14,30},{16,0},... | collective-permute-start | bytes 786440 | tf_op jit(solution)/shard_map/ppermute | solution.py:331
  7.5 2.4 %shard_map.150 = (s32[26,128]{1,0:T(8,128)S(1)}, s32[128,128]{1,0:T(8,128)S(1)}) custom-call(bf16[1024,128]{1,0:T(8,128)(2,1)S(1)} %get-tuple-element.26.after_ref, s32[26,1,128]{2,1,0:T(1,128)} %bitcast.59, s32[26,2,128]{2,1,0:T(2,128)} %bitcast.57, s32[26,128]{1,0:T(8,128)} %bitcast.58), custom_call_target="tpu_custom_call" | custom-call | flops 1024 | bytes 1024 | tf_op jit(solution)/shard_map/pallas_call | solution.py:345
  10.0 12.3 %all_to_all.15 = s32[8,16,128]{2,1,0:T(8,128)S(1)} all-to-all(s32[8,16,128]{2,1,0:T(8,128)S(1)} %bitcast.43), channel_id=1, replica_groups={{0,2,4,6,8,10,12,14},{16,18,20,22,24,26,28,30},{1,3,5,7,9,11,13,15},{17..., dimensions={0} | all-to-all | bytes 131072 | tf_op jit(solution)/shard_map/all_to_all | solution.py:334
  22.2 1.5 %collective-permute-done.3.refs_1_ = bf16[1024,128]{1,0:T(8,128)(2,1)S(1)} collective-permute-done((bf16[1024,128]{1,0:T(8,128)(2,1)S(1)}, bf16[1024,128]{1,0:T(8,128)(2,1)S(1)}, u32[]{:S(2)}, u32[]{:S(2)}) %collective-permute-start.3) | collective-permute-done | bytes 262176 | tf_op jit(solution)/shard_map/ppermute | solution.py:328
  23.8 2.4 %shard_map.151 = (bf16[640,128]{1,0:T(8,128)(2,1)S(1)}, bf16[640,128]{1,0:T(8,128)(2,1)S(1)}) custom-call(s32[128,128]{1,0:T(8,128)S(1)} %bitcast.30, s32[128,128]{1,0:T(8,128)S(1)} %bitcast.31, bf16[2048,256]{1,0:T(8,128)(2,1)S(1)} %get-tuple-element.30.table_ref, bf16[1024,128]{1,0:T(8,128)(2,1)S(1)} %collective-permute-done.refs_0_, ...), custom_call_target="tpu_custom_call" | custom-call | flops 1024 | bytes 1024 | tf_op jit(solution)/shard_map/pallas_call | solution.py:375
  26.3 2.4 %shard_map.153 = (bf16[640,128]{1,0:T(8,128)(2,1)S(1)}, bf16[640,128]{1,0:T(8,128)(2,1)S(1)}) custom-call(s32[128,128]{1,0:T(8,128)S(1)} %bitcast.32, s32[128,128]{1,0:T(8,128)S(1)} %bitcast.33, bf16[2048,256]{1,0:T(8,128)(2,1)S(1)} %get-tuple-element.30.table_ref, bf16[1024,128]{1,0:T(8,128)(2,1)S(1)} %collective-permute-done.refs_0_, ...), custom_call_target="tpu_custom_call" | custom-call | flops 1024 | bytes 1024 | tf_op jit(solution)/shard_map/pallas_call | solution.py:375
  28.7 0.6 collective-permute-start.5
  29.3 3.8 %collective-permute-start.9 = (bf16[640,128]{1,0:T(8,128)(2,1)S(1)}, bf16[640,128]{1,0:T(8,128)(2,1)S(1)}, u32[]{:S(2)}, u32[]{:S(2)}) collective-permute-start(bf16[640,128]{1,0:T(8,128)(2,1)S(1)} %get-tuple-element.38), channel_id=1, source_target_pairs={{0,10},{2,8},{4,14},{6,12},{8,2},{10,0},{12,6},{14,4},{16,26},{18,... | collective-permute-start | bytes 491528 | tf_op jit(solution)/shard_map/ppermute | solution.py:366
  33.1 2.4 %shard_map.152 = (bf16[640,128]{1,0:T(8,128)(2,1)S(1)}, bf16[640,128]{1,0:T(8,128)(2,1)S(1)}) custom-call(s32[128,128]{1,0:T(8,128)S(1)} %bitcast.34, s32[128,128]{1,0:T(8,128)S(1)} %bitcast.35, bf16[2048,256]{1,0:T(8,128)(2,1)S(1)} %get-tuple-element.30.table_ref, bf16[1024,128]{1,0:T(8,128)(2,1)S(1)} %collective-permute-done.refs_0_, ...), custom_call_target="tpu_custom_call" | custom-call | flops 1024 | bytes 1024 | tf_op jit(solution)/shard_map/pallas_call | solution.py:375
  35.5 0.6 collective-permute-start.4
  36.2 2.4 %shard_map.154 = (bf16[640,128]{1,0:T(8,128)(2,1)S(1)}, bf16[640,128]{1,0:T(8,128)(2,1)S(1)}) custom-call(bf16[640,128]{1,0:T(8,128)(2,1)S(1)} %collective-permute-done.6.after_ref.refs_7_, s32[128,128]{1,0:T(8,128)S(1)} %bitcast.36, bf16[2048,256]{1,0:T(8,128)(2,1)S(1)} %get-tuple-element.30.table_ref, bf16[1024,128]{1,0:T(8,128)(2,1)S(1)} %collective-permute-done.refs_0_, ...), custom_call_target="tpu_custom_call" | custom-call | flops 1024 | bytes 1024 | tf_op jit(solution)/shard_map/pallas_call | solution.py:375
  38.6 1.5 %collective-permute-start.7 = (bf16[640,128]{1,0:T(8,128)(2,1)S(1)}, bf16[640,128]{1,0:T(8,128)(2,1)S(1)}, u32[]{:S(2)}, u32[]{:S(2)}) collective-permute-start(bf16[640,128]{1,0:T(8,128)(2,1)S(1)} %get-tuple-element.36), channel_id=1, source_target_pairs={{0,6},{2,4},{4,2},{6,0},{8,14},{10,12},{12,10},{14,8},{16,22},{18,... | collective-permute-start | bytes 491528 | tf_op jit(solution)/shard_map/ppermute | solution.py:366
  40.0 2.9 %collective-permute-start.8 = (bf16[640,128]{1,0:T(8,128)(2,1)S(1)}, bf16[640,128]{1,0:T(8,128)(2,1)S(1)}, u32[]{:S(2)}, u32[]{:S(2)}) collective-permute-start(bf16[640,128]{1,0:T(8,128)(2,1)S(1)} %get-tuple-element.37), channel_id=1, source_target_pairs={{0,8},{2,10},{4,12},{6,14},{8,0},{10,2},{12,4},{14,6},{16,24},{18,... | collective-permute-start | bytes 491528 | tf_op jit(solution)/shard_map/ppermute | solution.py:366
  43.0 2.4 %collective-permute-done.7.refs_3_ = bf16[640,128]{1,0:T(8,128)(2,1)S(1)} collective-permute-done((bf16[640,128]{1,0:T(8,128)(2,1)S(1)}, bf16[640,128]{1,0:T(8,128)(2,1)S(1)}, u32[]{:S(2)}, u32[]{:S(2)}) %collective-permute-start.7) | collective-permute-done | bytes 163872 | tf_op jit(solution)/shard_map/ppermute | solution.py:366
  45.3 0.9 collective-permute-done.8.refs_4_
  46.2 11.6 %shard_map.155 = (f32[1,128]{1,0:T(1,128)}, bf16[2560,128]{1,0:T(8,128)(2,1)}, bf16[2560,128]{1,0:T(8,128)(2,1)S(1)}) custom-call(bf16[640,128]{1,0:T(8,128)(2,1)S(1)} %get-tuple-element.32.refs_0_, bf16[640,128]{1,0:T(8,128)(2,1)S(1)} %collective-permute-done.4.refs_1_, bf16[640,128]{1,0:T(8,128)(2,1)S(1)} %collective-permute-done.5.refs_2_, ...), custom_call_target="tpu_custom_call" | custom-call | flops 1024 | bytes 1024 | tf_op jit(solution)/shard_map/pallas_call | solution.py:385
  57.8 12.3 %all_to_all.16 = bf16[8,320,128]{2,1,0:T(8,128)(2,1)S(1)} all-to-all(bf16[8,320,128]{2,1,0:T(8,128)(2,1)S(1)} %bitcast.42), channel_id=1, replica_groups={{0,2,4,6,8,10,12,14},{16,18,20,22,24,26,28,30},{1,3,5,7,9,11,13,15},{17..., dimensions={0} | all-to-all | bytes 1310720 | tf_op jit(solution)/shard_map/all_to_all | solution.py:334
  70.2 3.5 %all-to-all-start.2 = ((bf16[8,320,128]{2,1,0:T(8,128)(2,1)}), bf16[8,320,128]{2,1,0:T(8,128)(2,1)S(1)}, u32[]{:S(2)}, u32[]{:S(2)}) async-start(bf16[8,320,128]{2,1,0:T(8,128)(2,1)} %bitcast.16), calls=%async_computation.2 | async-start | bytes 1310720 | tf_op jit(solution)/shard_map/all_to_all | solution.py:334
  73.9 1.5 %shard_map.156.after_ref = f32[1024,128]{1,0:T(8,128)S(1)} custom-call(s32[128,128]{1,0:T(8,128)S(1)} %bitcast.38, s32[40,128]{1,0:T(8,128)S(1)} %pad_add_fusion.refs_0_, bf16[2560,128]{1,0:T(8,128)(2,1)S(1)} %bitcast.40), custom_call_target="tpu_custom_call" | custom-call | flops 1024 | bytes 1024 | tf_op jit(solution)/shard_map/pallas_call | solution.py:428
  75.7 0.6 collective-permute-start.12
  76.2 1.5 %shard_map.157 = f32[1024,128]{1,0:T(8,128)S(1)} custom-call(f32[1024,128]{1,0:T(8,128)S(1)} %shard_map.156.after_ref, s32[40,128]{1,0:T(8,128)S(1)} %pad_add_fusion.refs_0_, bf16[2560,128]{1,0:T(8,128)(2,1)S(1)} %bitcast.41), custom_call_target="tpu_custom_call" | custom-call | flops 1024 | bytes 1024 | tf_op jit(solution)/shard_map/pallas_call | solution.py:428
  77.8 3.0 %collective-permute-start.17 = (bf16[1024,128]{1,0:T(8,128)(2,1)S(1)}, bf16[1024,128]{1,0:T(8,128)(2,1)S(1)}, u32[]{:S(2)}, u32[]{:S(2)}) collective-permute-start(bf16[1024,128]{1,0:T(8,128)(2,1)S(1)} %add_convert_fusion.after_ref), channel_id=1, source_target_pairs={{0,16},{2,18},{4,20},{6,22},{8,24},{10,26},{12,28},{14,30},{16,0},... | collective-permute-start | bytes 786440 | tf_op jit(solution)/shard_map/ppermute | solution.py:331
  80.9 1.0 %all-to-all-done.2 = bf16[8,320,128]{2,1,0:T(8,128)(2,1)S(1)} async-done(((bf16[8,320,128]{2,1,0:T(8,128)(2,1)}), bf16[8,320,128]{2,1,0:T(8,128)(2,1)S(1)}, u32[]{:S(2)}, u32[]{:S(2)}) %all-to-all-start.2) | async-done | bytes 655392 | tf_op jit(solution)/shard_map/all_to_all | solution.py:334
  82.0 0.5 collective-permute-start.14
  82.5 0.4 collective-permute-start.16
  83.0 0.4 collective-permute-done.13.refs_3_
  83.6 0.3 collective-permute-done.15.refs_5_
  84.1 2.9 %shard_map.158 = f32[1024,128]{1,0:T(8,128)S(1)} custom-call(bf16[1024,128]{1,0:T(8,128)(2,1)S(1)} %add_convert_fusion.after_ref, s32[40,128]{1,0:T(8,128)S(1)} %pad_add_fusion.1.refs_0_, s32[40,128]{1,0:T(8,128)S(1)} %collective-permute-done.12.refs_1_, bf16[2560,128]{1,0:T(8,128)(2,1)S(1)} %bitcast.39, ...), custom_call_target="tpu_custom_call" | custom-call | flops 1024 | bytes 1024 | tf_op jit(solution)/shard_map/pallas_call | solution.py:428
  87.0 6.0 %collective-permute-done.17 = bf16[1024,128]{1,0:T(8,128)(2,1)S(1)} collective-permute-done((bf16[1024,128]{1,0:T(8,128)(2,1)S(1)}, bf16[1024,128]{1,0:T(8,128)(2,1)S(1)}, u32[]{:S(2)}, u32[]{:S(2)}) %collective-permute-start.17) | collective-permute-done | bytes 262176 | tf_op jit(solution)/shard_map/ppermute | solution.py:331
  93.0 0.9 convert_add_fusion
  (39 shorter events, 1.5 us)
Async XLA Ops:
  0.6 21.6 %collective-permute-start.1 = (bf16[3456,256]{1,0:T(8,128)(2,1)}, bf16[3456,256]{1,0:T(8,128)(2,1)S(1)}, u32[]{:S(2)}, u32[]{:S(2)}) collective-permute-start(bf16[3456,256]{1,0:T(8,128)(2,1)} %bitcast.45), channel_id=1, source_target_pairs={{0,1},{1,0},{2,3},{3,2},{4,5},{5,4},{6,7},{7,6},{8,9},{9,8},{10,11... | collective-permute-start | bytes 5308424 | tf_op jit(solution)/shard_map/ppermute | solution.py:328
  1.1 21.1 %collective-permute-start.2 = (bf16[256,3456]{1,0:T(8,128)(2,1)}, bf16[256,3456]{1,0:T(8,128)(2,1)S(1)}, u32[]{:S(2)}, u32[]{:S(2)}) collective-permute-start(bf16[256,3456]{1,0:T(8,128)(2,1)} %bitcast.47), channel_id=1, source_target_pairs={{0,1},{1,0},{2,3},{3,2},{4,5},{5,4},{6,7},{7,6},{8,9},{9,8},{10,11... | collective-permute-start | bytes 5308424 | tf_op jit(solution)/shard_map/ppermute | solution.py:328
  3.4 18.8 %collective-permute-start = (bf16[1024,128]{1,0:T(8,128)(2,1)S(1)}, bf16[1024,128]{1,0:T(8,128)(2,1)S(1)}, u32[]{:S(2)}, u32[]{:S(2)}) collective-permute-start(bf16[1024,128]{1,0:T(8,128)(2,1)S(1)} %get-tuple-element.26.after_ref), channel_id=1, source_target_pairs={{0,16},{2,18},{4,20},{6,22},{8,24},{10,26},{12,28},{14,30},{16,0},... | collective-permute-start | bytes 786440 | tf_op jit(solution)/shard_map/ppermute | solution.py:331
  22.2 1.5 %collective-permute-start.3 = (bf16[1024,128]{1,0:T(8,128)(2,1)S(1)}, bf16[1024,128]{1,0:T(8,128)(2,1)S(1)}, u32[]{:S(2)}, u32[]{:S(2)}) collective-permute-start(bf16[1024,128]{1,0:T(8,128)(2,1)S(1)} %collective-permute-done.refs_0_), channel_id=1, source_target_pairs={{0,1},{1,0},{2,3},{3,2},{4,5},{5,4},{6,7},{7,6},{8,9},{9,8},{10,11... | collective-permute-start | bytes 786440 | tf_op jit(solution)/shard_map/ppermute | solution.py:328
  26.1 10.0 %collective-permute-start.6 = (bf16[640,128]{1,0:T(8,128)(2,1)S(1)}, bf16[640,128]{1,0:T(8,128)(2,1)S(1)}, u32[]{:S(2)}, u32[]{:S(2)}) collective-permute-start(bf16[640,128]{1,0:T(8,128)(2,1)S(1)} %get-tuple-element.35), channel_id=1, source_target_pairs={{0,14},{2,12},{4,10},{6,8},{8,6},{10,4},{12,2},{14,0},{16,30},{18,... | collective-permute-start | bytes 491528 | tf_op jit(solution)/shard_map/ppermute | solution.py:366
  28.7 14.2 %copy-start.3 = (f32[3456]{0:T(1024)S(1)}, f32[3456]{0:T(1024)}, u32[]{:S(2)}) copy-start(f32[3456]{0:T(1024)} %param.27) | copy-start | bytes 41476
  28.7 11.3 %collective-permute-start.5 = (bf16[640,128]{1,0:T(8,128)(2,1)S(1)}, bf16[640,128]{1,0:T(8,128)(2,1)S(1)}, u32[]{:S(2)}, u32[]{:S(2)}) collective-permute-start(bf16[640,128]{1,0:T(8,128)(2,1)S(1)} %get-tuple-element.34), channel_id=1, source_target_pairs={{0,4},{2,6},{4,0},{6,2},{8,12},{10,14},{12,8},{14,10},{16,20},{18,... | collective-permute-start | bytes 491528 | tf_op jit(solution)/shard_map/ppermute | solution.py:366
  29.3 16.9 %copy-start = (bf16[128,128]{1,0:T(8,128)(2,1)S(1)}, bf16[128,128]{1,0:T(8,128)(2,1)}, u32[]{:S(2)}) copy-start(bf16[128,128]{1,0:T(8,128)(2,1)} %refs_9_.1) | copy-start | bytes 98308
  29.3 16.9 %copy-start.1 = (f32[1,3456]{1,0:T(1,128)S(1)}, f32[1,3456]{1,0:T(1,128)}, u32[]{:S(2)}) copy-start(f32[1,3456]{1,0:T(1,128)} %refs_15_.1) | copy-start | bytes 41476
  29.3 16.9 %copy-start.2 = (s32[128]{0:T(128)S(1)}, s32[128]{0:T(128)}, u32[]{:S(2)}) copy-start(s32[128]{0:T(128)} %param.23) | copy-start | bytes 1540
  29.3 13.7 %collective-permute-start.9 = (bf16[640,128]{1,0:T(8,128)(2,1)S(1)}, bf16[640,128]{1,0:T(8,128)(2,1)S(1)}, u32[]{:S(2)}, u32[]{:S(2)}) collective-permute-start(bf16[640,128]{1,0:T(8,128)(2,1)S(1)} %get-tuple-element.38), channel_id=1, source_target_pairs={{0,10},{2,8},{4,14},{6,12},{8,2},{10,0},{12,6},{14,4},{16,26},{18,... | collective-permute-start | bytes 491528 | tf_op jit(solution)/shard_map/ppermute | solution.py:366
  35.5 7.5 %collective-permute-start.10 = (bf16[640,128]{1,0:T(8,128)(2,1)S(1)}, bf16[640,128]{1,0:T(8,128)(2,1)S(1)}, u32[]{:S(2)}, u32[]{:S(2)}) collective-permute-start(bf16[640,128]{1,0:T(8,128)(2,1)S(1)} %get-tuple-element.39), channel_id=1, source_target_pairs={{0,12},{2,14},{4,8},{6,10},{8,4},{10,6},{12,0},{14,2},{16,28},{18,... | collective-permute-start | bytes 491528 | tf_op jit(solution)/shard_map/ppermute | solution.py:366
  35.5 7.4 %collective-permute-start.4 = (bf16[640,128]{1,0:T(8,128)(2,1)S(1)}, bf16[640,128]{1,0:T(8,128)(2,1)S(1)}, u32[]{:S(2)}, u32[]{:S(2)}) collective-permute-start(bf16[640,128]{1,0:T(8,128)(2,1)S(1)} %get-tuple-element.33), channel_id=1, source_target_pairs={{0,2},{2,0},{4,6},{6,4},{8,10},{10,8},{12,14},{14,12},{16,18},{18,... | collective-permute-start | bytes 491528 | tf_op jit(solution)/shard_map/ppermute | solution.py:366
  38.6 6.8 %collective-permute-start.7 = (bf16[640,128]{1,0:T(8,128)(2,1)S(1)}, bf16[640,128]{1,0:T(8,128)(2,1)S(1)}, u32[]{:S(2)}, u32[]{:S(2)}) collective-permute-start(bf16[640,128]{1,0:T(8,128)(2,1)S(1)} %get-tuple-element.36), channel_id=1, source_target_pairs={{0,6},{2,4},{4,2},{6,0},{8,14},{10,12},{12,10},{14,8},{16,22},{18,... | collective-permute-start | bytes 491528 | tf_op jit(solution)/shard_map/ppermute | solution.py:366
  40.0 6.2 %collective-permute-start.8 = (bf16[640,128]{1,0:T(8,128)(2,1)S(1)}, bf16[640,128]{1,0:T(8,128)(2,1)S(1)}, u32[]{:S(2)}, u32[]{:S(2)}) collective-permute-start(bf16[640,128]{1,0:T(8,128)(2,1)S(1)} %get-tuple-element.37), channel_id=1, source_target_pairs={{0,8},{2,10},{4,12},{6,14},{8,0},{10,2},{12,4},{14,6},{16,24},{18,... | collective-permute-start | bytes 491528 | tf_op jit(solution)/shard_map/ppermute | solution.py:366
  70.2 11.7 %all-to-all-start.2 = ((bf16[8,320,128]{2,1,0:T(8,128)(2,1)}), bf16[8,320,128]{2,1,0:T(8,128)(2,1)S(1)}, u32[]{:S(2)}, u32[]{:S(2)}) async-start(bf16[8,320,128]{2,1,0:T(8,128)(2,1)} %bitcast.16), calls=%async_computation.2 | async-start | bytes 1310720 | tf_op jit(solution)/shard_map/all_to_all | solution.py:334
  75.4 2.3 %collective-permute-start.11 = (f32[1024,128]{1,0:T(8,128)S(1)}, f32[1024,128]{1,0:T(8,128)S(1)}, u32[]{:S(2)}, u32[]{:S(2)}) collective-permute-start(f32[1024,128]{1,0:T(8,128)S(1)} %shard_map.156.after_ref), channel_id=1, source_target_pairs={{0,1},{1,0},{2,3},{3,2},{4,5},{5,4},{6,7},{7,6},{8,9},{9,8},{10,11... | collective-permute-start | bytes 1572872 | tf_op jit(solution)/shard_map/ppermute | solution.py:328
  75.7 6.9 %collective-permute-start.12 = (s32[40,128]{1,0:T(8,128)S(1)}, s32[40,128]{1,0:T(8,128)S(1)}, u32[]{:S(2)}, u32[]{:S(2)}) collective-permute-start(s32[40,128]{1,0:T(8,128)S(1)} %pad_add_fusion.1.refs_0_), channel_id=1, source_target_pairs={{0,1},{1,0},{2,3},{3,2},{4,5},{5,4},{6,7},{7,6},{8,9},{9,8},{10,11... | collective-permute-start | bytes 61448 | tf_op jit(solution)/shard_map/ppermute | solution.py:328
  77.8 15.1 %collective-permute-start.17 = (bf16[1024,128]{1,0:T(8,128)(2,1)S(1)}, bf16[1024,128]{1,0:T(8,128)(2,1)S(1)}, u32[]{:S(2)}, u32[]{:S(2)}) collective-permute-start(bf16[1024,128]{1,0:T(8,128)(2,1)S(1)} %add_convert_fusion.after_ref), channel_id=1, source_target_pairs={{0,16},{2,18},{4,20},{6,22},{8,24},{10,26},{12,28},{14,30},{16,0},... | collective-permute-start | bytes 786440 | tf_op jit(solution)/shard_map/ppermute | solution.py:331
  81.9 1.5 %collective-permute-start.13 = (bf16[640,128]{1,0:T(8,128)(2,1)S(1)}, bf16[640,128]{1,0:T(8,128)(2,1)S(1)}, u32[]{:S(2)}, u32[]{:S(2)}) collective-permute-start(bf16[640,128]{1,0:T(8,128)(2,1)S(1)} %bitcast.52), channel_id=1, source_target_pairs={{0,1},{1,0},{2,3},{3,2},{4,5},{5,4},{6,7},{7,6},{8,9},{9,8},{10,11... | collective-permute-start | bytes 491528 | tf_op jit(solution)/shard_map/ppermute | solution.py:328
  82.0 1.6 %collective-permute-start.14 = (bf16[640,128]{1,0:T(8,128)(2,1)S(1)}, bf16[640,128]{1,0:T(8,128)(2,1)S(1)}, u32[]{:S(2)}, u32[]{:S(2)}) collective-permute-start(bf16[640,128]{1,0:T(8,128)(2,1)S(1)} %bitcast.51), channel_id=1, source_target_pairs={{0,1},{1,0},{2,3},{3,2},{4,5},{5,4},{6,7},{7,6},{8,9},{9,8},{10,11... | collective-permute-start | bytes 491528 | tf_op jit(solution)/shard_map/ppermute | solution.py:328
  82.5 1.4 %collective-permute-start.15 = (bf16[640,128]{1,0:T(8,128)(2,1)S(1)}, bf16[640,128]{1,0:T(8,128)(2,1)S(1)}, u32[]{:S(2)}, u32[]{:S(2)}) collective-permute-start(bf16[640,128]{1,0:T(8,128)(2,1)S(1)} %bitcast.50), channel_id=1, source_target_pairs={{0,1},{1,0},{2,3},{3,2},{4,5},{5,4},{6,7},{7,6},{8,9},{9,8},{10,11... | collective-permute-start | bytes 491528 | tf_op jit(solution)/shard_map/ppermute | solution.py:328
  82.5 1.5 %collective-permute-start.16 = (bf16[640,128]{1,0:T(8,128)(2,1)S(1)}, bf16[640,128]{1,0:T(8,128)(2,1)S(1)}, u32[]{:S(2)}, u32[]{:S(2)}) collective-permute-start(bf16[640,128]{1,0:T(8,128)(2,1)S(1)} %bitcast.49), channel_id=1, source_target_pairs={{0,1},{1,0},{2,3},{3,2},{4,5},{5,4},{6,7},{7,6},{8,9},{9,8},{10,11... | collective-permute-start | bytes 491528 | tf_op jit(solution)/shard_map/ppermute | solution.py:328

commit v6 on v5

--- a/solution.py
+++ b/solution.py
@@ -30,9 +30,13 @@
 
 
 def route_kernel(
-    peers, cap, after_ref, owner_ref, rows_ref, len_ref, pos_ref, req_ref, own_s, one_s, two_s, a_s, b_s
+    peers, cap, table_ref, owner_ref, rows_ref, len_ref, pos_ref, req_ref, table_out_ref, own_s, one_s, two_s, a_s, b_s
 ):
-    del after_ref
+    held_rows, width = table_out_ref.shape[0], table_ref.shape[1]
+    table = table_ref[0:held_rows, :]
+    high = table.astype(BF16)
+    table_out_ref[:, 0:width] = high
+    table_out_ref[:, width:] = (table - high.astype(F32)).astype(BF16)
     feats, lanes = len_ref.shape
     padded = own_s.shape[0]
     chunks = -(-cap // LANES)
@@ -64,6 +68,7 @@
     column = jnp.where(far, own - half, own)
     side = (lax.axis_index("table") >= half).astype(I32)
     mirrored = jnp.where(far, 1 - side, side)
+    column = jnp.where(mirrored > 0, column ^ (half // 2), column)
     place = jnp.where(own < 0, -8, column * 2 + mirrored)
     pos_ref[...] = ((mirrored * half + column) * cap + rank)[0:feats, :]
     first = place * per + lax.shift_right_logical(rank, 7)
@@ -86,7 +91,7 @@
 
 
 def update_kernel(
-    local_ref, new_ref, versions_ref, table_ref, values_ref, table_out_ref, part_ref, rows_s
+    local_ref, new_ref, versions_ref, table_ref, values_ref, rows_s, part_ref
 ):
     held_rows, width = table_ref.shape
     rows_s[0:held_rows, :] = table_ref[...]
@@ -97,11 +102,7 @@
         rows_s[pl.ds(to, 1), :] = values_ref[pl.ds(i, 1), :]
         return carry
 
-    lax.fori_loop(0, values_ref.shape[0], entry, 0, unroll=8)
-    table = rows_s[0:held_rows, :]
-    high = table.astype(BF16)
-    table_out_ref[:, 0:width] = high
-    table_out_ref[:, width:] = (table - high.astype(F32)).astype(BF16)
+    lax.fori_loop(0, values_ref.shape[0], entry, 0, unroll=32)
     own_rows = part_ref.shape[0]
     start = pl.multiple_of(lax.axis_index("dp") * own_rows, own_rows)
     part_ref[...] = rows_s[pl.ds(start, own_rows), :].astype(BF16)
@@ -212,14 +213,14 @@
     for span in spans:
         lifts.append(((signal * head_ref[:, span]) * x_s[:, span].astype(F32)).astype(BF16))
     lift = jnp.concatenate(lifts, axis=1)
-    back = [dot(lift, w[...], NT).astype(BF16) for w in up]
+    back = [dot(w[...], lift, NT).astype(BF16) for w in up]
     for start in range(width, wide, step):
         span = slice(start, min(start + step, wide))
         outer = signal * head_ref[:, span]
-        grad = outer
+        turned = 0.0
         for c, w in zip(back, down):
-            grad = grad + dot(c, w[span, :], NT)
-        grad = grad + outer * factor_s[:, span]
+            turned = turned + dot(w[span, :], c)
+        grad = outer + turned.T + outer * factor_s[:, span]
         for k in range(0, grad.shape[1], width):
             f = (start + k) // width - 1
             bags_s[f * samples : (f + 1) * samples, :] = grad[:, k : k + width]
@@ -328,7 +329,8 @@
         return lax.ppermute(x, "dp", [(i, (i + by) % replicas) for i in range(replicas)])
 
     def across(x):
-        return lax.ppermute(x, "table", [(i, (i + half) % peers) for i in range(peers)])
+        far = half + half // 2
+        return lax.ppermute(x, "table", [(i, i ^ far) for i in range(peers)])
 
     def exchange(x):
         return lax.all_to_all(
@@ -336,22 +338,25 @@
         )
 
 
-    table, part = call(
+    rows, part = call(
         update_kernel,
-        (shape((rows_dev, 2 * width), BF16), shape((own_rows, width), BF16)),
+        (shape((rows_dev + 8, width), F32), shape((own_rows, width), BF16)),
         [SMEM] * 3 + [VMEM] * 2,
-        [pltpu.VMEM((rows_dev + 8, width), F32)],
     )(*map(in_hbm, (conf_local, conf_version, versions, emb_table, conf_values)))
-    position, requests = call(
+    position, requests, table = call(
         functools.partial(route_kernel, peers, cap),
-        (shape((feats, samples), I32), shape((peers * per, LANES), I32)),
-        [ANY] + [VMEM] * 3,
+        (
+            shape((feats, samples), I32),
+            shape((peers * per, LANES), I32),
+            shape((rows_dev, 2 * width), BF16),
+        ),
+        [VMEM] * 4,
         [pltpu.VMEM((round_up(feats, 8), samples), I32)] * 3
         + [
             pltpu.VMEM((2 * peers * per, feats * samples), BF16),
             pltpu.VMEM((LANES, feats * samples), BF16),
         ],
-    )(part, *map(in_hbm, (owners.transpose(1, 2, 0), row_local.transpose(1, 2, 0), lengths.T)))
+    )(rows, *map(in_hbm, (owners.transpose(1, 2, 0), row_local.transpose(1, 2, 0), lengths.T)))
     down = [shift(cross_down[0], by) for by in range(replicas)]
     up = [shift(cross_up[0], by) for by in range(replicas)]
     asked = exchange(requests.reshape(half, 2 * per, LANES)).reshape(2 * half * per, LANES)
@@ -440,6 +445,7 @@
     own = scatter(0, last, [mirror_lines], [got_mirror])
     mirrored = functools.reduce(jnp.add, [own] + parts).astype(BF16)
     returned = across(mirrored)
+    _, native_lines = lax.optimization_barrier((mirrored, native_lines))
     every_line = [shift(native_lines, by) for by in range(replicas)]
     pieces = 4 if half * cap % 64 == 0 else 1
     size = half * cap // pieces

time: 94.2 us -> 89.8 us (0.953)
  the two profiles are of different devices: /device:TPU:0 before, /device:TPU:18 now
where the time goes in v6:
time: 89.8 us; the launch traced here: 89.4 us
  Pallas kernels  31.6 us (35%)
  blocking collectives  21.9 us (24%)
  starting transfers between devices  17.4 us (19%)
  waiting for transfers between devices  16.4 us (18%)
  other arithmetic  0.93 us (1%)
    all_to_all x2, blocking collectives, exchange(): lax.all_to_all(x, 'table', split_axis=0, concat_axis=0, axis_index_groups...  21.9 us
    pallas_call x1, Pallas kernels, body(): call(functools.partial(dense_kernel, replicas, half, cap), (shape((1, sam...  11.5 us
    ppermute x7, starting transfers between devices, meet(): return lax.ppermute(x, 'table', [(i, i ^ partner) for i in range(peers)])  9.6 us
    pallas_call x4, Pallas kernels, body(): call(functools.partial(lookup_kernel, half, cap, partners, replicas), tup...  9.51 us
    ppermute x2, waiting for transfers between devices, across(): return lax.ppermute(x, 'table', [(i, i ^ far) for i in range(peers)])  7.56 us
    pallas_call x3, Pallas kernels, scatter(): call(functools.partial(scatter_kernel, by, len(lines)), shape((own_rows,...  5.97 us
    all_to_all x1, starting transfers between devices, exchange(): lax.all_to_all(x, 'table', split_axis=0, concat_axis=0, axis_index_groups...  5.08 us
    ppermute x7, waiting for transfers between devices, meet(): return lax.ppermute(x, 'table', [(i, i ^ partner) for i in range(peers)])  3.39 us
  transfers between devices with their start and end apart: 19, of which 11 were waited for; matrix products, arithmetic and copies ran while one was open for 0% of the time, Pallas kernels for 20%

profile of v6, /device:TPU:18, one launch (start us, length us, event | category | flops | bytes accessed | tf_op | source)
XLA Modules:
  0.0 89.4 jit_solution(17261881515082426579)
XLA Ops:
  0.7 0.5 collective-permute-start.2
  1.2 1.9 %shard_map.149 = (f32[2056,128]{1,0:T(8,128)S(1)}, bf16[1024,128]{1,0:T(8,128)(2,1)S(1)}) custom-call(s32[256]{0:T(256)} %local_ref.1, s32[256]{0:T(256)} %new_ref.1, s32[2048]{0:T(1024)} %versions_ref.1, f32[2048,128]{1,0:T(8,128)} %table_ref.1, f32[256,128]{1,0:T(8,128)} %values_ref.1), custom_call_target="tpu_custom_call" | custom-call | flops 1024 | bytes 1024 | tf_op jit(solution)/shard_map/pallas_call | solution.py:341
  3.1 0.5 collective-permute-start
  3.6 2.7 %shard_map.150 = (s32[26,128]{1,0:T(8,128)S(1)}, s32[128,128]{1,0:T(8,128)S(1)}, bf16[2048,256]{1,0:T(8,128)(2,1)S(1)}) custom-call(f32[2056,128]{1,0:T(8,128)S(1)} %get-tuple-element.29.table_ref, s32[26,1,128]{2,1,0:T(1,128)} %bitcast.59, s32[26,2,128]{2,1,0:T(2,128)} %bitcast.57, s32[26,128]{1,0:T(8,128)} %bitcast.58), custom_call_target="tpu_custom_call" | custom-call | flops 1024 | bytes 1024 | tf_op jit(solution)/shard_map/pallas_call | solution.py:346
  6.3 9.1 %all_to_all.15 = s32[8,16,128]{2,1,0:T(8,128)S(1)} all-to-all(s32[8,16,128]{2,1,0:T(8,128)S(1)} %bitcast.43), channel_id=1, replica_groups={{0,2,4,6,8,10,12,14},{16,18,20,22,24,26,28,30},{1,3,5,7,9,11,13,15},{17..., dimensions={0} | all-to-all | bytes 131072 | tf_op jit(solution)/shard_map/all_to_all | solution.py:336
  15.4 1.6 %collective-permute-done.refs_0_ = bf16[1024,128]{1,0:T(8,128)(2,1)S(1)} collective-permute-done((bf16[1024,128]{1,0:T(8,128)(2,1)S(1)}, bf16[1024,128]{1,0:T(8,128)(2,1)S(1)}, u32[]{:S(2)}, u32[]{:S(2)}) %collective-permute-start) | collective-permute-done | bytes 262176 | tf_op jit(solution)/shard_map/ppermute | solution.py:333
  17.1 1.5 %collective-permute-done.3.refs_1_ = bf16[1024,128]{1,0:T(8,128)(2,1)S(1)} collective-permute-done((bf16[1024,128]{1,0:T(8,128)(2,1)S(1)}, bf16[1024,128]{1,0:T(8,128)(2,1)S(1)}, u32[]{:S(2)}, u32[]{:S(2)}) %collective-permute-start.3) | collective-permute-done | bytes 262176 | tf_op jit(solution)/shard_map/ppermute | solution.py:329
  18.6 2.4 %shard_map.151 = (bf16[640,128]{1,0:T(8,128)(2,1)S(1)}, bf16[640,128]{1,0:T(8,128)(2,1)S(1)}) custom-call(s32[128,128]{1,0:T(8,128)S(1)} %bitcast.30, s32[128,128]{1,0:T(8,128)S(1)} %bitcast.31, bf16[2048,256]{1,0:T(8,128)(2,1)S(1)} %get-tuple-element.33.table_ref, bf16[1024,128]{1,0:T(8,128)(2,1)S(1)} %collective-permute-done.refs_0_, ...), custom_call_target="tpu_custom_call" | custom-call | flops 1024 | bytes 1024 | tf_op jit(solution)/shard_map/pallas_call | solution.py:380
  21.0 0.3 collective-permute-start.6
  21.3 2.4 %shard_map.153 = (bf16[640,128]{1,0:T(8,128)(2,1)S(1)}, bf16[640,128]{1,0:T(8,128)(2,1)S(1)}) custom-call(s32[128,128]{1,0:T(8,128)S(1)} %bitcast.32, s32[128,128]{1,0:T(8,128)S(1)} %bitcast.33, bf16[2048,256]{1,0:T(8,128)(2,1)S(1)} %get-tuple-element.33.table_ref, bf16[1024,128]{1,0:T(8,128)(2,1)S(1)} %collective-permute-done.refs_0_, ...), custom_call_target="tpu_custom_call" | custom-call | flops 1024 | bytes 1024 | tf_op jit(solution)/shard_map/pallas_call | solution.py:380
  23.7 1.6 %collective-permute-start.5 = (bf16[640,128]{1,0:T(8,128)(2,1)S(1)}, bf16[640,128]{1,0:T(8,128)(2,1)S(1)}, u32[]{:S(2)}, u32[]{:S(2)}) collective-permute-start(bf16[640,128]{1,0:T(8,128)(2,1)S(1)} %get-tuple-element.37), channel_id=1, source_target_pairs={{0,4},{2,6},{4,0},{6,2},{8,12},{10,14},{12,8},{14,10},{16,20},{18,... | collective-permute-start | bytes 491528 | tf_op jit(solution)/shard_map/ppermute | solution.py:371
  25.3 2.6 %collective-permute-start.9 = (bf16[640,128]{1,0:T(8,128)(2,1)S(1)}, bf16[640,128]{1,0:T(8,128)(2,1)S(1)}, u32[]{:S(2)}, u32[]{:S(2)}) collective-permute-start(bf16[640,128]{1,0:T(8,128)(2,1)S(1)} %get-tuple-element.41), channel_id=1, source_target_pairs={{0,10},{2,8},{4,14},{6,12},{8,2},{10,0},{12,6},{14,4},{16,26},{18,... | collective-permute-start | bytes 491528 | tf_op jit(solution)/shard_map/ppermute | solution.py:371
  27.9 2.4 %shard_map.152 = (bf16[640,128]{1,0:T(8,128)(2,1)S(1)}, bf16[640,128]{1,0:T(8,128)(2,1)S(1)}) custom-call(s32[128,128]{1,0:T(8,128)S(1)} %bitcast.34, s32[128,128]{1,0:T(8,128)S(1)} %bitcast.35, bf16[2048,256]{1,0:T(8,128)(2,1)S(1)} %get-tuple-element.33.table_ref, bf16[1024,128]{1,0:T(8,128)(2,1)S(1)} %collective-permute-done.refs_0_, ...), custom_call_target="tpu_custom_call" | custom-call | flops 1024 | bytes 1024 | tf_op jit(solution)/shard_map/pallas_call | solution.py:380
  30.4 1.5 %collective-permute-start.4 = (bf16[640,128]{1,0:T(8,128)(2,1)S(1)}, bf16[640,128]{1,0:T(8,128)(2,1)S(1)}, u32[]{:S(2)}, u32[]{:S(2)}) collective-permute-start(bf16[640,128]{1,0:T(8,128)(2,1)S(1)} %get-tuple-element.36), channel_id=1, source_target_pairs={{0,2},{2,0},{4,6},{6,4},{8,10},{10,8},{12,14},{14,12},{16,18},{18,... | collective-permute-start | bytes 491528 | tf_op jit(solution)/shard_map/ppermute | solution.py:371
  31.9 2.4 %shard_map.154 = (bf16[640,128]{1,0:T(8,128)(2,1)S(1)}, bf16[640,128]{1,0:T(8,128)(2,1)S(1)}) custom-call(bf16[640,128]{1,0:T(8,128)(2,1)S(1)} %collective-permute-done.6.after_ref.refs_7_, s32[128,128]{1,0:T(8,128)S(1)} %bitcast.36, bf16[2048,256]{1,0:T(8,128)(2,1)S(1)} %get-tuple-element.33.table_ref, bf16[1024,128]{1,0:T(8,128)(2,1)S(1)} %collective-permute-done.refs_0_, ...), custom_call_target="tpu_custom_call" | custom-call | flops 1024 | bytes 1024 | tf_op jit(solution)/shard_map/pallas_call | solution.py:380
  34.3 1.6 %collective-permute-start.7 = (bf16[640,128]{1,0:T(8,128)(2,1)S(1)}, bf16[640,128]{1,0:T(8,128)(2,1)S(1)}, u32[]{:S(2)}, u32[]{:S(2)}) collective-permute-start(bf16[640,128]{1,0:T(8,128)(2,1)S(1)} %get-tuple-element.39), channel_id=1, source_target_pairs={{0,6},{2,4},{4,2},{6,0},{8,14},{10,12},{12,10},{14,8},{16,22},{18,... | collective-permute-start | bytes 491528 | tf_op jit(solution)/shard_map/ppermute | solution.py:371
  35.9 1.9 %collective-permute-start.8 = (bf16[640,128]{1,0:T(8,128)(2,1)S(1)}, bf16[640,128]{1,0:T(8,128)(2,1)S(1)}, u32[]{:S(2)}, u32[]{:S(2)}) collective-permute-start(bf16[640,128]{1,0:T(8,128)(2,1)S(1)} %get-tuple-element.40), channel_id=1, source_target_pairs={{0,8},{2,10},{4,12},{6,14},{8,0},{10,2},{12,4},{14,6},{16,24},{18,... | collective-permute-start | bytes 491528 | tf_op jit(solution)/shard_map/ppermute | solution.py:371
  37.8 2.7 %collective-permute-done.7.refs_3_ = bf16[640,128]{1,0:T(8,128)(2,1)S(1)} collective-permute-done((bf16[640,128]{1,0:T(8,128)(2,1)S(1)}, bf16[640,128]{1,0:T(8,128)(2,1)S(1)}, u32[]{:S(2)}, u32[]{:S(2)}) %collective-permute-start.7) | collective-permute-done | bytes 163872 | tf_op jit(solution)/shard_map/ppermute | solution.py:371
  40.6 0.6 collective-permute-done.8.refs_4_
  41.2 11.5 %shard_map.155 = (f32[1,128]{1,0:T(1,128)}, bf16[2560,128]{1,0:T(8,128)(2,1)}, bf16[2560,128]{1,0:T(8,128)(2,1)S(1)}) custom-call(bf16[640,128]{1,0:T(8,128)(2,1)S(1)} %get-tuple-element.35.refs_0_, bf16[640,128]{1,0:T(8,128)(2,1)S(1)} %collective-permute-done.4.refs_1_, bf16[640,128]{1,0:T(8,128)(2,1)S(1)} %collective-permute-done.5.refs_2_, ...), custom_call_target="tpu_custom_call" | custom-call | flops 1024 | bytes 1024 | tf_op jit(solution)/shard_map/pallas_call | solution.py:390
  52.7 12.8 %all_to_all.16 = bf16[8,320,128]{2,1,0:T(8,128)(2,1)S(1)} all-to-all(bf16[8,320,128]{2,1,0:T(8,128)(2,1)S(1)} %bitcast.42), channel_id=1, replica_groups={{0,2,4,6,8,10,12,14},{16,18,20,22,24,26,28,30},{1,3,5,7,9,11,13,15},{17..., dimensions={0} | all-to-all | bytes 1310720 | tf_op jit(solution)/shard_map/all_to_all | solution.py:336
  65.5 5.1 %all-to-all-start.2 = ((bf16[8,320,128]{2,1,0:T(8,128)(2,1)}), bf16[8,320,128]{2,1,0:T(8,128)(2,1)S(1)}, u32[]{:S(2)}, u32[]{:S(2)}) async-start(bf16[8,320,128]{2,1,0:T(8,128)(2,1)} %bitcast.16), calls=%async_computation.2 | async-start | bytes 1310720 | tf_op jit(solution)/shard_map/all_to_all | solution.py:336
  70.8 1.5 %shard_map.156.after_ref = f32[1024,128]{1,0:T(8,128)S(1)} custom-call(s32[128,128]{1,0:T(8,128)S(1)} %bitcast.38, s32[40,128]{1,0:T(8,128)S(1)} %pad_add_fusion.refs_0_, bf16[2560,128]{1,0:T(8,128)(2,1)S(1)} %bitcast.40), custom_call_target="tpu_custom_call" | custom-call | flops 1024 | bytes 1024 | tf_op jit(solution)/shard_map/pallas_call | solution.py:433
  72.6 1.5 %shard_map.157 = f32[1024,128]{1,0:T(8,128)S(1)} custom-call(f32[1024,128]{1,0:T(8,128)S(1)} %shard_map.156.after_ref, s32[40,128]{1,0:T(8,128)S(1)} %pad_add_fusion.refs_0_, bf16[2560,128]{1,0:T(8,128)(2,1)S(1)} %bitcast.41), custom_call_target="tpu_custom_call" | custom-call | flops 1024 | bytes 1024 | tf_op jit(solution)/shard_map/pallas_call | solution.py:433
  74.4 0.5 collective-permute-start.17
  74.9 2.6 %all-to-all-done.2 = bf16[8,320,128]{2,1,0:T(8,128)(2,1)S(1)} async-done(((bf16[8,320,128]{2,1,0:T(8,128)(2,1)}), bf16[8,320,128]{2,1,0:T(8,128)(2,1)S(1)}, u32[]{:S(2)}, u32[]{:S(2)}) %all-to-all-start.2) | async-done | bytes 655392 | tf_op jit(solution)/shard_map/all_to_all | solution.py:336
  77.6 0.5 collective-permute-start.14
  78.2 0.4 collective-permute-start.16
  78.6 0.4 collective-permute-done.13.refs_3_
  79.7 2.9 %shard_map.158 = f32[1024,128]{1,0:T(8,128)S(1)} custom-call(bf16[1024,128]{1,0:T(8,128)(2,1)S(1)} %add_convert_fusion.after_ref, s32[40,128]{1,0:T(8,128)S(1)} %pad_add_fusion.1.refs_0_, s32[40,128]{1,0:T(8,128)S(1)} %collective-permute-done.12.refs_1_, bf16[2560,128]{1,0:T(8,128)(2,1)S(1)} %bitcast.39, ...), custom_call_target="tpu_custom_call" | custom-call | flops 1024 | bytes 1024 | tf_op jit(solution)/shard_map/pallas_call | solution.py:433
  82.7 5.9 %collective-permute-done.17 = bf16[1024,128]{1,0:T(8,128)(2,1)S(1)} collective-permute-done((bf16[1024,128]{1,0:T(8,128)(2,1)S(1)}, bf16[1024,128]{1,0:T(8,128)(2,1)S(1)}, u32[]{:S(2)}, u32[]{:S(2)}) %collective-permute-start.17) | collective-permute-done | bytes 262176 | tf_op jit(solution)/shard_map/ppermute | solution.py:333
  88.6 0.9 convert_add_fusion
  (39 shorter events, 1.8 us)
Async XLA Ops:
  0.6 16.4 %collective-permute-start.1 = (bf16[3456,256]{1,0:T(8,128)(2,1)}, bf16[3456,256]{1,0:T(8,128)(2,1)S(1)}, u32[]{:S(2)}, u32[]{:S(2)}) collective-permute-start(bf16[3456,256]{1,0:T(8,128)(2,1)} %bitcast.45), channel_id=1, source_target_pairs={{0,1},{1,0},{2,3},{3,2},{4,5},{5,4},{6,7},{7,6},{8,9},{9,8},{10,11... | collective-permute-start | bytes 5308424 | tf_op jit(solution)/shard_map/ppermute | solution.py:329
  0.7 16.4 %collective-permute-start.2 = (bf16[256,3456]{1,0:T(8,128)(2,1)}, bf16[256,3456]{1,0:T(8,128)(2,1)S(1)}, u32[]{:S(2)}, u32[]{:S(2)}) collective-permute-start(bf16[256,3456]{1,0:T(8,128)(2,1)} %bitcast.47), channel_id=1, source_target_pairs={{0,1},{1,0},{2,3},{3,2},{4,5},{5,4},{6,7},{7,6},{8,9},{9,8},{10,11... | collective-permute-start | bytes 5308424 | tf_op jit(solution)/shard_map/ppermute | solution.py:329
  3.1 14.0 %collective-permute-start = (bf16[1024,128]{1,0:T(8,128)(2,1)S(1)}, bf16[1024,128]{1,0:T(8,128)(2,1)S(1)}, u32[]{:S(2)}, u32[]{:S(2)}) collective-permute-start(bf16[1024,128]{1,0:T(8,128)(2,1)S(1)} %get-tuple-element.28), channel_id=1, source_target_pairs={{0,24},{2,26},{4,28},{6,30},{8,16},{10,18},{12,20},{14,22},{16,8},... | collective-permute-start | bytes 786440 | tf_op jit(solution)/shard_map/ppermute | solution.py:333
  17.1 1.5 %collective-permute-start.3 = (bf16[1024,128]{1,0:T(8,128)(2,1)S(1)}, bf16[1024,128]{1,0:T(8,128)(2,1)S(1)}, u32[]{:S(2)}, u32[]{:S(2)}) collective-permute-start(bf16[1024,128]{1,0:T(8,128)(2,1)S(1)} %collective-permute-done.refs_0_), channel_id=1, source_target_pairs={{0,1},{1,0},{2,3},{3,2},{4,5},{5,4},{6,7},{7,6},{8,9},{9,8},{10,11... | collective-permute-start | bytes 786440 | tf_op jit(solution)/shard_map/ppermute | solution.py:329
  21.0 10.9 %collective-permute-start.6 = (bf16[640,128]{1,0:T(8,128)(2,1)S(1)}, bf16[640,128]{1,0:T(8,128)(2,1)S(1)}, u32[]{:S(2)}, u32[]{:S(2)}) collective-permute-start(bf16[640,128]{1,0:T(8,128)(2,1)S(1)} %get-tuple-element.38), channel_id=1, source_target_pairs={{0,14},{2,12},{4,10},{6,8},{8,6},{10,4},{12,2},{14,0},{16,30},{18,... | collective-permute-start | bytes 491528 | tf_op jit(solution)/shard_map/ppermute | solution.py:371
  23.7 14.1 %copy-start.3 = (f32[3456]{0:T(1024)S(1)}, f32[3456]{0:T(1024)}, u32[]{:S(2)}) copy-start(f32[3456]{0:T(1024)} %param.27) | copy-start | bytes 41476
  23.7 12.2 %collective-permute-start.5 = (bf16[640,128]{1,0:T(8,128)(2,1)S(1)}, bf16[640,128]{1,0:T(8,128)(2,1)S(1)}, u32[]{:S(2)}, u32[]{:S(2)}) collective-permute-start(bf16[640,128]{1,0:T(8,128)(2,1)S(1)} %get-tuple-element.37), channel_id=1, source_target_pairs={{0,4},{2,6},{4,0},{6,2},{8,12},{10,14},{12,8},{14,10},{16,20},{18,... | collective-permute-start | bytes 491528 | tf_op jit(solution)/shard_map/ppermute | solution.py:371
  25.3 15.9 %copy-start = (bf16[128,128]{1,0:T(8,128)(2,1)S(1)}, bf16[128,128]{1,0:T(8,128)(2,1)}, u32[]{:S(2)}) copy-start(bf16[128,128]{1,0:T(8,128)(2,1)} %refs_9_.1) | copy-start | bytes 98308
  25.3 15.9 %copy-start.1 = (f32[1,3456]{1,0:T(1,128)S(1)}, f32[1,3456]{1,0:T(1,128)}, u32[]{:S(2)}) copy-start(f32[1,3456]{1,0:T(1,128)} %refs_15_.1) | copy-start | bytes 41476
  25.3 15.9 %copy-start.2 = (s32[128]{0:T(128)S(1)}, s32[128]{0:T(128)}, u32[]{:S(2)}) copy-start(s32[128]{0:T(128)} %param.23) | copy-start | bytes 1540
  25.3 12.5 %collective-permute-start.9 = (bf16[640,128]{1,0:T(8,128)(2,1)S(1)}, bf16[640,128]{1,0:T(8,128)(2,1)S(1)}, u32[]{:S(2)}, u32[]{:S(2)}) collective-permute-start(bf16[640,128]{1,0:T(8,128)(2,1)S(1)} %get-tuple-element.41), channel_id=1, source_target_pairs={{0,10},{2,8},{4,14},{6,12},{8,2},{10,0},{12,6},{14,4},{16,26},{18,... | collective-permute-start | bytes 491528 | tf_op jit(solution)/shard_map/ppermute | solution.py:371
  30.3 7.5 %collective-permute-start.10 = (bf16[640,128]{1,0:T(8,128)(2,1)S(1)}, bf16[640,128]{1,0:T(8,128)(2,1)S(1)}, u32[]{:S(2)}, u32[]{:S(2)}) collective-permute-start(bf16[640,128]{1,0:T(8,128)(2,1)S(1)} %get-tuple-element.42), channel_id=1, source_target_pairs={{0,12},{2,14},{4,8},{6,10},{8,4},{10,6},{12,0},{14,2},{16,28},{18,... | collective-permute-start | bytes 491528 | tf_op jit(solution)/shard_map/ppermute | solution.py:371
  30.4 7.4 %collective-permute-start.4 = (bf16[640,128]{1,0:T(8,128)(2,1)S(1)}, bf16[640,128]{1,0:T(8,128)(2,1)S(1)}, u32[]{:S(2)}, u32[]{:S(2)}) collective-permute-start(bf16[640,128]{1,0:T(8,128)(2,1)S(1)} %get-tuple-element.36), channel_id=1, source_target_pairs={{0,2},{2,0},{4,6},{6,4},{8,10},{10,8},{12,14},{14,12},{16,18},{18,... | collective-permute-start | bytes 491528 | tf_op jit(solution)/shard_map/ppermute | solution.py:371
  34.3 6.3 %collective-permute-start.7 = (bf16[640,128]{1,0:T(8,128)(2,1)S(1)}, bf16[640,128]{1,0:T(8,128)(2,1)S(1)}, u32[]{:S(2)}, u32[]{:S(2)}) collective-permute-start(bf16[640,128]{1,0:T(8,128)(2,1)S(1)} %get-tuple-element.39), channel_id=1, source_target_pairs={{0,6},{2,4},{4,2},{6,0},{8,14},{10,12},{12,10},{14,8},{16,22},{18,... | collective-permute-start | bytes 491528 | tf_op jit(solution)/shard_map/ppermute | solution.py:371
  35.9 5.3 %collective-permute-start.8 = (bf16[640,128]{1,0:T(8,128)(2,1)S(1)}, bf16[640,128]{1,0:T(8,128)(2,1)S(1)}, u32[]{:S(2)}, u32[]{:S(2)}) collective-permute-start(bf16[640,128]{1,0:T(8,128)(2,1)S(1)} %get-tuple-element.40), channel_id=1, source_target_pairs={{0,8},{2,10},{4,12},{6,14},{8,0},{10,2},{12,4},{14,6},{16,24},{18,... | collective-permute-start | bytes 491528 | tf_op jit(solution)/shard_map/ppermute | solution.py:371
  65.5 12.0 %all-to-all-start.2 = ((bf16[8,320,128]{2,1,0:T(8,128)(2,1)}), bf16[8,320,128]{2,1,0:T(8,128)(2,1)S(1)}, u32[]{:S(2)}, u32[]{:S(2)}) async-start(bf16[8,320,128]{2,1,0:T(8,128)(2,1)} %bitcast.16), calls=%async_computation.2 | async-start | bytes 1310720 | tf_op jit(solution)/shard_map/all_to_all | solution.py:336
  72.3 2.0 %collective-permute-start.11 = (f32[1024,128]{1,0:T(8,128)S(1)}, f32[1024,128]{1,0:T(8,128)S(1)}, u32[]{:S(2)}, u32[]{:S(2)}) collective-permute-start(f32[1024,128]{1,0:T(8,128)S(1)} %shard_map.156.after_ref), channel_id=1, source_target_pairs={{0,1},{1,0},{2,3},{3,2},{4,5},{5,4},{6,7},{7,6},{8,9},{9,8},{10,11... | collective-permute-start | bytes 1572872 | tf_op jit(solution)/shard_map/ppermute | solution.py:329
  74.4 14.2 %collective-permute-start.17 = (bf16[1024,128]{1,0:T(8,128)(2,1)S(1)}, bf16[1024,128]{1,0:T(8,128)(2,1)S(1)}, u32[]{:S(2)}, u32[]{:S(2)}) collective-permute-start(bf16[1024,128]{1,0:T(8,128)(2,1)S(1)} %add_convert_fusion.after_ref), channel_id=1, source_target_pairs={{0,24},{2,26},{4,28},{6,30},{8,16},{10,18},{12,20},{14,22},{16,8},... | collective-permute-start | bytes 786440 | tf_op jit(solution)/shard_map/ppermute | solution.py:333
  74.8 3.3 %collective-permute-start.12 = (s32[40,128]{1,0:T(8,128)S(1)}, s32[40,128]{1,0:T(8,128)S(1)}, u32[]{:S(2)}, u32[]{:S(2)}) collective-permute-start(s32[40,128]{1,0:T(8,128)S(1)} %pad_add_fusion.1.refs_0_), channel_id=1, source_target_pairs={{0,1},{1,0},{2,3},{3,2},{4,5},{5,4},{6,7},{7,6},{8,9},{9,8},{10,11... | collective-permute-start | bytes 61448 | tf_op jit(solution)/shard_map/ppermute | solution.py:329
  77.5 1.5 %collective-permute-start.13 = (bf16[640,128]{1,0:T(8,128)(2,1)S(1)}, bf16[640,128]{1,0:T(8,128)(2,1)S(1)}, u32[]{:S(2)}, u32[]{:S(2)}) collective-permute-start(bf16[640,128]{1,0:T(8,128)(2,1)S(1)} %bitcast.52), channel_id=1, source_target_pairs={{0,1},{1,0},{2,3},{3,2},{4,5},{5,4},{6,7},{7,6},{8,9},{9,8},{10,11... | collective-permute-start | bytes 491528 | tf_op jit(solution)/shard_map/ppermute | solution.py:329
  77.6 1.6 %collective-permute-start.14 = (bf16[640,128]{1,0:T(8,128)(2,1)S(1)}, bf16[640,128]{1,0:T(8,128)(2,1)S(1)}, u32[]{:S(2)}, u32[]{:S(2)}) collective-permute-start(bf16[640,128]{1,0:T(8,128)(2,1)S(1)} %bitcast.51), channel_id=1, source_target_pairs={{0,1},{1,0},{2,3},{3,2},{4,5},{5,4},{6,7},{7,6},{8,9},{9,8},{10,11... | collective-permute-start | bytes 491528 | tf_op jit(solution)/shard_map/ppermute | solution.py:329
  78.1 1.4 %collective-permute-start.15 = (bf16[640,128]{1,0:T(8,128)(2,1)S(1)}, bf16[640,128]{1,0:T(8,128)(2,1)S(1)}, u32[]{:S(2)}, u32[]{:S(2)}) collective-permute-start(bf16[640,128]{1,0:T(8,128)(2,1)S(1)} %bitcast.50), channel_id=1, source_target_pairs={{0,1},{1,0},{2,3},{3,2},{4,5},{5,4},{6,7},{7,6},{8,9},{9,8},{10,11... | collective-permute-start | bytes 491528 | tf_op jit(solution)/shard_map/ppermute | solution.py:329
  78.2 1.5 %collective-permute-start.16 = (bf16[640,128]{1,0:T(8,128)(2,1)S(1)}, bf16[640,128]{1,0:T(8,128)(2,1)S(1)}, u32[]{:S(2)}, u32[]{:S(2)}) collective-permute-start(bf16[640,128]{1,0:T(8,128)(2,1)S(1)} %bitcast.49), channel_id=1, source_target_pairs={{0,1},{1,0},{2,3},{3,2},{4,5},{5,4},{6,7},{7,6},{8,9},{9,8},{10,11... | collective-permute-start | bytes 491528 | tf_op jit(solution)/shard_map/ppermute | solution.py:329

commit v7 on v6

--- a/solution.py
+++ b/solution.py
@@ -414,10 +414,7 @@
     )
     ids = asked.reshape(half, 2, per, LANES)
     got_mirror = exchange(to_mirror.reshape(half, cap, width)).reshape(half * cap, width)
-    got_mirror, to_native = lax.optimization_barrier((got_mirror, to_native))
-    got_native = exchange(to_native.reshape(half, cap, width)).reshape(half * cap, width)
-    whole_native = got_native
-    got_mirror, got_native = in_vmem(got_mirror), in_vmem(got_native)
+    got_mirror = in_vmem(got_mirror)
 
     def lines_of(kind):
         return jnp.concatenate(
@@ -442,6 +439,9 @@
     for by in range(1, replicas):
         last = scatter(by, last, [mirror_lines], [got_mirror])
         parts.append(shift(last, by))
+    last, to_native = lax.optimization_barrier((last, to_native))
+    whole_native = exchange(to_native.reshape(half, cap, width)).reshape(half * cap, width)
+    got_native = in_vmem(whole_native)
     own = scatter(0, last, [mirror_lines], [got_mirror])
     mirrored = functools.reduce(jnp.add, [own] + parts).astype(BF16)
     returned = across(mirrored)

time: 89.8 us -> 90 us (level)
  the two profiles are of different devices: /device:TPU:18 before, /device:TPU:0 now
where the time goes in v7:
time: 90 us; the launch traced here: 89.6 us
  Pallas kernels  31.8 us (35%)
  starting transfers between devices  27 us (30%)
  waiting for transfers between devices  19.2 us (21%)
  blocking collectives  9.35 us (10%)
  other arithmetic  0.95 us (1%)
    pallas_call x1, Pallas kernels, body(): call(functools.partial(dense_kernel, replicas, half, cap), (shape((1, sam...  11.8 us
    all_to_all x2, waiting for transfers between devices, exchange(): lax.all_to_all(x, 'table', split_axis=0, concat_axis=0, axis_index_groups...  10.6 us
    ppermute x7, starting transfers between devices, meet(): return lax.ppermute(x, 'table', [(i, i ^ partner) for i in range(peers)])  9.6 us
    pallas_call x4, Pallas kernels, body(): call(functools.partial(lookup_kernel, half, cap, partners, replicas), tup...  9.5 us
    all_to_all x1, blocking collectives, exchange(): lax.all_to_all(x, 'table', split_axis=0, concat_axis=0, axis_index_groups...  9.35 us
    ppermute x2, starting transfers between devices, across(): return lax.ppermute(x, 'table', [(i, i ^ far) for i in range(peers)])  8.52 us
    all_to_all x2, starting transfers between devices, exchange(): lax.all_to_all(x, 'table', split_axis=0, concat_axis=0, axis_index_groups...  7.1 us
    pallas_call x3, Pallas kernels, scatter(): call(functools.partial(scatter_kernel, by, len(lines)), shape((own_rows,...  5.97 us
  transfers between devices with their start and end apart: 20, of which 11 were waited for; matrix products, arithmetic and copies ran while one was open for 1% of the time, Pallas kernels for 18%

profile of v7, /device:TPU:0, one launch (start us, length us, event | category | flops | bytes accessed | tf_op | source)
XLA Modules:
  0.0 89.6 jit_solution(4398922761006811797)
XLA Ops:
  0.6 0.5 collective-permute-start.1
  1.2 1.9 %shard_map.149 = (f32[2056,128]{1,0:T(8,128)S(1)}, bf16[1024,128]{1,0:T(8,128)(2,1)S(1)}) custom-call(s32[256]{0:T(256)} %local_ref.1, s32[256]{0:T(256)} %new_ref.1, s32[2048]{0:T(1024)} %versions_ref.1, f32[2048,128]{1,0:T(8,128)} %table_ref.1, f32[256,128]{1,0:T(8,128)} %values_ref.1), custom_call_target="tpu_custom_call" | custom-call | flops 1024 | bytes 1024 | tf_op jit(solution)/shard_map/pallas_call | solution.py:341
  3.1 5.1 %collective-permute-start = (bf16[1024,128]{1,0:T(8,128)(2,1)S(1)}, bf16[1024,128]{1,0:T(8,128)(2,1)S(1)}, u32[]{:S(2)}, u32[]{:S(2)}) collective-permute-start(bf16[1024,128]{1,0:T(8,128)(2,1)S(1)} %get-tuple-element.28), channel_id=1, source_target_pairs={{0,24},{2,26},{4,28},{6,30},{8,16},{10,18},{12,20},{14,22},{16,8},... | collective-permute-start | bytes 786440 | tf_op jit(solution)/shard_map/ppermute | solution.py:333
  8.2 2.7 %shard_map.150 = (s32[26,128]{1,0:T(8,128)S(1)}, s32[128,128]{1,0:T(8,128)S(1)}, bf16[2048,256]{1,0:T(8,128)(2,1)S(1)}) custom-call(f32[2056,128]{1,0:T(8,128)S(1)} %get-tuple-element.29.table_ref, s32[26,1,128]{2,1,0:T(1,128)} %bitcast.58, s32[26,2,128]{2,1,0:T(2,128)} %bitcast.56, s32[26,128]{1,0:T(8,128)} %bitcast.57), custom_call_target="tpu_custom_call" | custom-call | flops 1024 | bytes 1024 | tf_op jit(solution)/shard_map/pallas_call | solution.py:346
  10.9 9.3 %all_to_all.15 = s32[8,16,128]{2,1,0:T(8,128)S(1)} all-to-all(s32[8,16,128]{2,1,0:T(8,128)S(1)} %bitcast.42), channel_id=1, replica_groups={{0,2,4,6,8,10,12,14},{16,18,20,22,24,26,28,30},{1,3,5,7,9,11,13,15},{17..., dimensions={0} | all-to-all | bytes 131072 | tf_op jit(solution)/shard_map/all_to_all | solution.py:336
  20.3 1.5 %collective-permute-done.3.refs_1_ = bf16[1024,128]{1,0:T(8,128)(2,1)S(1)} collective-permute-done((bf16[1024,128]{1,0:T(8,128)(2,1)S(1)}, bf16[1024,128]{1,0:T(8,128)(2,1)S(1)}, u32[]{:S(2)}, u32[]{:S(2)}) %collective-permute-start.3) | collective-permute-done | bytes 262176 | tf_op jit(solution)/shard_map/ppermute | solution.py:329
  21.8 2.4 %shard_map.151 = (bf16[640,128]{1,0:T(8,128)(2,1)S(1)}, bf16[640,128]{1,0:T(8,128)(2,1)S(1)}) custom-call(s32[128,128]{1,0:T(8,128)S(1)} %bitcast.30, s32[128,128]{1,0:T(8,128)S(1)} %bitcast.31, bf16[2048,256]{1,0:T(8,128)(2,1)S(1)} %get-tuple-element.33.table_ref, bf16[1024,128]{1,0:T(8,128)(2,1)S(1)} %collective-permute-done.refs_0_, ...), custom_call_target="tpu_custom_call" | custom-call | flops 1024 | bytes 1024 | tf_op jit(solution)/shard_map/pallas_call | solution.py:380
  24.2 1.8 %collective-permute-start.6 = (bf16[640,128]{1,0:T(8,128)(2,1)S(1)}, bf16[640,128]{1,0:T(8,128)(2,1)S(1)}, u32[]{:S(2)}, u32[]{:S(2)}) collective-permute-start(bf16[640,128]{1,0:T(8,128)(2,1)S(1)} %get-tuple-element.38), channel_id=1, source_target_pairs={{0,14},{2,12},{4,10},{6,8},{8,6},{10,4},{12,2},{14,0},{16,30},{18,... | collective-permute-start | bytes 491528 | tf_op jit(solution)/shard_map/ppermute | solution.py:371
  26.0 2.4 %shard_map.153 = (bf16[640,128]{1,0:T(8,128)(2,1)S(1)}, bf16[640,128]{1,0:T(8,128)(2,1)S(1)}) custom-call(s32[128,128]{1,0:T(8,128)S(1)} %bitcast.32, s32[128,128]{1,0:T(8,128)S(1)} %bitcast.33, bf16[2048,256]{1,0:T(8,128)(2,1)S(1)} %get-tuple-element.33.table_ref, bf16[1024,128]{1,0:T(8,128)(2,1)S(1)} %collective-permute-done.refs_0_, ...), custom_call_target="tpu_custom_call" | custom-call | flops 1024 | bytes 1024 | tf_op jit(solution)/shard_map/pallas_call | solution.py:380
  28.4 0.6 collective-permute-start.5
  28.9 2.2 %collective-permute-start.9 = (bf16[640,128]{1,0:T(8,128)(2,1)S(1)}, bf16[640,128]{1,0:T(8,128)(2,1)S(1)}, u32[]{:S(2)}, u32[]{:S(2)}) collective-permute-start(bf16[640,128]{1,0:T(8,128)(2,1)S(1)} %get-tuple-element.41), channel_id=1, source_target_pairs={{0,10},{2,8},{4,14},{6,12},{8,2},{10,0},{12,6},{14,4},{16,26},{18,... | collective-permute-start | bytes 491528 | tf_op jit(solution)/shard_map/ppermute | solution.py:371
  31.1 2.4 %shard_map.152 = (bf16[640,128]{1,0:T(8,128)(2,1)S(1)}, bf16[640,128]{1,0:T(8,128)(2,1)S(1)}) custom-call(s32[128,128]{1,0:T(8,128)S(1)} %bitcast.34, s32[128,128]{1,0:T(8,128)S(1)} %bitcast.35, bf16[2048,256]{1,0:T(8,128)(2,1)S(1)} %get-tuple-element.33.table_ref, bf16[1024,128]{1,0:T(8,128)(2,1)S(1)} %collective-permute-done.refs_0_, ...), custom_call_target="tpu_custom_call" | custom-call | flops 1024 | bytes 1024 | tf_op jit(solution)/shard_map/pallas_call | solution.py:380
  33.5 0.8 collective-permute-start.10
  34.3 1.5 %collective-permute-start.4 = (bf16[640,128]{1,0:T(8,128)(2,1)S(1)}, bf16[640,128]{1,0:T(8,128)(2,1)S(1)}, u32[]{:S(2)}, u32[]{:S(2)}) collective-permute-start(bf16[640,128]{1,0:T(8,128)(2,1)S(1)} %get-tuple-element.36), channel_id=1, source_target_pairs={{0,2},{2,0},{4,6},{6,4},{8,10},{10,8},{12,14},{14,12},{16,18},{18,... | collective-permute-start | bytes 491528 | tf_op jit(solution)/shard_map/ppermute | solution.py:371
  35.8 2.4 %shard_map.154 = (bf16[640,128]{1,0:T(8,128)(2,1)S(1)}, bf16[640,128]{1,0:T(8,128)(2,1)S(1)}) custom-call(bf16[640,128]{1,0:T(8,128)(2,1)S(1)} %collective-permute-done.6.after_ref.refs_7_, s32[128,128]{1,0:T(8,128)S(1)} %bitcast.36, bf16[2048,256]{1,0:T(8,128)(2,1)S(1)} %get-tuple-element.33.table_ref, bf16[1024,128]{1,0:T(8,128)(2,1)S(1)} %collective-permute-done.refs_0_, ...), custom_call_target="tpu_custom_call" | custom-call | flops 1024 | bytes 1024 | tf_op jit(solution)/shard_map/pallas_call | solution.py:380
  38.2 1.4 %collective-permute-start.7 = (bf16[640,128]{1,0:T(8,128)(2,1)S(1)}, bf16[640,128]{1,0:T(8,128)(2,1)S(1)}, u32[]{:S(2)}, u32[]{:S(2)}) collective-permute-start(bf16[640,128]{1,0:T(8,128)(2,1)S(1)} %get-tuple-element.39), channel_id=1, source_target_pairs={{0,6},{2,4},{4,2},{6,0},{8,14},{10,12},{12,10},{14,8},{16,22},{18,... | collective-permute-start | bytes 491528 | tf_op jit(solution)/shard_map/ppermute | solution.py:371
  39.6 1.4 %collective-permute-start.8 = (bf16[640,128]{1,0:T(8,128)(2,1)S(1)}, bf16[640,128]{1,0:T(8,128)(2,1)S(1)}, u32[]{:S(2)}, u32[]{:S(2)}) collective-permute-start(bf16[640,128]{1,0:T(8,128)(2,1)S(1)} %get-tuple-element.40), channel_id=1, source_target_pairs={{0,8},{2,10},{4,12},{6,14},{8,0},{10,2},{12,4},{14,6},{16,24},{18,... | collective-permute-start | bytes 491528 | tf_op jit(solution)/shard_map/ppermute | solution.py:371
  41.0 3.5 %collective-permute-done.7.refs_3_ = bf16[640,128]{1,0:T(8,128)(2,1)S(1)} collective-permute-done((bf16[640,128]{1,0:T(8,128)(2,1)S(1)}, bf16[640,128]{1,0:T(8,128)(2,1)S(1)}, u32[]{:S(2)}, u32[]{:S(2)}) %collective-permute-start.7) | collective-permute-done | bytes 163872 | tf_op jit(solution)/shard_map/ppermute | solution.py:371
  44.5 0.4 collective-permute-done.8.refs_4_
  44.9 11.8 %shard_map.155 = (f32[1,128]{1,0:T(1,128)}, bf16[2560,128]{1,0:T(8,128)(2,1)}, bf16[2560,128]{1,0:T(8,128)(2,1)}) custom-call(bf16[640,128]{1,0:T(8,128)(2,1)S(1)} %get-tuple-element.35.refs_0_, bf16[640,128]{1,0:T(8,128)(2,1)S(1)} %collective-permute-done.4.refs_1_, bf16[640,128]{1,0:T(8,128)(2,1)S(1)} %collective-permute-done.5.refs_2_, ...), custom_call_target="tpu_custom_call" | custom-call | flops 1024 | bytes 1024 | tf_op jit(solution)/shard_map/pallas_call | solution.py:390
  56.7 3.6 %all-to-all-start.1 = ((bf16[8,320,128]{2,1,0:T(8,128)(2,1)}), bf16[8,320,128]{2,1,0:T(8,128)(2,1)S(1)}, u32[]{:S(2)}, u32[]{:S(2)}) async-start(bf16[8,320,128]{2,1,0:T(8,128)(2,1)} %bitcast.12), calls=%async_computation.1 | async-start | bytes 1310720 | tf_op jit(solution)/shard_map/all_to_all | solution.py:336
  60.4 7.9 %all-to-all-done.1 = bf16[8,320,128]{2,1,0:T(8,128)(2,1)S(1)} async-done(((bf16[8,320,128]{2,1,0:T(8,128)(2,1)}), bf16[8,320,128]{2,1,0:T(8,128)(2,1)S(1)}, u32[]{:S(2)}, u32[]{:S(2)}) %all-to-all-start.1) | async-done | bytes 655392 | tf_op jit(solution)/shard_map/all_to_all | solution.py:336
  68.4 1.5 %shard_map.156.after_ref = f32[1024,128]{1,0:T(8,128)S(1)} custom-call(s32[128,128]{1,0:T(8,128)S(1)} %bitcast.38, s32[40,128]{1,0:T(8,128)S(1)} %pad_add_fusion.refs_0_, bf16[2560,128]{1,0:T(8,128)(2,1)S(1)} %bitcast.40), custom_call_target="tpu_custom_call" | custom-call | flops 1024 | bytes 1024 | tf_op jit(solution)/shard_map/pallas_call | solution.py:430
  69.9 3.6 %all-to-all-start.2 = ((bf16[8,320,128]{2,1,0:T(8,128)(2,1)}), bf16[8,320,128]{2,1,0:T(8,128)(2,1)S(1)}, u32[]{:S(2)}, u32[]{:S(2)}) async-start(bf16[8,320,128]{2,1,0:T(8,128)(2,1)} %bitcast.16), calls=%async_computation.2 | async-start | bytes 1310720 | tf_op jit(solution)/shard_map/all_to_all | solution.py:336
  73.7 1.5 %shard_map.157 = f32[1024,128]{1,0:T(8,128)S(1)} custom-call(f32[1024,128]{1,0:T(8,128)S(1)} %shard_map.156.after_ref, s32[40,128]{1,0:T(8,128)S(1)} %pad_add_fusion.refs_0_, bf16[2560,128]{1,0:T(8,128)(2,1)S(1)} %bitcast.41), custom_call_target="tpu_custom_call" | custom-call | flops 1024 | bytes 1024 | tf_op jit(solution)/shard_map/pallas_call | solution.py:430
  75.5 3.4 %collective-permute-start.17 = (bf16[1024,128]{1,0:T(8,128)(2,1)S(1)}, bf16[1024,128]{1,0:T(8,128)(2,1)S(1)}, u32[]{:S(2)}, u32[]{:S(2)}) collective-permute-start(bf16[1024,128]{1,0:T(8,128)(2,1)S(1)} %add_convert_fusion.after_ref), channel_id=1, source_target_pairs={{0,24},{2,26},{4,28},{6,30},{8,16},{10,18},{12,20},{14,22},{16,8},... | collective-permute-start | bytes 786440 | tf_op jit(solution)/shard_map/ppermute | solution.py:333
  79.0 2.6 %all-to-all-done.2 = bf16[8,320,128]{2,1,0:T(8,128)(2,1)S(1)} async-done(((bf16[8,320,128]{2,1,0:T(8,128)(2,1)}), bf16[8,320,128]{2,1,0:T(8,128)(2,1)S(1)}, u32[]{:S(2)}, u32[]{:S(2)}) %all-to-all-start.2) | async-done | bytes 655392 | tf_op jit(solution)/shard_map/all_to_all | solution.py:336
  81.7 0.5 collective-permute-start.14
  82.3 0.4 collective-permute-start.16
  83.9 2.9 %shard_map.158 = f32[1024,128]{1,0:T(8,128)S(1)} custom-call(bf16[1024,128]{1,0:T(8,128)(2,1)S(1)} %add_convert_fusion.after_ref, s32[40,128]{1,0:T(8,128)S(1)} %pad_add_fusion.1.refs_0_, s32[40,128]{1,0:T(8,128)S(1)} %collective-permute-done.12.refs_1_, bf16[2560,128]{1,0:T(8,128)(2,1)S(1)} %bitcast.39, ...), custom_call_target="tpu_custom_call" | custom-call | flops 1024 | bytes 1024 | tf_op jit(solution)/shard_map/pallas_call | solution.py:430
  86.8 1.9 %collective-permute-done.17 = bf16[1024,128]{1,0:T(8,128)(2,1)S(1)} collective-permute-done((bf16[1024,128]{1,0:T(8,128)(2,1)S(1)}, bf16[1024,128]{1,0:T(8,128)(2,1)S(1)}, u32[]{:S(2)}, u32[]{:S(2)}) %collective-permute-start.17) | collective-permute-done | bytes 262176 | tf_op jit(solution)/shard_map/ppermute | solution.py:333
  88.7 0.9 convert_add_fusion
  (40 shorter events, 2.1 us)
Async XLA Ops:
  0.6 19.6 %collective-permute-start.1 = (bf16[3456,256]{1,0:T(8,128)(2,1)}, bf16[3456,256]{1,0:T(8,128)(2,1)S(1)}, u32[]{:S(2)}, u32[]{:S(2)}) collective-permute-start(bf16[3456,256]{1,0:T(8,128)(2,1)} %bitcast.44), channel_id=1, source_target_pairs={{0,1},{1,0},{2,3},{3,2},{4,5},{5,4},{6,7},{7,6},{8,9},{9,8},{10,11... | collective-permute-start | bytes 5308424 | tf_op jit(solution)/shard_map/ppermute | solution.py:329
  1.1 19.1 %collective-permute-start.2 = (bf16[256,3456]{1,0:T(8,128)(2,1)}, bf16[256,3456]{1,0:T(8,128)(2,1)S(1)}, u32[]{:S(2)}, u32[]{:S(2)}) collective-permute-start(bf16[256,3456]{1,0:T(8,128)(2,1)} %bitcast.46), channel_id=1, source_target_pairs={{0,1},{1,0},{2,3},{3,2},{4,5},{5,4},{6,7},{7,6},{8,9},{9,8},{10,11... | collective-permute-start | bytes 5308424 | tf_op jit(solution)/shard_map/ppermute | solution.py:329
  3.1 17.2 %collective-permute-start = (bf16[1024,128]{1,0:T(8,128)(2,1)S(1)}, bf16[1024,128]{1,0:T(8,128)(2,1)S(1)}, u32[]{:S(2)}, u32[]{:S(2)}) collective-permute-start(bf16[1024,128]{1,0:T(8,128)(2,1)S(1)} %get-tuple-element.28), channel_id=1, source_target_pairs={{0,24},{2,26},{4,28},{6,30},{8,16},{10,18},{12,20},{14,22},{16,8},... | collective-permute-start | bytes 786440 | tf_op jit(solution)/shard_map/ppermute | solution.py:333
  20.3 1.5 %collective-permute-start.3 = (bf16[1024,128]{1,0:T(8,128)(2,1)S(1)}, bf16[1024,128]{1,0:T(8,128)(2,1)S(1)}, u32[]{:S(2)}, u32[]{:S(2)}) collective-permute-start(bf16[1024,128]{1,0:T(8,128)(2,1)S(1)} %collective-permute-done.refs_0_), channel_id=1, source_target_pairs={{0,1},{1,0},{2,3},{3,2},{4,5},{5,4},{6,7},{7,6},{8,9},{9,8},{10,11... | collective-permute-start | bytes 786440 | tf_op jit(solution)/shard_map/ppermute | solution.py:329
  24.2 11.6 %collective-permute-start.6 = (bf16[640,128]{1,0:T(8,128)(2,1)S(1)}, bf16[640,128]{1,0:T(8,128)(2,1)S(1)}, u32[]{:S(2)}, u32[]{:S(2)}) collective-permute-start(bf16[640,128]{1,0:T(8,128)(2,1)S(1)} %get-tuple-element.38), channel_id=1, source_target_pairs={{0,14},{2,12},{4,10},{6,8},{8,6},{10,4},{12,2},{14,0},{16,30},{18,... | collective-permute-start | bytes 491528 | tf_op jit(solution)/shard_map/ppermute | solution.py:371
  28.3 12.6 %copy-start.3 = (f32[3456]{0:T(1024)S(1)}, f32[3456]{0:T(1024)}, u32[]{:S(2)}) copy-start(f32[3456]{0:T(1024)} %param.27) | copy-start | bytes 41476
  28.4 11.2 %collective-permute-start.5 = (bf16[640,128]{1,0:T(8,128)(2,1)S(1)}, bf16[640,128]{1,0:T(8,128)(2,1)S(1)}, u32[]{:S(2)}, u32[]{:S(2)}) collective-permute-start(bf16[640,128]{1,0:T(8,128)(2,1)S(1)} %get-tuple-element.37), channel_id=1, source_target_pairs={{0,4},{2,6},{4,0},{6,2},{8,12},{10,14},{12,8},{14,10},{16,20},{18,... | collective-permute-start | bytes 491528 | tf_op jit(solution)/shard_map/ppermute | solution.py:371
  28.9 16.0 %copy-start = (bf16[128,128]{1,0:T(8,128)(2,1)S(1)}, bf16[128,128]{1,0:T(8,128)(2,1)}, u32[]{:S(2)}) copy-start(bf16[128,128]{1,0:T(8,128)(2,1)} %refs_9_.1) | copy-start | bytes 98308
  28.9 16.0 %copy-start.1 = (f32[1,3456]{1,0:T(1,128)S(1)}, f32[1,3456]{1,0:T(1,128)}, u32[]{:S(2)}) copy-start(f32[1,3456]{1,0:T(1,128)} %refs_15_.1) | copy-start | bytes 41476
  28.9 16.0 %copy-start.2 = (s32[128]{0:T(128)S(1)}, s32[128]{0:T(128)}, u32[]{:S(2)}) copy-start(s32[128]{0:T(128)} %param.23) | copy-start | bytes 1540
  28.9 12.1 %collective-permute-start.9 = (bf16[640,128]{1,0:T(8,128)(2,1)S(1)}, bf16[640,128]{1,0:T(8,128)(2,1)S(1)}, u32[]{:S(2)}, u32[]{:S(2)}) collective-permute-start(bf16[640,128]{1,0:T(8,128)(2,1)S(1)} %get-tuple-element.41), channel_id=1, source_target_pairs={{0,10},{2,8},{4,14},{6,12},{8,2},{10,0},{12,6},{14,4},{16,26},{18,... | collective-permute-start | bytes 491528 | tf_op jit(solution)/shard_map/ppermute | solution.py:371
  33.5 7.5 %collective-permute-start.10 = (bf16[640,128]{1,0:T(8,128)(2,1)S(1)}, bf16[640,128]{1,0:T(8,128)(2,1)S(1)}, u32[]{:S(2)}, u32[]{:S(2)}) collective-permute-start(bf16[640,128]{1,0:T(8,128)(2,1)S(1)} %get-tuple-element.42), channel_id=1, source_target_pairs={{0,12},{2,14},{4,8},{6,10},{8,4},{10,6},{12,0},{14,2},{16,28},{18,... | collective-permute-start | bytes 491528 | tf_op jit(solution)/shard_map/ppermute | solution.py:371
  34.3 6.7 %collective-permute-start.4 = (bf16[640,128]{1,0:T(8,128)(2,1)S(1)}, bf16[640,128]{1,0:T(8,128)(2,1)S(1)}, u32[]{:S(2)}, u32[]{:S(2)}) collective-permute-start(bf16[640,128]{1,0:T(8,128)(2,1)S(1)} %get-tuple-element.36), channel_id=1, source_target_pairs={{0,2},{2,0},{4,6},{6,4},{8,10},{10,8},{12,14},{14,12},{16,18},{18,... | collective-permute-start | bytes 491528 | tf_op jit(solution)/shard_map/ppermute | solution.py:371
  38.2 6.3 %collective-permute-start.7 = (bf16[640,128]{1,0:T(8,128)(2,1)S(1)}, bf16[640,128]{1,0:T(8,128)(2,1)S(1)}, u32[]{:S(2)}, u32[]{:S(2)}) collective-permute-start(bf16[640,128]{1,0:T(8,128)(2,1)S(1)} %get-tuple-element.39), channel_id=1, source_target_pairs={{0,6},{2,4},{4,2},{6,0},{8,14},{10,12},{12,10},{14,8},{16,22},{18,... | collective-permute-start | bytes 491528 | tf_op jit(solution)/shard_map/ppermute | solution.py:371
  39.6 5.3 %collective-permute-start.8 = (bf16[640,128]{1,0:T(8,128)(2,1)S(1)}, bf16[640,128]{1,0:T(8,128)(2,1)S(1)}, u32[]{:S(2)}, u32[]{:S(2)}) collective-permute-start(bf16[640,128]{1,0:T(8,128)(2,1)S(1)} %get-tuple-element.40), channel_id=1, source_target_pairs={{0,8},{2,10},{4,12},{6,14},{8,0},{10,2},{12,4},{14,6},{16,24},{18,... | collective-permute-start | bytes 491528 | tf_op jit(solution)/shard_map/ppermute | solution.py:371
  56.7 11.7 %all-to-all-start.1 = ((bf16[8,320,128]{2,1,0:T(8,128)(2,1)}), bf16[8,320,128]{2,1,0:T(8,128)(2,1)S(1)}, u32[]{:S(2)}, u32[]{:S(2)}) async-start(bf16[8,320,128]{2,1,0:T(8,128)(2,1)} %bitcast.12), calls=%async_computation.1 | async-start | bytes 1310720 | tf_op jit(solution)/shard_map/all_to_all | solution.py:336
  69.9 11.7 %all-to-all-start.2 = ((bf16[8,320,128]{2,1,0:T(8,128)(2,1)}), bf16[8,320,128]{2,1,0:T(8,128)(2,1)S(1)}, u32[]{:S(2)}, u32[]{:S(2)}) async-start(bf16[8,320,128]{2,1,0:T(8,128)(2,1)} %bitcast.16), calls=%async_computation.2 | async-start | bytes 1310720 | tf_op jit(solution)/shard_map/all_to_all | solution.py:336
  73.5 2.0 %collective-permute-start.11 = (f32[1024,128]{1,0:T(8,128)S(1)}, f32[1024,128]{1,0:T(8,128)S(1)}, u32[]{:S(2)}, u32[]{:S(2)}) collective-permute-start(f32[1024,128]{1,0:T(8,128)S(1)} %shard_map.156.after_ref), channel_id=1, source_target_pairs={{0,1},{1,0},{2,3},{3,2},{4,5},{5,4},{6,7},{7,6},{8,9},{9,8},{10,11... | collective-permute-start | bytes 1572872 | tf_op jit(solution)/shard_map/ppermute | solution.py:329
  75.5 13.2 %collective-permute-start.17 = (bf16[1024,128]{1,0:T(8,128)(2,1)S(1)}, bf16[1024,128]{1,0:T(8,128)(2,1)S(1)}, u32[]{:S(2)}, u32[]{:S(2)}) collective-permute-start(bf16[1024,128]{1,0:T(8,128)(2,1)S(1)} %add_convert_fusion.after_ref), channel_id=1, source_target_pairs={{0,24},{2,26},{4,28},{6,30},{8,16},{10,18},{12,20},{14,22},{16,8},... | collective-permute-start | bytes 786440 | tf_op jit(solution)/shard_map/ppermute | solution.py:333
  79.0 3.4 %collective-permute-start.12 = (s32[40,128]{1,0:T(8,128)S(1)}, s32[40,128]{1,0:T(8,128)S(1)}, u32[]{:S(2)}, u32[]{:S(2)}) collective-permute-start(s32[40,128]{1,0:T(8,128)S(1)} %pad_add_fusion.1.refs_0_), channel_id=1, source_target_pairs={{0,1},{1,0},{2,3},{3,2},{4,5},{5,4},{6,7},{7,6},{8,9},{9,8},{10,11... | collective-permute-start | bytes 61448 | tf_op jit(solution)/shard_map/ppermute | solution.py:329
  81.7 1.5 %collective-permute-start.13 = (bf16[640,128]{1,0:T(8,128)(2,1)S(1)}, bf16[640,128]{1,0:T(8,128)(2,1)S(1)}, u32[]{:S(2)}, u32[]{:S(2)}) collective-permute-start(bf16[640,128]{1,0:T(8,128)(2,1)S(1)} %bitcast.51), channel_id=1, source_target_pairs={{0,1},{1,0},{2,3},{3,2},{4,5},{5,4},{6,7},{7,6},{8,9},{9,8},{10,11... | collective-permute-start | bytes 491528 | tf_op jit(solution)/shard_map/ppermute | solution.py:329
  81.7 1.6 %collective-permute-start.14 = (bf16[640,128]{1,0:T(8,128)(2,1)S(1)}, bf16[640,128]{1,0:T(8,128)(2,1)S(1)}, u32[]{:S(2)}, u32[]{:S(2)}) collective-permute-start(bf16[640,128]{1,0:T(8,128)(2,1)S(1)} %bitcast.50), channel_id=1, source_target_pairs={{0,1},{1,0},{2,3},{3,2},{4,5},{5,4},{6,7},{7,6},{8,9},{9,8},{10,11... | collective-permute-start | bytes 491528 | tf_op jit(solution)/shard_map/ppermute | solution.py:329
  82.2 1.4 %collective-permute-start.15 = (bf16[640,128]{1,0:T(8,128)(2,1)S(1)}, bf16[640,128]{1,0:T(8,128)(2,1)S(1)}, u32[]{:S(2)}, u32[]{:S(2)}) collective-permute-start(bf16[640,128]{1,0:T(8,128)(2,1)S(1)} %bitcast.49), channel_id=1, source_target_pairs={{0,1},{1,0},{2,3},{3,2},{4,5},{5,4},{6,7},{7,6},{8,9},{9,8},{10,11... | collective-permute-start | bytes 491528 | tf_op jit(solution)/shard_map/ppermute | solution.py:329
  82.3 1.5 %collective-permute-start.16 = (bf16[640,128]{1,0:T(8,128)(2,1)S(1)}, bf16[640,128]{1,0:T(8,128)(2,1)S(1)}, u32[]{:S(2)}, u32[]{:S(2)}) collective-permute-start(bf16[640,128]{1,0:T(8,128)(2,1)S(1)} %bitcast.48), channel_id=1, source_target_pairs={{0,1},{1,0},{2,3},{3,2},{4,5},{5,4},{6,7},{7,6},{8,9},{9,8},{10,11... | collective-permute-start | bytes 491528 | tf_op jit(solution)/shard_map/ppermute | solution.py:329
